TPU v7x, 32 devices: a whole 2x2x4 slice. The times are simulated.
32 devices in a mesh: ep: 8 (over y, x, core), tp: 4 (over z).
Axes of the slice: x: 2, y: 2, z: 4, core: 2. Of those that a mesh axis runs over, the one named last changes fastest.
Arguments:
- hidden_in: bfloat16 [4096, 2048], P(('ep', 'tp')), may hold values from -6 to 6
- w_query: bfloat16 [2048, 2048], P(('ep', 'tp')), may hold values from -0.125 to 0.125
- w_key: bfloat16 [2048, 2048], P(('ep', 'tp')), may hold values from -0.125 to 0.125
- w_value: bfloat16 [2048, 2048], P(('ep', 'tp')), may hold values from -0.125 to 0.125
- w_output: bfloat16 [2048, 2048], P(('ep', 'tp')), may hold values from -0.5 to 0.5
- w_router: bfloat16 [2048, 64], P(('ep', 'tp')), may hold values from -0.0625 to 0.0625
- gain_attn: bfloat16 [2048], P(('ep', 'tp')), may hold values from 0.25 to 1.75
- gain_ffn: bfloat16 [2048], P(('ep', 'tp')), may hold values from 0.25 to 1.75
- gain_query: bfloat16 [2048], P(('ep', 'tp')), may hold values from 0.25 to 1.75
- gain_key: bfloat16 [2048], P(('ep', 'tp')), may hold values from 0.25 to 1.75
- w_gate: bfloat16 [64, 2048, 1024], P('ep', None, 'tp'), may hold values from -0.125 to 0.125
- w_up: bfloat16 [64, 2048, 1024], P('ep', None, 'tp'), may hold values from -0.125 to 0.125
- w_down: bfloat16 [64, 1024, 2048], P('ep', 'tp'), may hold values from -6 to 6
- expert_ids: int32 [4096, 8], P(('ep', 'tp')), may hold values from 0 to 63, all different within a row; in each aligned block of 128 rows (0 to 127, 128 to 255, ...) at most 32 rows name the same one
- grad_out: bfloat16 [4096, 2048], P(('ep', 'tp')), may hold values from -6 to 6
Outputs:
- block_out: bfloat16 [4096, 2048], P(('ep', 'tp'))
- grad_input: float32 [4096, 2048], P(('ep', 'tp'))
- grad_query: float32 [2048, 2048], P(('ep', 'tp'))
- grad_key: float32 [2048, 2048], P(('ep', 'tp'))
- grad_value: float32 [2048, 2048], P(('ep', 'tp'))
- grad_output: float32 [2048, 2048], P(('ep', 'tp'))
- grad_router: float32 [2048, 64], P(('ep', 'tp'))
- grad_gain_attn: float32 [2048], P(('ep', 'tp'))
- grad_gain_ffn: float32 [2048], P(('ep', 'tp'))
- grad_gain_query: float32 [2048], P(('ep', 'tp'))
- grad_gain_key: float32 [2048], P(('ep', 'tp'))
- grad_gate: float32 [64, 2048, 1024], P('ep', None, 'tp')
- grad_up: float32 [64, 2048, 1024], P('ep', None, 'tp')
- grad_down: float32 [64, 1024, 2048], P('ep', 'tp')
Inputs may be any that keep to these rules, and one draw needn't show every extreme that they name: `expert_ids`: in each aligned block of 128 rows no expert is named by more than 32 rows, a bound that some block reaches.
All inputs are finite; a program needn't handle non-finite values.
Results may differ from a plain program's by a relative error of at most 0.019.
Values may be sent and summed in bfloat16 or wider, within the bound.
No kernel may reach another device: no remote copies, remote signals or barrier semaphores. Data moves between devices by JAX's collectives and lax.ppermute only.
A program may use at most 448 MiB of HBM per device.

v0:
```python
import math

import jax
import jax.numpy as jnp
from jax import lax
from jax.sharding import PartitionSpec as P

HEADS = 16
HEAD_DIM = 128
CAP = 32


epsilon = 1e-05
rope_base = 10000.0
masked_value = -1e30


def rope_tables(length, head_dim):
    half_dim = head_dim // 2
    position = jnp.arange(length, dtype=jnp.float32)
    frequency = jnp.exp(
        jnp.arange(half_dim, dtype=jnp.float32) * (-2.0 * math.log(rope_base) / head_dim)
    )
    angles = position[:, None] * frequency[None, :]
    return (jnp.cos(angles)[:, None, :], jnp.sin(angles)[:, None, :])


def rotate(values, cosines, sines):
    half_dim = values.shape[-1] // 2
    first_half = values[..., :half_dim]
    second = values[..., half_dim:]
    return jnp.concatenate(
        [first_half * cosines - second * sines, second * cosines + first_half * sines], axis=-1
    )


def unrotate(grad_vals, cosines, sines):
    half_dim = grad_vals.shape[-1] // 2
    first_half = grad_vals[..., :half_dim]
    second = grad_vals[..., half_dim:]
    return jnp.concatenate(
        [first_half * cosines + second * sines, second * cosines - first_half * sines], axis=-1
    )


def rms_back(grad_normed, unit_vals, gain_vals, inv_scale):
    scaled = grad_normed * gain_vals
    return inv_scale * (scaled - unit_vals * jnp.mean(scaled * unit_vals, axis=-1, keepdims=True))


def bounce(values):
    return lax.optimization_barrier(values.astype(jnp.bfloat16)).astype(jnp.float32)


def on_device(
    hidden_in,
    w_query,
    w_key,
    w_value,
    w_output,
    w_router,
    gain_attn,
    gain_ffn,
    gain_query,
    gain_key,
    w_gate,
    w_up,
    w_down,
    expert_ids,
    grad_out,
):
    tokens_dev, model_width = hidden_in.shape
    local_experts = w_gate.shape[0]
    expert_count = w_router.shape[1]
    top_count = expert_ids.shape[1]
    ep_count = lax.axis_size("ep")
    pair_count = tokens_dev * top_count
    inv_root = 1.0 / math.sqrt(HEAD_DIM)
    inputs_full = hidden_in.astype(jnp.float32)
    scale_attn = lax.rsqrt(jnp.mean(inputs_full * inputs_full, axis=-1, keepdims=True) + epsilon)
    unit_attn = inputs_full * scale_attn
    piece_q = lax.all_gather(w_query, ("ep", "tp"), axis=0, tiled=True)
    piece_k = lax.all_gather(w_key, ("ep", "tp"), axis=0, tiled=True)
    piece_v = lax.all_gather(w_value, ("ep", "tp"), axis=0, tiled=True)
    piece_o = lax.all_gather(w_output, ("ep", "tp"), axis=0, tiled=True)
    piece_r = lax.all_gather(w_router, ("ep", "tp"), axis=0, tiled=True)
    piece_ga = lax.all_gather(gain_attn, ("ep", "tp"), axis=0, tiled=True)
    piece_gf = lax.all_gather(gain_ffn, ("ep", "tp"), axis=0, tiled=True)
    piece_gq = lax.all_gather(gain_query, ("ep", "tp"), axis=0, tiled=True)
    piece_gk = lax.all_gather(gain_key, ("ep", "tp"), axis=0, tiled=True)
    features_part = (unit_attn * piece_ga.astype(jnp.float32)).astype(jnp.bfloat16)
    query_acc = jnp.dot(features_part, piece_q, preferred_element_type=jnp.float32)
    key_acc = jnp.dot(features_part, piece_k, preferred_element_type=jnp.float32)
    value_acc = jnp.dot(features_part, piece_v, preferred_element_type=jnp.float32)
    output_full = piece_o
    router_full = piece_r
    carried = (
        query_acc,
        key_acc,
        value_acc,
        features_part,
        output_full,
        router_full,
        piece_ga,
        piece_gf,
        piece_gq,
        piece_gk,
    )
    (
        query_raw,
        key_raw,
        value_raw,
        normed_attn,
        output_full,
        router_full,
        attn_gain,
        ffn_gain,
        query_gain,
        key_gain,
    ) = carried
    scale_query = lax.rsqrt(jnp.mean(query_raw * query_raw, axis=-1, keepdims=True) + epsilon)
    unit_query = query_raw * scale_query
    scale_key = lax.rsqrt(jnp.mean(key_raw * key_raw, axis=-1, keepdims=True) + epsilon)
    unit_key = key_raw * scale_key
    cosines, sines = rope_tables(tokens_dev, HEAD_DIM)
    query_rot = rotate(
        (unit_query * query_gain.astype(jnp.float32)).reshape(tokens_dev, HEADS, HEAD_DIM),
        cosines,
        sines,
    ).astype(jnp.bfloat16)
    key_rot = rotate(
        (unit_key * key_gain.astype(jnp.float32)).reshape(tokens_dev, HEADS, HEAD_DIM),
        cosines,
        sines,
    ).astype(jnp.bfloat16)
    value_low = value_raw.astype(jnp.bfloat16)
    value_heads = value_low.reshape(tokens_dev, HEADS, HEAD_DIM)
    causal = jnp.arange(tokens_dev)[:, None] >= jnp.arange(tokens_dev)[None, :]

    def attention_scores():
        raw_scores = (
            jnp.einsum("qhd,khd->hqk", query_rot, key_rot, preferred_element_type=jnp.float32)
            * inv_root
        )
        return jnp.where(causal[None], raw_scores, masked_value)

    scores = attention_scores()
    row_peak = jnp.max(scores, axis=-1, keepdims=True)
    exponent = jnp.exp(scores - row_peak)
    row_total = jnp.sum(exponent, axis=-1, keepdims=True)
    att_probs = exponent / row_total
    log_total = row_peak + jnp.log(row_total)
    attended = (
        jnp.einsum(
            "hqk,khd->qhd",
            att_probs.astype(jnp.bfloat16),
            value_heads,
            preferred_element_type=jnp.float32,
        )
        .reshape(tokens_dev, model_width)
        .astype(jnp.bfloat16)
    )
    mixed = inputs_full + jnp.dot(attended, output_full, preferred_element_type=jnp.float32)
    scale_ffn = lax.rsqrt(jnp.mean(mixed * mixed, axis=-1, keepdims=True) + epsilon)
    unit_ffn = mixed * scale_ffn
    normed_ffn = (unit_ffn * ffn_gain.astype(jnp.float32)).astype(jnp.bfloat16)
    logits = jnp.dot(normed_ffn, router_full, preferred_element_type=jnp.float32)
    router_probs = jax.nn.softmax(logits, axis=-1)
    choose = (expert_ids[:, :, None] == jnp.arange(expert_count, dtype=jnp.int32)).astype(
        jnp.float32
    )
    gate_values = jnp.sum(choose * router_probs[:, None, :], axis=-1)
    flat_ids = expert_ids.reshape(-1)
    onehot = (flat_ids[:, None] == jnp.arange(expert_count, dtype=jnp.int32)).astype(jnp.int32)
    slot_index = jnp.sum(jnp.cumsum(onehot, axis=0) * onehot, axis=1) - 1
    owner_index = flat_ids // local_experts
    member = flat_ids % local_experts
    place_index = (owner_index * CAP + slot_index) * local_experts + member
    source = (
        jnp.full((expert_count * CAP,), pair_count, jnp.int32)
        .at[place_index]
        .set(jnp.arange(pair_count, dtype=jnp.int32))
    )
    filled = source < pair_count
    picked = jnp.minimum(source, pair_count - 1)
    token_of = picked // top_count
    outgoing = jnp.where(
        filled[:, None], normed_ffn[token_of], jnp.zeros((), jnp.bfloat16)
    ).reshape(ep_count, CAP, local_experts, model_width)
    received = lax.all_to_all(outgoing, "ep", split_axis=0, concat_axis=0, tiled=True)
    rows_own = received.reshape(ep_count * CAP, local_experts, model_width)
    joined = jnp.concatenate([w_gate, w_up], axis=2)
    hidden_units = w_gate.shape[2]
    pre_all = jnp.einsum(
        "rld,ldh->rlh",
        lax.all_gather(rows_own, "tp", axis=0, tiled=True),
        joined,
        preferred_element_type=jnp.float32,
    )
    gate_pre = pre_all[..., :hidden_units]
    up_pre = pre_all[..., hidden_units:]
    inner_act = (jax.nn.silu(gate_pre) * up_pre).astype(jnp.bfloat16)
    expert_out = lax.psum_scatter(
        jnp.einsum("rlh,lhd->rld", inner_act, w_down, preferred_element_type=jnp.float32).astype(
            jnp.bfloat16
        ),
        "tp",
        scatter_dimension=0,
        tiled=True,
    )
    returned = lax.all_to_all(
        expert_out.reshape(ep_count, CAP, local_experts, model_width),
        "ep",
        split_axis=0,
        concat_axis=0,
        tiled=True,
    )
    pair_out = (
        returned.reshape(expert_count * CAP, model_width)[place_index]
        .reshape(tokens_dev, top_count, model_width)
        .astype(jnp.float32)
    )
    expert_sum = jnp.sum(gate_values[:, :, None] * pair_out, axis=1)
    block_out = (mixed + expert_sum).astype(jnp.bfloat16)
    upstream = grad_out.astype(jnp.float32)
    grad_gates = jnp.sum(upstream[:, None, :] * pair_out, axis=-1)
    pair_grads = (
        (gate_values[:, :, None] * upstream[:, None, :])
        .astype(jnp.bfloat16)
        .reshape(pair_count, model_width)
    )
    outgoing_grads = jnp.where(
        filled[:, None], pair_grads[picked], jnp.zeros((), jnp.bfloat16)
    ).reshape(ep_count, CAP, local_experts, model_width)
    grads_own = lax.all_to_all(
        outgoing_grads, "ep", split_axis=0, concat_axis=0, tiled=True
    ).reshape(ep_count * CAP, local_experts, model_width)
    rows_piece = lax.all_gather(rows_own, "tp", axis=0, tiled=True)
    grads_piece = lax.all_gather(grads_own, "tp", axis=0, tiled=True)
    sigmoid_g = jax.nn.sigmoid(gate_pre)
    grad_inner = jnp.einsum("rld,lhd->rlh", grads_piece, w_down, preferred_element_type=jnp.float32)
    grad_gate_part = (
        grad_inner * up_pre * sigmoid_g * (1.0 + gate_pre * (1.0 - sigmoid_g))
    ).astype(jnp.bfloat16)
    grad_up_part = (grad_inner * gate_pre * sigmoid_g).astype(jnp.bfloat16)
    acc_down = jnp.einsum(
        "rlh,rld->lhd", inner_act, grads_piece, preferred_element_type=jnp.float32
    )
    acc_gate = jnp.einsum(
        "rld,rlh->ldh", rows_piece, grad_gate_part, preferred_element_type=jnp.float32
    )
    acc_up = jnp.einsum(
        "rld,rlh->ldh", rows_piece, grad_up_part, preferred_element_type=jnp.float32
    )
    accumulate_grads_pre = jnp.concatenate([grad_gate_part, grad_up_part], axis=2)
    rows_grad = lax.psum_scatter(
        jnp.einsum(
            "rlh,ldh->rld", accumulate_grads_pre, joined, preferred_element_type=jnp.float32
        ).astype(jnp.bfloat16),
        "tp",
        scatter_dimension=0,
        tiled=True,
    )
    back_rows = lax.all_to_all(
        rows_grad.reshape(ep_count, CAP, local_experts, model_width),
        "ep",
        split_axis=0,
        concat_axis=0,
        tiled=True,
    )
    grad_ffn_normed = jnp.sum(
        back_rows.reshape(expert_count * CAP, model_width)[place_index]
        .reshape(tokens_dev, top_count, model_width)
        .astype(jnp.float32),
        axis=1,
    )
    grad_probs = jnp.sum(choose * grad_gates[:, :, None], axis=1)
    grad_logits = router_probs * (
        grad_probs - jnp.sum(router_probs * grad_probs, axis=-1, keepdims=True)
    )
    router_wide = router_full.astype(jnp.float32)
    grad_ffn_normed = grad_ffn_normed + jnp.dot(
        grad_logits, router_wide.T, precision=lax.Precision.HIGHEST
    )
    grad_router_local = jnp.dot(
        normed_ffn.astype(jnp.float32).T, grad_logits, precision=lax.Precision.HIGHEST
    )
    grad_ffn_gain = jnp.sum(grad_ffn_normed * unit_ffn, axis=0)
    grad_mixed = upstream + rms_back(
        grad_ffn_normed, unit_ffn, ffn_gain.astype(jnp.float32), scale_ffn
    )
    grad_branch = grad_mixed.astype(jnp.bfloat16)
    grad_attended = jnp.einsum(
        "te,de->td", grad_branch, output_full, preferred_element_type=jnp.float32
    ).astype(jnp.bfloat16)
    grad_heads = grad_attended.reshape(tokens_dev, HEADS, HEAD_DIM)
    scores = attention_scores()
    att_probs = jnp.exp(scores - log_total)
    grad_probs_att = jnp.einsum(
        "qhd,khd->hqk", grad_heads, value_heads, preferred_element_type=jnp.float32
    )
    grad_scores = (
        att_probs * (grad_probs_att - jnp.sum(att_probs * grad_probs_att, axis=-1, keepdims=True))
    ).astype(jnp.bfloat16)
    grad_qrot = (
        jnp.einsum("hqk,khd->qhd", grad_scores, key_rot, preferred_element_type=jnp.float32)
        * inv_root
    )
    grad_krot = (
        jnp.einsum("hqk,qhd->khd", grad_scores, query_rot, preferred_element_type=jnp.float32)
        * inv_root
    )
    grad_value_rows = (
        jnp.einsum(
            "hqk,qhd->khd",
            att_probs.astype(jnp.bfloat16),
            grad_heads,
            preferred_element_type=jnp.float32,
        )
        .reshape(tokens_dev, model_width)
        .astype(jnp.bfloat16)
    )
    grad_qnorm = unrotate(bounce(grad_qrot), cosines, sines).reshape(tokens_dev, model_width)
    grad_knorm = unrotate(bounce(grad_krot), cosines, sines).reshape(tokens_dev, model_width)
    grad_query_gain = jnp.sum(grad_qnorm * unit_query, axis=0)
    grad_key_gain = jnp.sum(grad_knorm * unit_key, axis=0)
    grad_query_raw = rms_back(
        grad_qnorm, unit_query, query_gain.astype(jnp.float32), scale_query
    ).astype(jnp.bfloat16)
    grad_key_raw = rms_back(grad_knorm, unit_key, key_gain.astype(jnp.float32), scale_key).astype(
        jnp.bfloat16
    )
    piece_q, piece_k, piece_v = lax.all_gather(
        (w_query, w_key, w_value), ("ep", "tp"), axis=0, tiled=True
    )
    grad_attn_normed = (
        jnp.einsum("te,ce->tc", grad_query_raw, piece_q, preferred_element_type=jnp.float32)
        + jnp.einsum("te,ce->tc", grad_key_raw, piece_k, preferred_element_type=jnp.float32)
        + jnp.einsum("te,ce->tc", grad_value_rows, piece_v, preferred_element_type=jnp.float32)
    )
    grad_attn_gain = jnp.sum(grad_attn_normed * unit_attn, axis=0)
    grad_input = grad_mixed + rms_back(
        grad_attn_normed, unit_attn, attn_gain.astype(jnp.float32), scale_attn
    )
    grad_stack = jnp.concatenate([grad_query_raw, grad_key_raw, grad_value_rows], axis=1)
    dense_rows = lax.psum_scatter(
        jnp.concatenate(
            [
                jnp.einsum(
                    "tc,te->ce", normed_attn, grad_stack, preferred_element_type=jnp.float32
                ),
                jnp.einsum("tc,te->ce", attended, grad_branch, preferred_element_type=jnp.float32),
            ],
            axis=1,
        ),
        ("ep", "tp"),
        scatter_dimension=0,
        tiled=True,
    )
    small_sums = (
        lax.psum_scatter(grad_router_local, ("ep", "tp"), scatter_dimension=0, tiled=True),
        lax.psum_scatter(grad_attn_gain, ("ep", "tp"), scatter_dimension=0, tiled=True),
        lax.psum_scatter(grad_ffn_gain, ("ep", "tp"), scatter_dimension=0, tiled=True),
        lax.psum_scatter(grad_query_gain, ("ep", "tp"), scatter_dimension=0, tiled=True),
        lax.psum_scatter(grad_key_gain, ("ep", "tp"), scatter_dimension=0, tiled=True),
    )
    return (
        block_out,
        grad_input,
        dense_rows[:, :model_width],
        dense_rows[:, model_width : 2 * model_width],
        dense_rows[:, 2 * model_width : 3 * model_width],
        dense_rows[:, 3 * model_width :],
        small_sums[0],
        small_sums[1],
        small_sums[2],
        small_sums[3],
        small_sums[4],
        acc_gate,
        acc_up,
        acc_down,
    )


def solution(mesh):
    placed = (
        P(("ep", "tp"), None),
        P(("ep", "tp"), None),
        P(("ep", "tp"), None),
        P(("ep", "tp"), None),
        P(("ep", "tp"), None),
        P(("ep", "tp"), None),
        P(("ep", "tp")),
        P(("ep", "tp")),
        P(("ep", "tp")),
        P(("ep", "tp")),
        P("ep", None, "tp"),
        P("ep", None, "tp"),
        P("ep", "tp", None),
        P(("ep", "tp"), None),
        P(("ep", "tp"), None),
    )
    return jax.shard_map(
        on_device,
        mesh=mesh,
        in_specs=placed,
        out_specs=(
            P(("ep", "tp"), None),
            P(("ep", "tp"), None),
            P(("ep", "tp"), None),
            P(("ep", "tp"), None),
            P(("ep", "tp"), None),
            P(("ep", "tp"), None),
            P(("ep", "tp"), None),
            P(("ep", "tp")),
            P(("ep", "tp")),
            P(("ep", "tp")),
            P(("ep", "tp")),
            P("ep", None, "tp"),
            P("ep", None, "tp"),
            P("ep", "tp", None),
        ),
        check_vma=False,
    )
```

profile of v0, /device:TPU:0, one launch (start us, length us, event | category | flops | bytes accessed | tf_op | source)
XLA Modules:
  0.0 4588.3 jit_solution(5921774270021594314)
XLA Ops:
  14.5 42.6 all-reduce.9
  57.2 18.0 reduce-window.6
  81.7 74.2 %all_gather.45 = bf16[2048,64]{1,0:T(8,128)(2,1)S(1)} all-gather(bf16[64,64]{1,0:T(8,128)(2,1)} %param.20), channel_id=1, replica_groups=mesh['ep'=8,'tp'=4] {'ep','tp'}, dimensions={0}, use_global_device_ids=true | all-gather | bytes 270336 | tf_op jit(solution)/shard_map/all_gather | solution.py:86
  182.5 69.2 %all-gather.7.cloned.1.call-done = bf16[2048,2048]{1,0:T(8,128)(2,1)} async-done(((bf16[64,2048]{1,0:T(8,128)(2,1)}), bf16[2048,2048]{1,0:T(8,128)(2,1)}) %all-gather.7.cloned.1.call-update) | async-done | bytes 8388624 | tf_op jit(solution)/shard_map/all_gather | solution.py:84
  258.5 72.0 %all-gather.13.cloned.1.call-done = bf16[2048,2048]{1,0:T(8,128)(2,1)} async-done(((bf16[64,2048]{1,0:T(8,128)(2,1)}), bf16[2048,2048]{1,0:T(8,128)(2,1)}) %all-gather.13.cloned.1.call-update) | async-done | bytes 8388624 | tf_op jit(solution)/shard_map/all_gather | solution.py:85
  352.0 19.0 gather_fusion.2
  371.1 32.2 copy_select_fusion
  403.3 97.4 %all_to_all.20 = bf16[8,32,8,2048]{3,1,2,0:T(8,128)(2,1)} all-to-all(bf16[8,32,8,2048]{3,1,2,0:T(8,128)(2,1)S(1)} %get-tuple-element.58), channel_id=1, replica_groups=mesh['ep'=8,'tp'=4] {'ep'}, dimensions={0} | all-to-all | bytes 16777216 | tf_op jit(solution)/shard_map/all_to_all | solution.py:190
  509.3 100.2 %all_to_all.21 = bf16[8,32,8,2048]{3,1,2,0:T(8,128)(2,1)} all-to-all(bf16[8,32,8,2048]{3,1,2,0:T(8,128)(2,1)} %get-tuple-element.57), channel_id=1, replica_groups=mesh['ep'=8,'tp'=4] {'ep'}, dimensions={0} | all-to-all | bytes 16777216 | tf_op jit(solution)/shard_map/all_to_all | solution.py:235
  617.9 11.4 copy.200
  629.3 11.4 copy.201
  640.7 427.8 %all-gather.15.cloned.1.call-done = bf16[1024,8,2048]{2,0,1:T(8,128)(2,1)} async-done(((bf16[256,8,2048]{2,0,1:T(8,128)(2,1)}), bf16[1024,8,2048]{2,0,1:T(8,128)(2,1)}) %all-gather.15.cloned.1.call-update) | async-done | bytes 33554448 | tf_op jit(solution)/shard_map/all_gather | solution.py:196
  1068.5 30.3 fusion.1
  1098.7 530.8 %all-gather.17.cloned.1.call-done = bf16[1024,8,2048]{2,0,1:T(8,128)(2,1)} async-done(((bf16[256,8,2048]{2,0,1:T(8,128)(2,1)}), bf16[1024,8,2048]{2,0,1:T(8,128)(2,1)}) %all-gather.17.cloned.1.call-update) | async-done | bytes 33554448 | tf_op jit(solution)/shard_map/all_gather | solution.py:239
  1629.5 26.0 fusion.9
  1655.5 26.5 convert_bitcast_fusion
  1682.1 17.9 convert_bitcast_fusion.1
  1700.0 532.4 %reduce-scatter.7.cloned.1.call-done = bf16[256,8,2048]{0,2,1:T(8,128)(2,1)} async-done(((bf16[1024,8,2048]{0,2,1:T(8,128)(2,1)}), bf16[256,8,2048]{0,2,1:T(8,128)(2,1)}) %reduce-scatter.7.cloned.1.call-update) | async-done | bytes 8388624 | tf_op jit(solution)/shard_map/reduce_scatter | solution.py:256
  2232.4 12.7 copy.218
  2250.1 537.7 %reduce-scatter.5.cloned.1.call-done = bf16[256,8,2048]{2,0,1:T(8,128)(2,1)} async-done(((bf16[1024,8,2048]{2,0,1:T(8,128)(2,1)}), bf16[256,8,2048]{2,0,1:T(8,128)(2,1)}) %reduce-scatter.5.cloned.1.call-update) | async-done | bytes 8388624 | tf_op jit(solution)/shard_map/reduce_scatter | solution.py:203
  2801.4 13.5 gather_fusion.3
  2820.9 74.5 %all-to-all-done.1 = bf16[8,32,8,2048]{3,1,2,0:T(8,128)(2,1)} async-done(((bf16[8,32,8,2048]{3,1,2,0:T(8,128)(2,1)}), bf16[8,32,8,2048]{3,1,2,0:T(8,128)(2,1)}, u32[]{:S(2)}, u32[]{:S(2)}) %all-to-all-start.1) | async-done | bytes 8388640 | tf_op jit(solution)/shard_map/all_to_all | solution.py:211
  2895.3 12.3 copy.212
  2907.7 13.4 gather_fusion.1
  2968.2 20.8 fusion.13
  2989.0 43.4 pad_maximum_fusion
  3032.5 20.5 fusion.87
  3053.0 21.0 fusion.85
  3074.0 21.3 fusion.86
  3112.3 45.3 all-reduce.8
  3164.2 1279.1 %reduce-scatter.9.cloned.1.call-done = f32[64,8192]{1,0:T(8,128)} async-done(((f32[2048,8192]{1,0:T(8,128)}), f32[64,8192]{1,0:T(8,128)}) %reduce-scatter.9.cloned.1.call-update) | async-done | bytes 2097168 | tf_op jit(solution)/shard_map/reduce_scatter | solution.py:346
  4446.1 135.2 %reduce-scatter.11.cloned.1.call-done = f32[64,64]{1,0:T(8,128)} async-done(((f32[2048,64]{1,0:T(8,128)}), f32[64,64]{1,0:T(8,128)}) %reduce-scatter.11.cloned.1.call-update) | async-done | bytes 16400 | tf_op jit(solution)/shard_map/reduce_scatter | solution.py:361
  (273 shorter events, 182.8 us)
Async XLA Ops:
  7.2 150.5 %all-gather.9.cloned.1.call-start = ((), (), s32[]{:S(2)}) async-start(), calls=%async_computation.9 | async-start | bytes 8650752 | tf_op jit(solution)/shard_map/all_gather | solution.py:82
  7.9 164.5 %all-gather.11.cloned.1.call-start = ((), (), s32[]{:S(2)}) async-start(), calls=%async_computation.10 | async-start | bytes 8650752 | tf_op jit(solution)/shard_map/all_gather | solution.py:83
  8.7 243.1 %all-gather.7.cloned.1.call-start = ((), (), s32[]{:S(2)}) async-start(), calls=%async_computation.8 | async-start | bytes 8650752 | tf_op jit(solution)/shard_map/all_gather | solution.py:84
  9.4 321.1 %all-gather.13.cloned.1.call-start = ((), (), s32[]{:S(2)}) async-start(), calls=%async_computation.11 | async-start | bytes 8650752 | tf_op jit(solution)/shard_map/all_gather | solution.py:85
  10.0 1058.5 %all-gather.15.cloned.1.call-start = ((), (), s32[]{:S(2)}) async-start(), calls=%async_computation.12 | async-start | bytes 41943040 | tf_op jit(solution)/shard_map/all_gather | solution.py:196
  57.1 194.6 %copy-start.25 = (f32[2048]{0:T(1024)}, f32[2048]{0:T(1024)S(1)}, u32[]{:S(2)}) copy-start(f32[2048]{0:T(1024)S(1)} %convert_element_type.143) | copy-start | bytes 24580
  57.1 120.1 %copy-start.42 = (f32[2048]{0:T(1024)}, f32[2048]{0:T(1024)S(1)}, u32[]{:S(2)}) copy-start(f32[2048]{0:T(1024)S(1)} %convert_element_type.147) | copy-start | bytes 24580
  57.1 105.6 %copy-start.40 = (f32[2048]{0:T(1024)}, f32[2048]{0:T(1024)S(1)}, u32[]{:S(2)}) copy-start(f32[2048]{0:T(1024)S(1)} %convert_element_type.146) | copy-start | bytes 24580
  57.1 278.4 %copy-start.44 = (f32[2048]{0:T(1024)}, f32[2048]{0:T(1024)S(1)}, u32[]{:S(2)}) copy-start(f32[2048]{0:T(1024)S(1)} %convert_element_type.152) | copy-start | bytes 24580
  81.6 267.9 %copy-start.11 = (f32[128,2048]{1,0:T(8,128)}, f32[128,2048]{1,0:T(8,128)S(1)}, u32[]{:S(2)}) copy-start(f32[128,2048]{1,0:T(8,128)S(1)} %convert_element_type.161) | copy-start | bytes 3145732
  155.9 180.7 %copy-start.15 = (bf16[2048,64]{1,0:T(8,128)(2,1)}, bf16[2048,64]{1,0:T(8,128)(2,1)S(1)}, u32[]{:S(2)}) copy-start(bf16[2048,64]{1,0:T(8,128)(2,1)S(1)} %all_gather.45) | copy-start | bytes 786436
  157.3 94.4 %copy-start.46 = (f32[128]{0:T(128)}, f32[128]{0:T(128)S(1)}, u32[]{:S(2)}) copy-start(f32[128]{0:T(128)S(1)} %add_rsqrt_fusion.3) | copy-start | bytes 1540
  157.6 21.6 copy-start.27
  157.6 21.6 copy-start.29
  182.3 74.2 %copy-start.4 = (f32[16,128,128]{1,2,0:T(8,128)}, f32[16,128,128]{1,2,0:T(8,128)S(1)}, u32[]{:S(2)}) copy-start(f32[16,128,128]{1,2,0:T(8,128)S(1)} %get-tuple-element.68) | copy-start | bytes 3145732
  182.3 74.2 %copy-start.48 = (f32[16,128]{1,0:T(8,128)}, f32[16,128]{1,0:T(8,128)S(1)}, u32[]{:S(2)}) copy-start(f32[16,128]{1,0:T(8,128)S(1)} %get-tuple-element.67) | copy-start | bytes 24580
  182.5 76.0 %copy-start.52 = (f32[16,128]{1,0:T(8,128)}, f32[16,128]{1,0:T(8,128)S(1)}, u32[]{:S(2)}) copy-start(f32[16,128]{1,0:T(8,128)S(1)} %fusion.38) | copy-start | bytes 24580
  509.2 1120.3 %all-gather.17.cloned.1.call-start = ((), (), s32[]{:S(2)}) async-start(), calls=%async_computation.14 | async-start | bytes 41943040 | tf_op jit(solution)/shard_map/all_gather | solution.py:239
  617.8 1614.6 %reduce-scatter.7.cloned.1.call-start = ((), (), s32[]{:S(2)}) async-start(), calls=%async_computation.15 | async-start | bytes 41943040 | tf_op jit(solution)/shard_map/reduce_scatter | solution.py:256
  1682.0 1105.7 %reduce-scatter.5.cloned.1.call-start = ((), (), s32[]{:S(2)}) async-start(), calls=%async_computation.13 | async-start | bytes 41943040 | tf_op jit(solution)/shard_map/reduce_scatter | solution.py:203
  2245.1 551.1 %all-to-all-start.3 = ((bf16[8,32,8,2048]{3,2,1,0:T(8,128)(2,1)}), bf16[8,32,8,2048]{3,2,1,0:T(8,128)(2,1)}, u32[]{:S(2)}, u32[]{:S(2)}) async-start(bf16[8,32,8,2048]{3,2,1,0:T(8,128)(2,1)} %bitcast.148), calls=%async_computation.5 | async-start | bytes 16777216 | tf_op jit(solution)/shard_map/all_to_all | solution.py:264
  2796.2 99.2 %all-to-all-start.1 = ((bf16[8,32,8,2048]{3,1,2,0:T(8,128)(2,1)}), bf16[8,32,8,2048]{3,1,2,0:T(8,128)(2,1)}, u32[]{:S(2)}, u32[]{:S(2)}) async-start(bf16[8,32,8,2048]{3,1,2,0:T(8,128)(2,1)} %copy.211), calls=%async_computation.2 | async-start | bytes 16777216 | tf_op jit(solution)/shard_map/all_to_all | solution.py:211
  2801.3 1642.0 %reduce-scatter.9.cloned.1.call-start = ((), (), s32[]{:S(2)}) async-start(), calls=%async_computation.16 | async-start | bytes 69206016 | tf_op jit(solution)/shard_map/reduce_scatter | solution.py:346
  2907.6 20.0 copy-start.7
  2907.6 20.0 copy-start.16
  2907.7 20.0 copy-start.34
  2907.7 20.0 copy-start.45
  3032.5 1548.8 %reduce-scatter.11.cloned.1.call-start = ((), (), s32[]{:S(2)}) async-start(), calls=%async_computation.17 | async-start | bytes 1081344 | tf_op jit(solution)/shard_map/reduce_scatter | solution.py:361
  3108.3 51.6 %copy-start.1 = (bf16[128,2048]{1,0:T(8,128)(2,1)S(1)}, bf16[128,2048]{1,0:T(8,128)(2,1)}, u32[]{:S(2)}) copy-start(bf16[128,2048]{1,0:T(8,128)(2,1)} %copy-done) | copy-start | bytes 1572868
  3108.3 51.6 %copy-start.35 = (f32[128,64]{0,1:T(8,128)S(1)}, f32[128,64]{0,1:T(8,128)}, u32[]{:S(2)}) copy-start(f32[128,64]{0,1:T(8,128)} %copy-done.33) | copy-start | bytes 98308
  3108.3 51.6 %copy-start.37 = (f32[128,64]{0,1:T(8,128)S(1)}, f32[128,64]{0,1:T(8,128)}, u32[]{:S(2)}) copy-start(f32[128,64]{0,1:T(8,128)} %copy-done.36) | copy-start | bytes 98308
  3108.3 51.6 %copy-start.66 = (f32[128]{0:T(128)S(1)}, f32[128]{0:T(128)}, u32[]{:S(2)}) copy-start(f32[128]{0:T(128)} %copy-done.65) | copy-start | bytes 1540
  (51 other events, 406.6 us)
Sparse Core Ops, SparseCore 0:
  10.9 81.0 all-gather.8
  95.0 77.4 all-gather.10
  175.4 76.3 all-gather.6
  254.5 75.9 all-gather.12
  509.3 559.0 all-gather.14
  1069.9 559.5 all-gather.16
  1682.2 550.2 reduce-scatter.6
  2234.9 552.7 reduce-scatter.4
  3032.6 1410.6 reduce-scatter.8
  4445.9 135.3 reduce-scatter.10
where the time goes:
time: 4590 us
  waiting for transfers between devices  3670 us (80%)
  blocking collectives  360 us (8%)
  matrix products  249 us (5%)
  local copies, waits for them, and re-layouts  156 us (3%)
  other arithmetic  128 us (3%)
    reduce_scatter x1, waiting for transfers between devices, on_device(): lax.psum_scatter(jnp.concatenate([jnp.einsum('tc,te->ce', normed_attn, gr...  1280 us
    reduce_scatter x1, waiting for transfers between devices, on_device(): lax.psum_scatter(jnp.einsum('rlh,lhd->rld', inner_act, w_down, preferred_...  538 us
    reduce_scatter x1, waiting for transfers between devices, on_device(): lax.psum_scatter(jnp.einsum('rlh,ldh->rld', accumulate_grads_pre, joined,...  532 us
    all_gather x1, waiting for transfers between devices, on_device(): grads_piece = lax.all_gather(grads_own, 'tp', axis=0, tiled=True)  531 us
    all_gather x1, waiting for transfers between devices, on_device(): lax.all_gather(rows_own, 'tp', axis=0, tiled=True)  428 us
    reduce_scatter x1, waiting for transfers between devices, on_device(): lax.psum_scatter(grad_router_local, ('ep', 'tp'), scatter_dimension=0, ti...  135 us
    all_to_all x1, blocking collectives, on_device(): lax.all_to_all(outgoing_grads, 'ep', split_axis=0, concat_axis=0, tiled=T...  100 us
    all_to_all x1, blocking collectives, on_device(): lax.all_to_all(outgoing, 'ep', split_axis=0, concat_axis=0, tiled=True)  97.4 us
  transfers between devices with their start and end apart: 12, of which 10 were waited for; matrix products, arithmetic and copies ran while one was open for 6% of the time, Pallas kernels for 0%

commit v1 on v0

v1 whole, which is shorter than its diff:
```python
import math

import jax
import jax.numpy as jnp
from jax import lax
from jax.experimental import pallas as pl
from jax.experimental.pallas import tpu as pltpu
from jax.sharding import PartitionSpec as P

HEADS = 16
HEAD_DIM = 128
CAP = 32


epsilon = 1e-05
rope_base = 10000.0
masked_value = -1e30
low = jnp.bfloat16
wide = jnp.float32


def rope_tables(length, head_dim):
    half_dim = head_dim // 2
    position = jnp.arange(length, dtype=jnp.float32)
    frequency = jnp.exp(
        jnp.arange(half_dim, dtype=jnp.float32) * (-2.0 * math.log(rope_base) / head_dim)
    )
    angles = position[:, None] * frequency[None, :]
    return (jnp.cos(angles)[:, None, :], jnp.sin(angles)[:, None, :])


def rotate(values, cosines, sines):
    half_dim = values.shape[-1] // 2
    first_half = values[..., :half_dim]
    second = values[..., half_dim:]
    return jnp.concatenate(
        [first_half * cosines - second * sines, second * cosines + first_half * sines], axis=-1
    )


def unrotate(grad_vals, cosines, sines):
    half_dim = grad_vals.shape[-1] // 2
    first_half = grad_vals[..., :half_dim]
    second = grad_vals[..., half_dim:]
    return jnp.concatenate(
        [first_half * cosines + second * sines, second * cosines - first_half * sines], axis=-1
    )


def rms_back(grad_normed, unit_vals, gain_vals, inv_scale):
    scaled = grad_normed * gain_vals
    return inv_scale * (scaled - unit_vals * jnp.mean(scaled * unit_vals, axis=-1, keepdims=True))


def bounce(values):
    return lax.optimization_barrier(values.astype(low)).astype(wide)


class Grid:
    axes = "yxcz"

    def __init__(self):
        self.ep, self.tp = lax.axis_size("ep"), lax.axis_size("tp")
        chips = self.ep // 2
        nx = math.isqrt(chips)
        while chips % nx:
            nx -= 1
        self.size = {"y": chips // nx, "x": nx, "c": 2, "z": self.tp}
        self.stride = {"y": 2 * nx, "x": 2, "c": 1}
        self.shape = tuple(self.size[axis] for axis in self.axes)

    def place(self, axis):
        if axis == "z":
            return lax.axis_index("tp")
        return lax.axis_index("ep") // self.stride[axis] % self.size[axis]

    def shift(self, values, axis, step):
        count = self.size[axis]
        if axis == "z":
            return lax.ppermute(values, "tp", [(i, (i + step) % count) for i in range(count)])
        stride = self.stride[axis]
        pairs = []
        for i in range(self.ep):
            own = i // stride % count
            pairs.append((i, i + ((own + step) % count - own) * stride))
        return lax.ppermute(values, "ep", pairs)

    def gather(self, values, order):
        values = values[None, None, None, None]
        for axis in order:
            dim, count, own = self.axes.index(axis), self.size[axis], self.place(axis)
            parts = [values] + [self.shift(values, axis, step) for step in range(1, count)]
            shape = list(values.shape)
            shape[dim] = count
            values = jnp.zeros(shape, values.dtype)
            for step, part in enumerate(parts):
                values = lax.dynamic_update_slice_in_dim(
                    values, part, (own - step) % count, dim
                )
        return values

    def gather_rows(self, values, orders):
        share = values.shape[0] // len(orders)
        parts = [
            self.gather(values[i * share : (i + 1) * share], order)
            for i, order in enumerate(orders)
        ]
        return jnp.concatenate(parts, axis=4).reshape((-1,) + values.shape[1:])

    def reduce_scatter(self, values, order):
        left = list(self.axes)
        kind = values.dtype
        values = values.reshape(self.shape + values.shape[1:])
        for axis in order:
            dim, count, own = left.index(axis), self.size[axis], self.place(axis)

            def part(step):
                return lax.dynamic_index_in_dim(
                    values, (own - step) % count, dim, keepdims=False
                )

            total = part(0).astype(wide)
            for step in range(1, count):
                total = total + self.shift(part(step), axis, -step).astype(wide)
            values = total.astype(kind)
            left.remove(axis)
        return values


gather_orders = ("zxyc", "zyxc", "xzyc", "yzxc")
reduce_orders = ("cyxz", "cxyz", "cyzx", "cxzy")
nt_dims = (((1,), (1,)), ((), ()))
tn_dims = (((0,), (0,)), ((), ()))


def one_hot(slots):
    experts, tokens = slots.shape
    place = lax.broadcasted_iota(jnp.int32, (experts, CAP, tokens), 1).astype(wide) + 1.0
    return (slots[:, None, :] == place).astype(wide).reshape(experts * CAP, tokens)


def dot(left, right, dims=(((1,), (0,)), ((), ()))):
    return lax.dot_general(left, right, dims, preferred_element_type=wide)


def spread(target, rows, block):
    for e in range(target.shape[0]):
        target[e, block * CAP : (block + 1) * CAP, :] = rows[e * CAP : (e + 1) * CAP]


def joined_rows(source, block):
    return jnp.concatenate(
        [source[e, block * CAP : (block + 1) * CAP, :] for e in range(source.shape[0])], axis=0
    )


def weight_copies(sources, targets, sems):
    return [
        [
            pltpu.make_async_copy(source.at[e], target.at[e], sems.at[i, e])
            for i, (source, target) in enumerate(zip(sources, targets, strict=True))
        ]
        for e in range(targets[0].shape[0])
    ]


def forward_kernel(
    slots_ref,
    router_ref,
    x_ref,
    gate_hbm,
    up_hbm,
    down_hbm,
    y0_ref,
    y1_ref,
    y2_ref,
    y3_ref,
    gates_ref,
    pre_ref,
    inner_ref,
    rows_hbm,
    gate_w,
    up_w,
    down_w,
    rows_v,
    out_v,
    gate_rows,
    w_sems,
    row_sem,
):
    step = pl.program_id(0)
    chunk = x_ref.shape[0]
    experts, depth, _ = rows_v.shape
    hidden = gate_w.shape[2]
    copies = weight_copies((gate_hbm, up_hbm, down_hbm), (gate_w, up_w, down_w), w_sems)

    def rows_copy(at):
        return pltpu.make_async_copy(
            rows_v, rows_hbm.at[:, pl.ds(at * depth, depth), :], row_sem.at[0]
        )

    @pl.when(step == 0)
    def _():
        for expert in copies:
            for copy in expert:
                copy.start()

    @pl.when(step > 0)
    def _():
        rows_copy(step - 1).wait()

    picks = []
    for b in range(chunk):
        tokens = x_ref[b]
        logits = dot(router_ref[...], tokens, nt_dims)
        exponent = jnp.exp(logits - jnp.max(logits, axis=0, keepdims=True))
        probs = exponent / jnp.sum(exponent, axis=0, keepdims=True)
        gates = probs[:experts]
        gates_ref[b] = gates
        pick = one_hot(slots_ref[b])
        spread_gates = jnp.broadcast_to(gates[:, None, :], (experts, CAP, gates.shape[1]))
        gated = jnp.sum(pick * spread_gates.reshape(pick.shape), axis=1, keepdims=True)
        spread(gate_rows, gated, b)
        pick = pick.astype(low)
        spread(rows_v, dot(pick, tokens).astype(low), b)
        picks.append(pick)
    rows_copy(step).start()

    for e in range(experts):

        @pl.when(step == 0)
        def _(e=e):
            for copy in copies[e]:
                copy.wait()

        rows = rows_v[e]
        gate_pre = dot(rows, gate_w[e])
        up_pre = dot(rows, up_w[e])
        pre_ref[e, :, :hidden] = gate_pre
        pre_ref[e, :, hidden:] = up_pre
        inner = (gate_pre * jax.nn.sigmoid(gate_pre) * up_pre).astype(low).astype(wide)
        scaled = (inner * gate_rows[e]).astype(low)
        inner_ref[e] = scaled
        out_v[e] = dot(scaled, down_w[e]).astype(low)

    for b in range(chunk):
        total = dot(picks[b], joined_rows(out_v, b), tn_dims).astype(low)
        share = total.shape[0] // 4
        for i, y_ref in enumerate((y0_ref, y1_ref, y2_ref, y3_ref)):
            y_ref[b] = total[i * share : (i + 1) * share]

    @pl.when(step == pl.num_programs(0) - 1)
    def _():
        rows_copy(step).wait()


def backward_kernel(
    slots_ref,
    gates_ref,
    g_ref,
    pre_ref,
    gate_hbm,
    up_hbm,
    down_hbm,
    x0_ref,
    x1_ref,
    x2_ref,
    x3_ref,
    grads_ref,
    dgate_ref,
    dup_ref,
    rows_hbm,
    gate_w,
    up_w,
    down_w,
    rows_v,
    out_v,
    gate_rows,
    grad_rows,
    w_sems,
    row_sem,
):
    step = pl.program_id(0)
    chunk = g_ref.shape[0]
    experts, depth, _ = rows_v.shape
    hidden = gate_w.shape[2]
    copies = weight_copies((gate_hbm, up_hbm, down_hbm), (gate_w, up_w, down_w), w_sems)

    def rows_copy(at):
        return pltpu.make_async_copy(
            rows_v, rows_hbm.at[:, pl.ds(at * depth, depth), :], row_sem.at[0]
        )

    @pl.when(step == 0)
    def _():
        for expert in copies:
            for copy in expert:
                copy.start()

    @pl.when(step > 0)
    def _():
        rows_copy(step - 1).wait()

    picks = []
    for b in range(chunk):
        gates = gates_ref[b]
        pick = one_hot(slots_ref[b])
        spread_gates = jnp.broadcast_to(gates[:, None, :], (experts, CAP, gates.shape[1]))
        gated = jnp.sum(pick * spread_gates.reshape(pick.shape), axis=1, keepdims=True)
        spread(gate_rows, gated, b)
        pick = pick.astype(low)
        spread(rows_v, dot(pick, g_ref[b]).astype(low), b)
        picks.append(pick)
    rows_copy(step).start()

    for e in range(experts):

        @pl.when(step == 0)
        def _(e=e):
            for copy in copies[e]:
                copy.wait()

        pulled = dot(rows_v[e], down_w[e], nt_dims)
        gate_pre = pre_ref[e, :, :hidden]
        up_pre = pre_ref[e, :, hidden:]
        sigmoid = jax.nn.sigmoid(gate_pre)
        silu = gate_pre * sigmoid
        inner = (silu * up_pre).astype(low).astype(wide)
        grad_rows[e] = jnp.sum(inner * pulled, axis=1, keepdims=True)
        grad_inner = pulled * gate_rows[e]
        dgate = (grad_inner * up_pre * sigmoid * (1.0 + gate_pre * (1.0 - sigmoid))).astype(low)
        dup = (grad_inner * silu).astype(low)
        dgate_ref[e] = dgate
        dup_ref[e] = dup
        out_v[e] = (dot(dgate, gate_w[e], nt_dims) + dot(dup, up_w[e], nt_dims)).astype(low)

    for b in range(chunk):
        total = dot(picks[b], joined_rows(out_v, b), tn_dims).astype(low)
        share = total.shape[0] // 4
        for i, x_ref in enumerate((x0_ref, x1_ref, x2_ref, x3_ref)):
            x_ref[b] = total[i * share : (i + 1) * share]
        per_row = picks[b].astype(wide) * joined_rows(grad_rows, b)
        grads_ref[b] = jnp.sum(per_row.reshape(experts, CAP, per_row.shape[1]), axis=1)

    @pl.when(step == pl.num_programs(0) - 1)
    def _():
        rows_copy(step).wait()


def expert_calls(blocks, tokens, width, experts, hidden, chunk=4):
    depth = chunk * CAP
    rows = blocks * CAP
    quarter = tokens // 4
    any_spec = pl.BlockSpec(memory_space=pl.ANY)

    def by_block(*shape):
        return pl.BlockSpec((chunk,) + shape, lambda i: (i,) + (0,) * len(shape))

    def by_row(last):
        return pl.BlockSpec((experts, depth, last), lambda i: (0, i, 0))

    def shaped(kind, *shape):
        return jax.ShapeDtypeStruct(shape, kind)

    weights = [
        pltpu.VMEM((experts, width, hidden), low),
        pltpu.VMEM((experts, width, hidden), low),
        pltpu.VMEM((experts, hidden, width), low),
    ]
    buffers = [
        pltpu.VMEM((experts, depth, width), low),
        pltpu.VMEM((experts, depth, width), low),
        pltpu.VMEM((experts, depth, 1), wide),
    ]
    sems = [pltpu.SemaphoreType.DMA((3, experts)), pltpu.SemaphoreType.DMA((1,))]
    params = pltpu.CompilerParams(
        dimension_semantics=("arbitrary",), vmem_limit_bytes=60 * 1024 * 1024
    )
    quarters = [shaped(low, blocks, quarter, width)] * 4
    quarter_specs = [by_block(quarter, width)] * 4
    flops = 2 * experts * rows * width * (3 * hidden + 2 * tokens)
    cost = pl.CostEstimate(
        flops=flops, bytes_accessed=experts * rows * width * 6, transcendentals=0
    )
    router_rows = 64

    forward = pl.pallas_call(
        forward_kernel,
        grid=(blocks // chunk,),
        in_specs=[
            by_block(experts, tokens),
            pl.BlockSpec((router_rows, width), lambda i: (0, 0)),
            by_block(tokens, width),
            any_spec,
            any_spec,
            any_spec,
        ],
        out_specs=quarter_specs
        + [by_block(experts, tokens), by_row(2 * hidden), by_row(hidden), any_spec],
        out_shape=quarters
        + [
            shaped(wide, blocks, experts, tokens),
            shaped(wide, experts, rows, 2 * hidden),
            shaped(low, experts, rows, hidden),
            shaped(low, experts, rows, width),
        ],
        scratch_shapes=weights + buffers + sems,
        compiler_params=params,
        cost_estimate=cost,
        name="experts_forward",
    )
    backward = pl.pallas_call(
        backward_kernel,
        grid=(blocks // chunk,),
        in_specs=[
            by_block(experts, tokens),
            by_block(experts, tokens),
            by_block(tokens, width),
            by_row(2 * hidden),
            any_spec,
            any_spec,
            any_spec,
        ],
        out_specs=quarter_specs
        + [by_block(experts, tokens), by_row(hidden), by_row(hidden), any_spec],
        out_shape=quarters
        + [
            shaped(wide, blocks, experts, tokens),
            shaped(low, experts, rows, hidden),
            shaped(low, experts, rows, hidden),
            shaped(low, experts, rows, width),
        ],
        scratch_shapes=weights + buffers + [pltpu.VMEM((experts, depth, 1), wide)] + sems,
        compiler_params=params,
        cost_estimate=cost,
        name="experts_backward",
    )
    return forward, backward


def on_device(
    hidden_in,
    w_query,
    w_key,
    w_value,
    w_output,
    w_router,
    gain_attn,
    gain_ffn,
    gain_query,
    gain_key,
    w_gate,
    w_up,
    w_down,
    expert_ids,
    grad_out,
):
    tokens_dev, model_width = hidden_in.shape
    local_experts, _, hidden_units = w_gate.shape
    expert_count = w_router.shape[1]
    grid = Grid()
    blocks = grid.ep * grid.tp
    weight_rows = model_width // blocks
    both = ("ep", "tp")
    inv_root = 1.0 / math.sqrt(HEAD_DIM)

    def gathered(values):
        return lax.all_gather(values, both, axis=0, tiled=True)

    named = jnp.any(
        expert_ids[None, :, :] == jnp.arange(expert_count, dtype=jnp.int32)[:, None, None], axis=2
    )
    before = (jnp.arange(tokens_dev)[:, None] <= jnp.arange(tokens_dev)[None, :]).astype(low)
    counted = jnp.dot(named.astype(low), before, preferred_element_type=wide)
    slots = jnp.where(named, counted, 0.0).astype(low)

    shared = jnp.concatenate(
        [
            w_router,
            jnp.stack([gain_attn, gain_ffn, gain_query, gain_key], axis=1),
            jnp.zeros((w_router.shape[0], tokens_dev - expert_count - 4), low),
        ],
        axis=1,
    )
    small_all = grid.gather(jnp.concatenate([shared, slots], axis=0), "xyzc")
    small_all = small_all.reshape(blocks, weight_rows + expert_count, tokens_dev)
    shared_full = small_all[:, :weight_rows].reshape(model_width, tokens_dev)
    slots_all = small_all[:, weight_rows:]
    router_full = shared_full[:, :expert_count]
    gains = shared_full[:, expert_count : expert_count + 4].astype(wide).T
    attn_gain, ffn_gain, query_gain, key_gain = gains[0], gains[1], gains[2], gains[3]
    query_full = gathered(w_query)
    key_full = gathered(w_key)
    value_full = grid.gather_rows(w_value, gather_orders)
    output_full = grid.gather_rows(w_output, gather_orders)
    upstream_all = gathered(grad_out[None])

    inputs_full = hidden_in.astype(wide)
    scale_attn = lax.rsqrt(jnp.mean(inputs_full * inputs_full, axis=-1, keepdims=True) + epsilon)
    unit_attn = inputs_full * scale_attn
    normed_attn = (unit_attn * attn_gain).astype(low)
    query_raw = jnp.dot(normed_attn, query_full, preferred_element_type=wide)
    key_raw = jnp.dot(normed_attn, key_full, preferred_element_type=wide)
    value_raw = jnp.dot(normed_attn, value_full, preferred_element_type=wide)
    scale_query = lax.rsqrt(jnp.mean(query_raw * query_raw, axis=-1, keepdims=True) + epsilon)
    unit_query = query_raw * scale_query
    scale_key = lax.rsqrt(jnp.mean(key_raw * key_raw, axis=-1, keepdims=True) + epsilon)
    unit_key = key_raw * scale_key
    cosines, sines = rope_tables(tokens_dev, HEAD_DIM)
    query_rot = rotate(
        (unit_query * query_gain).reshape(tokens_dev, HEADS, HEAD_DIM), cosines, sines
    ).astype(low)
    key_rot = rotate(
        (unit_key * key_gain).reshape(tokens_dev, HEADS, HEAD_DIM), cosines, sines
    ).astype(low)
    value_heads = value_raw.astype(low).reshape(tokens_dev, HEADS, HEAD_DIM)
    causal = jnp.arange(tokens_dev)[:, None] >= jnp.arange(tokens_dev)[None, :]
    scores = (
        jnp.einsum("qhd,khd->hqk", query_rot, key_rot, preferred_element_type=wide) * inv_root
    )
    scores = jnp.where(causal[None], scores, masked_value)
    exponent = jnp.exp(scores - jnp.max(scores, axis=-1, keepdims=True))
    att_probs = exponent / jnp.sum(exponent, axis=-1, keepdims=True)
    probs_low = att_probs.astype(low)
    attended = (
        jnp.einsum("hqk,khd->qhd", probs_low, value_heads, preferred_element_type=wide)
        .reshape(tokens_dev, model_width)
        .astype(low)
    )
    mixed = inputs_full + jnp.dot(attended, output_full, preferred_element_type=wide)
    scale_ffn = lax.rsqrt(jnp.mean(mixed * mixed, axis=-1, keepdims=True) + epsilon)
    unit_ffn = mixed * scale_ffn
    normed_ffn = (unit_ffn * ffn_gain).astype(low)
    normed_all = gathered(normed_ffn[None])
    router_probs = jax.nn.softmax(
        jnp.dot(normed_ffn, router_full, preferred_element_type=wide), axis=-1
    )

    first_expert = lax.axis_index("ep") * local_experts
    slots_here = lax.dynamic_slice_in_dim(slots_all, first_expert, local_experts, 1).astype(wide)
    router_turned = lax.dynamic_slice_in_dim(
        jnp.concatenate([router_full, router_full], axis=1), first_expert, expert_count, 1
    ).T
    forward, backward = expert_calls(
        blocks, tokens_dev, model_width, local_experts, hidden_units
    )
    *expert_parts, gates_all, pre_all, inner_scaled, rows_in = forward(
        slots_here, router_turned, normed_all, w_gate, w_up, w_down
    )
    expert_sum = jnp.concatenate(
        [
            grid.reduce_scatter(part, order)
            for part, order in zip(expert_parts, reduce_orders, strict=True)
        ],
        axis=0,
    )
    block_out = (mixed + expert_sum.astype(wide)).astype(low)

    *back_parts, gate_grads, grad_gate_part, grad_up_part, rows_up = backward(
        slots_here, gates_all, upstream_all, pre_all, w_gate, w_up, w_down
    )
    back_sum = jnp.concatenate(
        [
            grid.reduce_scatter(part, order)
            for part, order in zip(back_parts, reduce_orders, strict=True)
        ],
        axis=0,
    )
    gate_grads = lax.dynamic_update_slice_in_dim(
        jnp.zeros((blocks, expert_count, tokens_dev), wide), gate_grads, first_expert, 1
    )
    grad_probs = grid.reduce_scatter(gate_grads, "cyxz").T
    acc_down = jnp.einsum("erh,erd->ehd", inner_scaled, rows_up, preferred_element_type=wide)
    acc_gate = jnp.einsum("erd,erh->edh", rows_in, grad_gate_part, preferred_element_type=wide)
    acc_up = jnp.einsum("erd,erh->edh", rows_in, grad_up_part, preferred_element_type=wide)

    upstream = grad_out.astype(wide)
    grad_logits = router_probs * (
        grad_probs - jnp.sum(router_probs * grad_probs, axis=-1, keepdims=True)
    )
    grad_ffn_normed = back_sum.astype(wide) + jnp.dot(
        grad_logits, router_full.astype(wide).T, precision=lax.Precision.HIGHEST
    )
    grad_router_local = jnp.dot(
        normed_ffn.astype(wide).T, grad_logits, precision=lax.Precision.HIGHEST
    )
    grad_ffn_gain = jnp.sum(grad_ffn_normed * unit_ffn, axis=0)
    grad_mixed = upstream + rms_back(grad_ffn_normed, unit_ffn, ffn_gain, scale_ffn)
    grad_branch = grad_mixed.astype(low)

    def outer_sum(left, right, order):
        local = jnp.einsum("tc,te->ce", left, right, preferred_element_type=wide).astype(low)
        return grid.reduce_scatter(
            local.reshape(blocks, weight_rows, model_width), order
        ).astype(wide)

    grad_output = outer_sum(attended, grad_branch, "cyxz")
    grad_router = grid.reduce_scatter(
        grad_router_local.reshape(blocks, weight_rows, expert_count), "cxyz"
    )
    grad_attended = jnp.einsum(
        "te,de->td", grad_branch, output_full, preferred_element_type=wide
    ).astype(low)
    grad_heads = grad_attended.reshape(tokens_dev, HEADS, HEAD_DIM)
    grad_value_rows = (
        jnp.einsum("hqk,qhd->khd", probs_low, grad_heads, preferred_element_type=wide)
        .reshape(tokens_dev, model_width)
        .astype(low)
    )
    grad_value = outer_sum(normed_attn, grad_value_rows, "cxyz")
    grad_probs_att = jnp.einsum(
        "qhd,khd->hqk", grad_heads, value_heads, preferred_element_type=wide
    )
    grad_scores = (
        att_probs * (grad_probs_att - jnp.sum(att_probs * grad_probs_att, axis=-1, keepdims=True))
    ).astype(low)
    grad_qrot = (
        jnp.einsum("hqk,khd->qhd", grad_scores, key_rot, preferred_element_type=wide) * inv_root
    )
    grad_krot = (
        jnp.einsum("hqk,qhd->khd", grad_scores, query_rot, preferred_element_type=wide) * inv_root
    )
    grad_qnorm = unrotate(bounce(grad_qrot), cosines, sines).reshape(tokens_dev, model_width)
    grad_knorm = unrotate(bounce(grad_krot), cosines, sines).reshape(tokens_dev, model_width)
    grad_query_gain = jnp.sum(grad_qnorm * unit_query, axis=0)
    grad_key_gain = jnp.sum(grad_knorm * unit_key, axis=0)
    grad_query_raw = rms_back(grad_qnorm, unit_query, query_gain, scale_query).astype(low)
    grad_key_raw = rms_back(grad_knorm, unit_key, key_gain, scale_key).astype(low)
    grad_query = outer_sum(normed_attn, grad_query_raw, "cyxz")
    grad_key = outer_sum(normed_attn, grad_key_raw, "cxyz")
    grad_attn_normed = (
        jnp.einsum("te,ce->tc", grad_query_raw, query_full, preferred_element_type=wide)
        + jnp.einsum("te,ce->tc", grad_key_raw, key_full, preferred_element_type=wide)
        + jnp.einsum("te,ce->tc", grad_value_rows, value_full, preferred_element_type=wide)
    )
    grad_attn_gain = jnp.sum(grad_attn_normed * unit_attn, axis=0)
    grad_input = grad_mixed + rms_back(grad_attn_normed, unit_attn, attn_gain, scale_attn)
    gain_sums = jnp.stack([grad_attn_gain, grad_ffn_gain, grad_query_gain, grad_key_gain])
    gain_sums = grid.reduce_scatter(
        gain_sums.reshape(4, blocks, weight_rows).transpose(1, 0, 2), "cyxz"
    )
    return (
        block_out,
        grad_input,
        grad_query,
        grad_key,
        grad_value,
        grad_output,
        grad_router,
        gain_sums[0],
        gain_sums[1],
        gain_sums[2],
        gain_sums[3],
        acc_gate,
        acc_up,
        acc_down,
    )


def solution(mesh):
    placed = (
        P(("ep", "tp"), None),
        P(("ep", "tp"), None),
        P(("ep", "tp"), None),
        P(("ep", "tp"), None),
        P(("ep", "tp"), None),
        P(("ep", "tp"), None),
        P(("ep", "tp")),
        P(("ep", "tp")),
        P(("ep", "tp")),
        P(("ep", "tp")),
        P("ep", None, "tp"),
        P("ep", None, "tp"),
        P("ep", "tp", None),
        P(("ep", "tp"), None),
        P(("ep", "tp"), None),
    )
    return jax.shard_map(
        on_device,
        mesh=mesh,
        in_specs=placed,
        out_specs=(
            P(("ep", "tp"), None),
            P(("ep", "tp"), None),
            P(("ep", "tp"), None),
            P(("ep", "tp"), None),
            P(("ep", "tp"), None),
            P(("ep", "tp"), None),
            P(("ep", "tp"), None),
            P(("ep", "tp")),
            P(("ep", "tp")),
            P(("ep", "tp")),
            P(("ep", "tp")),
            P("ep", None, "tp"),
            P("ep", None, "tp"),
            P("ep", "tp", None),
        ),
        check_vma=False,
    )
```

time: 4590 us -> 1350 us (0.29)
  waiting for transfers between devices: 3670 us -> 555 us
  blocking collectives: 360 us -> 0 us
  starting transfers between devices: 10.4 us -> 244 us
  Pallas kernels: 0 us -> 203 us
  matrix products: 249 us -> 135 us
  other arithmetic: 128 us -> 78.2 us
    reduce_scatter x4 -> x0, waiting for transfers between devices: 2480 us -> none  [the longest x1 1280 us: on_device(): lax.psum_scatter(jnp.concatenate([jnp.einsum('tc,te->ce', normed_attn, gr...]
    all_gather x6 -> x4, waiting for transfers between devices: 1110 us -> 150 us  [gathered(): return lax.all_gather(values, both, axis=0, tiled=True)]
    ppermute x0 -> x144, waiting for transfers between devices: none -> 404 us  [the longest x72 234 us: shift(): return lax.ppermute(values, 'ep', pairs)]
    ppermute x0 -> x144, starting transfers between devices: none -> 243 us  [the longest x72 174 us: shift(): lax.ppermute(values, 'tp', [(i, (i + step) % count) for i in range(count)])]
    pallas_call x0 -> x2, Pallas kernels: none -> 203 us  [the longest x1 127 us: on_device(): backward(slots_here, gates_all, upstream_all, pre_all, w_gate, w_up, w_down)]
    all_to_all x2 -> x0, blocking collectives: 198 us -> none  [the longest x1 100 us: on_device(): lax.all_to_all(outgoing_grads, 'ep', split_axis=0, concat_axis=0, tiled=T...]
    dot_general x23 -> x21, matrix products: 239 us -> 126 us  [the longest x1 23 us: on_device(): jnp.einsum('erd,erh->edh', rows_in, grad_gate_part, preferred_element_typ...]
    unnamed x2 -> x0, blocking collectives: 87.8 us -> none
  transfers between devices with their start and end apart: 12 -> 148, of which waited for: 10 -> 57; matrix products, arithmetic and copies ran while one was open for 6% -> 18% of each run, Pallas kernels for 0% -> 6%
where the time goes in v1:
time: 1350 us
  waiting for transfers between devices  555 us (41%)
  starting transfers between devices  244 us (18%)
  Pallas kernels  203 us (15%)
  matrix products  135 us (10%)
  local copies, waits for them, and re-layouts  114 us (8%)
  other arithmetic  78.2 us (6%)
  between operations  17.6 us (1%)
    ppermute x72, waiting for transfers between devices, shift(): return lax.ppermute(values, 'ep', pairs)  234 us
    ppermute x72, starting transfers between devices, shift(): lax.ppermute(values, 'tp', [(i, (i + step) % count) for i in range(count)])  174 us
    ppermute x72, waiting for transfers between devices, shift(): lax.ppermute(values, 'tp', [(i, (i + step) % count) for i in range(count)])  169 us
    all_gather x4, waiting for transfers between devices, gathered(): return lax.all_gather(values, both, axis=0, tiled=True)  150 us
    pallas_call x1, Pallas kernels, on_device(): backward(slots_here, gates_all, upstream_all, pre_all, w_gate, w_up, w_down)  127 us
    pallas_call x1, Pallas kernels, on_device(): forward(slots_here, router_turned, normed_all, w_gate, w_up, w_down)  75.7 us
    ppermute x72, starting transfers between devices, shift(): return lax.ppermute(values, 'ep', pairs)  69.1 us
    convert_element_type x42, other arithmetic, reduce_scatter(): values = total.astype(kind)  46.6 us
  transfers between devices with their start and end apart: 148, of which 57 were waited for; matrix products, arithmetic and copies ran while one was open for 18% of the time, Pallas kernels for 6%

profile of v1, /device:TPU:0, one launch (start us, length us, event | category | flops | bytes accessed | tf_op | source)
XLA Modules:
  0.0 1346.9 jit_solution(18029284418569031999)
XLA Ops:
  69.0 13.1 collective-permute-done.43
  82.1 14.1 %collective-permute-start.44 = (bf16[1,2,1,1,16,2048]{5,4,3,2,1,0:T(8,128)(2,1)S(1)}, bf16[1,2,1,1,16,2048]{5,4,3,2,1,0:T(8,128)(2,1)S(1)}, u32[]{:S(2)}, u32[]{:S(2)}) collective-permute-start(bf16[1,2,1,1,16,2048]{5,4,3,2,1,0:T(8,128)(2,1)S(1)} %constant_dynamic-update-slice_fusion.19), channel_id=1, source_target_pairs={{0,2},{1,3},{2,0},{3,1},{4,6},{5,7},{6,4},{7,5},{8,10},{9,11},{10,... | collective-permute-start | bytes 393224 | tf_op jit(solution)/shard_map/ppermute | solution.py:80
  96.1 10.4 collective-permute-done.44
  111.6 6.8 collective-permute-done.49
  118.4 6.5 collective-permute-done.50
  124.9 7.3 collective-permute-start.51
  147.1 7.8 collective-permute-start.3
  180.7 28.4 %collective-permute-done.46 = bf16[1,2,1,4,16,2048]{5,4,3,2,1,0:T(8,128)(2,1)S(1)} collective-permute-done((bf16[1,2,1,4,16,2048]{5,4,3,2,1,0:T(8,128)(2,1)S(1)}, bf16[1,2,1,4,16,2048]{5,4,3,2,1,0:T(8,128)(2,1)S(1)}, u32[]{:S(2)}, u32[]{:S(2)}) %collective-permute-start.46) | collective-permute-done | bytes 524320 | tf_op jit(solution)/shard_map/ppermute | solution.py:86
  278.8 110.0 %all-gather.11.cloned.1.call-done = bf16[4096,2048]{1,0:T(8,128)(2,1)} async-done(((bf16[128,2048]{1,0:T(8,128)(2,1)}), bf16[4096,2048]{1,0:T(8,128)(2,1)}) %all-gather.11.cloned.1.call-update) | async-done | bytes 16777232 | tf_op jit(solution)/shard_map/all_gather | solution.py:468
  388.9 75.7 %experts_forward.1 = (bf16[32,32,2048]{2,1,0:T(8,128)(2,1)}, bf16[32,32,2048]{2,1,0:T(8,128)(2,1)}, bf16[32,32,2048]{2,1,0:T(8,128)(2,1)}, bf16[32,32,2048]{2,1,...) custom-call(f32[32,8,128]{2,1,0:T(8,128)} %dynamic-slice_convert_fus, ...), custom_call_target="tpu_custom_call" | custom-call | flops 34359738368 | bytes 100663296 | tf_op jit(solution)/shard_map/experts_forward/pallas_call | solution.py:547
  464.5 40.3 %all-gather.13.cloned.1.call-done = bf16[4096,2048]{1,0:T(8,128)(2,1)} async-done(((bf16[128,2048]{1,0:T(8,128)(2,1)}), bf16[4096,2048]{1,0:T(8,128)(2,1)}) %all-gather.13.cloned.1.call-update) | async-done | bytes 16777232 | tf_op jit(solution)/shard_map/all_gather | solution.py:468
  504.9 127.4 %experts_backward.1 = (bf16[32,32,2048]{2,1,0:T(8,128)(2,1)}, bf16[32,32,2048]{2,1,0:T(8,128)(2,1)}, bf16[32,32,2048]{2,1,0:T(8,128)(2,1)}, bf16[32,32,2048]{2,1...) custom-call(f32[32,8,128]{2,1,0:T(8,128)} %dynamic-slice_convert_fus, ...), custom_call_target="tpu_custom_call" | custom-call | flops 34359738368 | bytes 100663296 | tf_op jit(solution)/shard_map/experts_backward/pallas_call | solution.py:559
  645.0 23.0 %fusion.173 = f32[8,2048,256]{2,1,0:T(8,128)} fusion(bf16[8,1024,2048]{2,1,0:T(8,128)(2,1)} %get-tuple-element.41, bf16[8,1024,256]{2,1,0:T(8,128)(2,1)S(1)} %copy-done.80), kind=kOutput, calls=%fused_computation.518 | convolution fusion | flops 8589934592 | bytes 54525952 | tf_op jit(solution)/shard_map/erd,erh->edh/dot_general | solution.py:574
  668.7 21.1 %fusion.174 = f32[8,2048,256]{2,1,0:T(8,128)} fusion(bf16[8,1024,2048]{2,1,0:T(8,128)(2,1)} %get-tuple-element.41, bf16[8,1024,256]{2,1,0:T(8,128)(2,1)} %get-tuple-element.43), kind=kOutput, calls=%fused_computation.519 | convolution fusion | flops 8589934592 | bytes 54525952 | tf_op jit(solution)/shard_map/erd,erh->edh/dot_general | solution.py:575
  703.4 19.8 %fusion.175 = f32[8,256,2048]{2,1,0:T(8,128)} fusion(bf16[8,1024,256]{2,1,0:T(8,128)(2,1)} %get-tuple-element.44, bf16[8,1024,2048]{2,1,0:T(8,128)(2,1)} %get-tuple-element.45), kind=kOutput, calls=%fused_computation.520 | convolution fusion | flops 8589934592 | bytes 54525952 | tf_op jit(solution)/shard_map/erh,erd->ehd/dot_general | solution.py:573
  772.9 40.7 %collective-permute-done.55 = bf16[2,4,32,2048]{3,2,1,0:T(8,128)(2,1)} collective-permute-done((bf16[2,4,32,2048]{3,2,1,0:T(8,128)(2,1)S(1)}, bf16[2,4,32,2048]{3,2,1,0:T(8,128)(2,1)}, u32[]{:S(2)}, u32[]{:S(2)}) %collective-permute-start.55) | collective-permute-done | bytes 1048608 | tf_op jit(solution)/shard_map/ppermute | solution.py:86
  819.5 16.5 %collective-permute-done.79 = bf16[2,4,32,2048]{3,2,1,0:T(8,128)(2,1)S(1)} collective-permute-done((bf16[2,4,32,2048]{3,2,1,0:T(8,128)(2,1)S(1)}, bf16[2,4,32,2048]{3,2,1,0:T(8,128)(2,1)S(1)}, u32[]{:S(2)}, u32[]{:S(2)}) %collective-permute-start.79) | collective-permute-done | bytes 1048608 | tf_op jit(solution)/shard_map/ppermute | solution.py:86
  845.0 12.6 collective-permute-done.91
  871.1 10.2 collective-permute-done.99
  881.4 15.5 %collective-permute-start.92 = (bf16[2,32,2048]{2,1,0:T(8,128)(2,1)S(1)}, bf16[2,32,2048]{2,1,0:T(8,128)(2,1)S(1)}, u32[]{:S(2)}, u32[]{:S(2)}) collective-permute-start(bf16[2,32,2048]{2,1,0:T(8,128)(2,1)S(1)} %get-tuple-element.96), channel_id=1, source_target_pairs={{0,3},{1,0},{2,1},{3,2},{4,7},{5,4},{6,5},{7,6},{8,11},{9,8},{10,9... | collective-permute-start | bytes 786440 | tf_op jit(solution)/shard_map/ppermute | solution.py:80
  909.5 10.0 collective-permute-start.68
  934.1 12.1 collective-permute-done.69
  947.6 12.0 collective-permute-done.101
  1153.5 24.0 %collective-permute-done.127 = bf16[2,4,64,2048]{3,2,1,0:T(8,128)(2,1)} collective-permute-done((bf16[2,4,64,2048]{3,2,1,0:T(8,128)(2,1)}, bf16[2,4,64,2048]{3,2,1,0:T(8,128)(2,1)}, u32[]{:S(2)}, u32[]{:S(2)}) %collective-permute-start.127) | collective-permute-done | bytes 2097184 | tf_op jit(solution)/shard_map/ppermute | solution.py:86
  1188.2 41.3 %collective-permute-done.115 = bf16[2,4,64,2048]{3,2,1,0:T(8,128)(2,1)} collective-permute-done((bf16[2,4,64,2048]{3,2,1,0:T(8,128)(2,1)}, bf16[2,4,64,2048]{3,2,1,0:T(8,128)(2,1)}, u32[]{:S(2)}, u32[]{:S(2)}) %collective-permute-start.115) | collective-permute-done | bytes 2097184 | tf_op jit(solution)/shard_map/ppermute | solution.py:86
  1235.8 16.1 %collective-permute-done.128 = bf16[4,64,2048]{2,1,0:T(8,128)(2,1)S(1)} collective-permute-done((bf16[4,64,2048]{2,1,0:T(8,128)(2,1)S(1)}, bf16[4,64,2048]{2,1,0:T(8,128)(2,1)S(1)}, u32[]{:S(2)}, u32[]{:S(2)}) %collective-permute-start.128) | collective-permute-done | bytes 1048608 | tf_op jit(solution)/shard_map/ppermute | solution.py:86
  1254.9 9.6 collective-permute-done.116
  1264.9 6.5 collective-permute-done.110
  1276.0 9.7 collective-permute-done.130
  1301.4 8.0 collective-permute-done.124
  1309.4 6.8 collective-permute-start.113
  1320.7 11.2 collective-permute-done.118
  (787 shorter events, 554.7 us)
Async XLA Ops:
  7.2 240.4 %all-gather.7.cloned.1.call-start = ((), (), s32[]{:S(2)}) async-start(), calls=%async_computation | async-start | bytes 8650752 | tf_op jit(solution)/shard_map/all_gather | solution.py:468
  7.9 245.8 %all-gather.9.cloned.1.call-start = ((), (), s32[]{:S(2)}) async-start(), calls=%async_computation.1 | async-start | bytes 8650752 | tf_op jit(solution)/shard_map/all_gather | solution.py:468
  23.2 365.6 %all-gather.11.cloned.1.call-start = ((), (), s32[]{:S(2)}) async-start(), calls=%async_computation.2 | async-start | bytes 17301504 | tf_op jit(solution)/shard_map/all_gather | solution.py:468
  59.8 83.5 %collective-permute-start.21 = (bf16[1,2,1,1,16,2048]{5,4,3,2,1,0:T(8,128)(2,1)S(1)}, bf16[1,2,1,1,16,2048]{5,4,3,2,1,0:T(8,128)(2,1)S(1)}, u32[]{:S(2)}, u32[]{:S(2)}) collective-permute-start(bf16[1,2,1,1,16,2048]{5,4,3,2,1,0:T(8,128)(2,1)S(1)} %constant_dynamic-update-slice_fusion.59), channel_id=1, source_target_pairs={{0,3},{1,0},{2,1},{3,2},{4,7},{5,4},{6,5},{7,6},{8,11},{9,8},{10,9... | collective-permute-start | bytes 393224 | tf_op jit(solution)/shard_map/ppermute | solution.py:80
  63.9 76.7 %collective-permute-start.20 = (bf16[1,2,1,1,16,2048]{5,4,3,2,1,0:T(8,128)(2,1)S(1)}, bf16[1,2,1,1,16,2048]{5,4,3,2,1,0:T(8,128)(2,1)S(1)}, u32[]{:S(2)}, u32[]{:S(2)}) collective-permute-start(bf16[1,2,1,1,16,2048]{5,4,3,2,1,0:T(8,128)(2,1)S(1)} %constant_dynamic-update-slice_fusion.59), channel_id=1, source_target_pairs={{0,2},{1,3},{2,0},{3,1},{4,6},{5,7},{6,4},{7,5},{8,10},{9,11},{10,... | collective-permute-start | bytes 393224 | tf_op jit(solution)/shard_map/ppermute | solution.py:80
  64.6 73.1 %collective-permute-start.19 = (bf16[1,2,1,1,16,2048]{5,4,3,2,1,0:T(8,128)(2,1)S(1)}, bf16[1,2,1,1,16,2048]{5,4,3,2,1,0:T(8,128)(2,1)S(1)}, u32[]{:S(2)}, u32[]{:S(2)}) collective-permute-start(bf16[1,2,1,1,16,2048]{5,4,3,2,1,0:T(8,128)(2,1)S(1)} %constant_dynamic-update-slice_fusion.59), channel_id=1, source_target_pairs={{0,1},{1,2},{2,3},{3,0},{4,5},{5,6},{6,7},{7,4},{8,9},{9,10},{10,1... | collective-permute-start | bytes 393224 | tf_op jit(solution)/shard_map/ppermute | solution.py:80
  66.0 89.0 %collective-permute-start.27 = (bf16[2,1,1,1,16,2048]{5,4,3,2,1,0:T(8,128)(2,1)S(1)}, bf16[2,1,1,1,16,2048]{5,4,3,2,1,0:T(8,128)(2,1)S(1)}, u32[]{:S(2)}, u32[]{:S(2)}) collective-permute-start(bf16[2,1,1,1,16,2048]{5,4,3,2,1,0:T(8,128)(2,1)S(1)} %constant_dynamic-update-slice_fusion.49), channel_id=1, source_target_pairs={{0,3},{1,0},{2,1},{3,2},{4,7},{5,4},{6,5},{7,6},{8,11},{9,8},{10,9... | collective-permute-start | bytes 393224 | tf_op jit(solution)/shard_map/ppermute | solution.py:80
  168.3 44.3 %collective-permute-start.28 = (bf16[2,1,1,4,16,2048]{5,4,3,2,1,0:T(8,128)(2,1)S(1)}, bf16[2,1,1,4,16,2048]{5,4,3,2,1,0:T(8,128)(2,1)S(1)}, u32[]{:S(2)}, u32[]{:S(2)}) collective-permute-start(bf16[2,1,1,4,16,2048]{5,4,3,2,1,0:T(8,128)(2,1)S(1)} %constant_dynamic-update-slice_fusion.45), channel_id=1, source_target_pairs={{0,8},{4,12},{8,0},{12,4},{16,24},{20,28},{24,16},{28,20},{1,9},{5... | collective-permute-start | bytes 1572872 | tf_op jit(solution)/shard_map/ppermute | solution.py:86
  275.3 229.6 %all-gather.13.cloned.1.call-start = ((), (), s32[]{:S(2)}) async-start(), calls=%async_computation.3 | async-start | bytes 17301504 | tf_op jit(solution)/shard_map/all_gather | solution.py:468
  642.8 112.9 %collective-permute-start.72 = (bf16[2,2,4,32,2048]{4,3,0,2,1:T(8,128)(2,1)}, bf16[2,2,4,32,2048]{4,3,0,2,1:T(8,128)(2,1)}, u32[]{:S(2)}, u32[]{:S(2)}) collective-permute-start(bf16[2,2,4,32,2048]{4,3,0,2,1:T(8,128)(2,1)} %bitcast.564), channel_id=1, source_target_pairs={{0,4},{4,0},{8,12},{12,8},{16,20},{20,16},{24,28},{28,24},{1,5},{5... | collective-permute-start | bytes 6291464 | tf_op jit(solution)/shard_map/ppermute | solution.py:86
  643.1 115.3 %collective-permute-start.66 = (bf16[2,2,4,32,2048]{4,3,1,2,0:T(8,128)(2,1)}, bf16[2,2,4,32,2048]{4,3,1,2,0:T(8,128)(2,1)}, u32[]{:S(2)}, u32[]{:S(2)}) collective-permute-start(bf16[2,2,4,32,2048]{4,3,1,2,0:T(8,128)(2,1)} %bitcast.565), channel_id=1, source_target_pairs={{0,4},{4,0},{8,12},{12,8},{16,20},{20,16},{24,28},{28,24},{1,5},{5... | collective-permute-start | bytes 6291464 | tf_op jit(solution)/shard_map/ppermute | solution.py:86
  695.2 57.6 %collective-permute-start.54 = (bf16[2,2,4,32,2048]{4,3,2,1,0:T(8,128)(2,1)}, bf16[2,2,4,32,2048]{4,3,2,1,0:T(8,128)(2,1)}, u32[]{:S(2)}, u32[]{:S(2)}) collective-permute-start(bf16[2,2,4,32,2048]{4,3,2,1,0:T(8,128)(2,1)} %dynamic-slice_bitcast_fusion.7), channel_id=1, source_target_pairs={{0,4},{4,0},{8,12},{12,8},{16,20},{20,16},{24,28},{28,24},{1,5},{5... | collective-permute-start | bytes 6291464 | tf_op jit(solution)/shard_map/ppermute | solution.py:86
  761.2 55.5 %collective-permute-start.73 = (bf16[2,4,32,2048]{3,2,0,1:T(8,128)(2,1)S(1)}, bf16[2,4,32,2048]{3,2,0,1:T(8,128)(2,1)S(1)}, u32[]{:S(2)}, u32[]{:S(2)}) collective-permute-start(bf16[2,4,32,2048]{3,2,0,1:T(8,128)(2,1)S(1)} %dynamic-slice_bitcast_fusion.16), channel_id=1, source_target_pairs={{0,8},{4,12},{8,0},{12,4},{16,24},{20,28},{24,16},{28,20},{1,9},{5... | collective-permute-start | bytes 3145736 | tf_op jit(solution)/shard_map/ppermute | solution.py:86
  765.0 76.7 %collective-permute-start.67 = (bf16[2,4,32,2048]{3,2,0,1:T(8,128)(2,1)S(1)}, bf16[2,4,32,2048]{3,2,0,1:T(8,128)(2,1)S(1)}, u32[]{:S(2)}, u32[]{:S(2)}) collective-permute-start(bf16[2,4,32,2048]{3,2,0,1:T(8,128)(2,1)S(1)} %dynamic-slice_bitcast_fusion.17), channel_id=1, source_target_pairs={{0,16},{4,20},{8,24},{12,28},{16,0},{20,4},{24,8},{28,12},{1,17},{... | collective-permute-start | bytes 3145736 | tf_op jit(solution)/shard_map/ppermute | solution.py:86
  767.2 46.4 %collective-permute-start.55 = (bf16[2,4,32,2048]{3,2,1,0:T(8,128)(2,1)S(1)}, bf16[2,4,32,2048]{3,2,1,0:T(8,128)(2,1)}, u32[]{:S(2)}, u32[]{:S(2)}) collective-permute-start(bf16[2,4,32,2048]{3,2,1,0:T(8,128)(2,1)S(1)} %dynamic-slice_bitcast_fusion.19), channel_id=1, source_target_pairs={{0,16},{4,20},{8,24},{12,28},{16,0},{20,4},{24,8},{28,12},{1,17},{... | collective-permute-start | bytes 3145736 | tf_op jit(solution)/shard_map/ppermute | solution.py:86
  768.9 67.1 %collective-permute-start.79 = (bf16[2,4,32,2048]{3,2,1,0:T(8,128)(2,1)S(1)}, bf16[2,4,32,2048]{3,2,1,0:T(8,128)(2,1)S(1)}, u32[]{:S(2)}, u32[]{:S(2)}) collective-permute-start(bf16[2,4,32,2048]{3,2,1,0:T(8,128)(2,1)S(1)} %dynamic-slice_bitcast_fusion.15), channel_id=1, source_target_pairs={{0,16},{4,20},{8,24},{12,28},{16,0},{20,4},{24,8},{28,12},{1,17},{... | collective-permute-start | bytes 3145736 | tf_op jit(solution)/shard_map/ppermute | solution.py:86
  771.0 46.4 %collective-permute-start.97 = (bf16[2,4,32,2048]{3,2,0,1:T(8,128)(2,1)S(1)}, bf16[2,4,32,2048]{3,2,0,1:T(8,128)(2,1)S(1)}, u32[]{:S(2)}, u32[]{:S(2)}) collective-permute-start(bf16[2,4,32,2048]{3,2,0,1:T(8,128)(2,1)S(1)} %dynamic-slice_bitcast_fusion.12), channel_id=1, source_target_pairs={{0,8},{4,12},{8,0},{12,4},{16,24},{20,28},{24,16},{28,20},{1,9},{5... | collective-permute-start | bytes 3145736 | tf_op jit(solution)/shard_map/ppermute | solution.py:86
  816.7 46.0 %collective-permute-start.85 = (bf16[2,4,32,2048]{3,2,1,0:T(8,128)(2,1)S(1)}, bf16[2,4,32,2048]{3,2,1,0:T(8,128)(2,1)S(1)}, u32[]{:S(2)}, u32[]{:S(2)}) collective-permute-start(bf16[2,4,32,2048]{3,2,1,0:T(8,128)(2,1)S(1)} %dynamic-slice_bitcast_fusion.14), channel_id=1, source_target_pairs={{0,8},{4,12},{8,0},{12,4},{16,24},{20,28},{24,16},{28,20},{1,9},{5... | collective-permute-start | bytes 3145736 | tf_op jit(solution)/shard_map/ppermute | solution.py:86
  817.3 40.3 %collective-permute-start.91 = (bf16[2,4,32,2048]{3,2,0,1:T(8,128)(2,1)S(1)}, bf16[2,4,32,2048]{3,2,0,1:T(8,128)(2,1)S(1)}, u32[]{:S(2)}, u32[]{:S(2)}) collective-permute-start(bf16[2,4,32,2048]{3,2,0,1:T(8,128)(2,1)S(1)} %dynamic-slice_bitcast_fusion.13), channel_id=1, source_target_pairs={{0,16},{4,20},{8,24},{12,28},{16,0},{20,4},{24,8},{28,12},{1,17},{... | collective-permute-start | bytes 3145736 | tf_op jit(solution)/shard_map/ppermute | solution.py:86
  836.0 139.6 %collective-permute-start.56 = (bf16[4,32,2048]{2,1,0:T(8,128)(2,1)S(1)}, bf16[4,32,2048]{2,1,0:T(8,128)(2,1)S(1)}, u32[]{:S(2)}, u32[]{:S(2)}) collective-permute-start(bf16[4,32,2048]{2,1,0:T(8,128)(2,1)S(1)} %dynamic-slice_bitcast_fusion.24), channel_id=1, source_target_pairs={{0,8},{4,12},{8,0},{12,4},{16,24},{20,28},{24,16},{28,20},{1,9},{5... | collective-permute-start | bytes 1572872 | tf_op jit(solution)/shard_map/ppermute | solution.py:86
  839.7 142.5 %collective-permute-start.80 = (bf16[4,32,2048]{2,1,0:T(8,128)(2,1)S(1)}, bf16[4,32,2048]{2,1,0:T(8,128)(2,1)S(1)}, u32[]{:S(2)}, u32[]{:S(2)}) collective-permute-start(bf16[4,32,2048]{2,1,0:T(8,128)(2,1)S(1)} %dynamic-slice_bitcast_fusion.22), channel_id=1, source_target_pairs={{0,8},{4,12},{8,0},{12,4},{16,24},{20,28},{24,16},{28,20},{1,9},{5... | collective-permute-start | bytes 1572872 | tf_op jit(solution)/shard_map/ppermute | solution.py:86
  932.0 50.7 %collective-permute-start.62 = (bf16[4,32,2048]{2,1,0:T(8,128)(2,1)S(1)}, bf16[4,32,2048]{2,1,0:T(8,128)(2,1)S(1)}, u32[]{:S(2)}, u32[]{:S(2)}) collective-permute-start(bf16[4,32,2048]{2,1,0:T(8,128)(2,1)S(1)} %dynamic-slice_bitcast_fusion.23), channel_id=1, source_target_pairs={{0,16},{4,20},{8,24},{12,28},{16,0},{20,4},{24,8},{28,12},{1,17},{... | collective-permute-start | bytes 1572872 | tf_op jit(solution)/shard_map/ppermute | solution.py:86
  933.3 51.4 %collective-permute-start.86 = (bf16[4,32,2048]{2,1,0:T(8,128)(2,1)S(1)}, bf16[4,32,2048]{2,1,0:T(8,128)(2,1)S(1)}, u32[]{:S(2)}, u32[]{:S(2)}) collective-permute-start(bf16[4,32,2048]{2,1,0:T(8,128)(2,1)S(1)} %dynamic-slice_bitcast_fusion.21), channel_id=1, source_target_pairs={{0,16},{4,20},{8,24},{12,28},{16,0},{20,4},{24,8},{28,12},{1,17},{... | collective-permute-start | bytes 1572872 | tf_op jit(solution)/shard_map/ppermute | solution.py:86
  975.8 41.1 %collective-permute-start.59 = (bf16[32,2048]{1,0:T(8,128)(2,1)S(1)}, bf16[32,2048]{1,0:T(8,128)(2,1)S(1)}, u32[]{:S(2)}, u32[]{:S(2)}) collective-permute-start(bf16[32,2048]{1,0:T(8,128)(2,1)S(1)} %get-tuple-element.121), channel_id=1, source_target_pairs={{0,1},{1,2},{2,3},{3,0},{4,5},{5,6},{6,7},{7,4},{8,9},{9,10},{10,1... | collective-permute-start | bytes 393224 | tf_op jit(solution)/shard_map/ppermute | solution.py:80
  1079.2 43.8 %collective-permute-start.126 = (bf16[2,2,4,64,2048]{4,3,2,1,0:T(8,128)(2,1)}, bf16[2,2,4,64,2048]{4,3,2,1,0:T(8,128)(2,1)}, u32[]{:S(2)}, u32[]{:S(2)}) collective-permute-start(bf16[2,2,4,64,2048]{4,3,2,1,0:T(8,128)(2,1)} %dynamic-slice_bitcast_fusion), channel_id=1, source_target_pairs={{0,4},{4,0},{8,12},{12,8},{16,20},{20,16},{24,28},{28,24},{1,5},{5... | collective-permute-start | bytes 12582920 | tf_op jit(solution)/shard_map/ppermute | solution.py:86
  1128.6 48.9 %collective-permute-start.127 = (bf16[2,4,64,2048]{3,2,1,0:T(8,128)(2,1)}, bf16[2,4,64,2048]{3,2,1,0:T(8,128)(2,1)}, u32[]{:S(2)}, u32[]{:S(2)}) collective-permute-start(bf16[2,4,64,2048]{3,2,1,0:T(8,128)(2,1)} %dynamic-slice_bitcast_fusion.2), channel_id=1, source_target_pairs={{0,16},{4,20},{8,24},{12,28},{16,0},{20,4},{24,8},{28,12},{1,17},{... | collective-permute-start | bytes 6291464 | tf_op jit(solution)/shard_map/ppermute | solution.py:86
  1135.6 48.9 %collective-permute-start.121 = (bf16[2,4,64,2048]{3,2,1,0:T(8,128)(2,1)}, bf16[2,4,64,2048]{3,2,1,0:T(8,128)(2,1)}, u32[]{:S(2)}, u32[]{:S(2)}) collective-permute-start(bf16[2,4,64,2048]{3,2,1,0:T(8,128)(2,1)} %dynamic-slice_bitcast_fusion.3), channel_id=1, source_target_pairs={{0,8},{4,12},{8,0},{12,4},{16,24},{20,28},{24,16},{28,20},{1,9},{5... | collective-permute-start | bytes 6291464 | tf_op jit(solution)/shard_map/ppermute | solution.py:86
  1143.4 86.0 %collective-permute-start.115 = (bf16[2,4,64,2048]{3,2,1,0:T(8,128)(2,1)}, bf16[2,4,64,2048]{3,2,1,0:T(8,128)(2,1)}, u32[]{:S(2)}, u32[]{:S(2)}) collective-permute-start(bf16[2,4,64,2048]{3,2,1,0:T(8,128)(2,1)} %dynamic-slice_bitcast_fusion.4), channel_id=1, source_target_pairs={{0,8},{4,12},{8,0},{12,4},{16,24},{20,28},{24,16},{28,20},{1,9},{5... | collective-permute-start | bytes 6291464 | tf_op jit(solution)/shard_map/ppermute | solution.py:86
  1152.4 80.9 %collective-permute-start.109 = (bf16[2,4,64,2048]{3,2,1,0:T(8,128)(2,1)S(1)}, bf16[2,4,64,2048]{3,2,1,0:T(8,128)(2,1)S(1)}, u32[]{:S(2)}, u32[]{:S(2)}) collective-permute-start(bf16[2,4,64,2048]{3,2,1,0:T(8,128)(2,1)S(1)} %dynamic-slice_bitcast_fusion.5), channel_id=1, source_target_pairs={{0,16},{4,20},{8,24},{12,28},{16,0},{20,4},{24,8},{28,12},{1,17},{... | collective-permute-start | bytes 6291464 | tf_op jit(solution)/shard_map/ppermute | solution.py:86
  1180.0 71.8 %collective-permute-start.128 = (bf16[4,64,2048]{2,1,0:T(8,128)(2,1)S(1)}, bf16[4,64,2048]{2,1,0:T(8,128)(2,1)S(1)}, u32[]{:S(2)}, u32[]{:S(2)}) collective-permute-start(bf16[4,64,2048]{2,1,0:T(8,128)(2,1)S(1)} %dynamic-slice_bitcast_fusion.8), channel_id=1, source_target_pairs={{0,8},{4,12},{8,0},{12,4},{16,24},{20,28},{24,16},{28,20},{1,9},{5... | collective-permute-start | bytes 3145736 | tf_op jit(solution)/shard_map/ppermute | solution.py:86
  1187.0 67.4 %collective-permute-start.122 = (bf16[4,64,2048]{2,1,0:T(8,128)(2,1)S(1)}, bf16[4,64,2048]{2,1,0:T(8,128)(2,1)S(1)}, u32[]{:S(2)}, u32[]{:S(2)}) collective-permute-start(bf16[4,64,2048]{2,1,0:T(8,128)(2,1)S(1)} %dynamic-slice_bitcast_fusion.9), channel_id=1, source_target_pairs={{0,16},{4,20},{8,24},{12,28},{16,0},{20,4},{24,8},{28,12},{1,17},{... | collective-permute-start | bytes 3145736 | tf_op jit(solution)/shard_map/ppermute | solution.py:86
  1272.8 44.4 %collective-permute-start.117 = (bf16[64,2048]{1,0:T(8,128)(2,1)S(1)}, bf16[64,2048]{1,0:T(8,128)(2,1)S(1)}, u32[]{:S(2)}, u32[]{:S(2)}) collective-permute-start(bf16[64,2048]{1,0:T(8,128)(2,1)S(1)} %get-tuple-element.88), channel_id=1, source_target_pairs={{0,3},{1,0},{2,1},{3,2},{4,7},{5,4},{6,5},{7,6},{8,11},{9,8},{10,9... | collective-permute-start | bytes 786440 | tf_op jit(solution)/shard_map/ppermute | solution.py:80
  (205 other events, 3634.0 us)
Sparse Core Ops, SparseCore 0:
  11.0 101.0 all-gather.6
  115.0 99.4 all-gather.8
  275.4 113.3 all-gather.10
  391.7 113.1 all-gather.12

commit v2 on v1

v2 whole, which is shorter than its diff:
```python
import functools
import math

import jax
import jax.numpy as jnp
from jax import lax
from jax.experimental import pallas as pl
from jax.experimental.pallas import tpu as pltpu
from jax.sharding import PartitionSpec as P

HEADS = 16
HEAD_DIM = 128
CAP = 32


epsilon = 1e-05
rope_base = 10000.0
masked_value = -1e30
low = jnp.bfloat16
wide = jnp.float32


def rope_tables(length, head_dim):
    half_dim = head_dim // 2
    position = jnp.arange(length, dtype=jnp.float32)
    frequency = jnp.exp(
        jnp.arange(half_dim, dtype=jnp.float32) * (-2.0 * math.log(rope_base) / head_dim)
    )
    angles = position[:, None] * frequency[None, :]
    return (jnp.cos(angles)[:, None, :], jnp.sin(angles)[:, None, :])


def rotate(values, cosines, sines):
    half_dim = values.shape[-1] // 2
    first_half = values[..., :half_dim]
    second = values[..., half_dim:]
    return jnp.concatenate(
        [first_half * cosines - second * sines, second * cosines + first_half * sines], axis=-1
    )


def unrotate(grad_vals, cosines, sines):
    half_dim = grad_vals.shape[-1] // 2
    first_half = grad_vals[..., :half_dim]
    second = grad_vals[..., half_dim:]
    return jnp.concatenate(
        [first_half * cosines + second * sines, second * cosines - first_half * sines], axis=-1
    )


def rms_back(grad_normed, unit_vals, gain_vals, inv_scale):
    scaled = grad_normed * gain_vals
    return inv_scale * (scaled - unit_vals * jnp.mean(scaled * unit_vals, axis=-1, keepdims=True))


def bounce(values):
    return lax.optimization_barrier(values.astype(low)).astype(wide)


def after(values, *needs):
    return lax.optimization_barrier((values, needs))[0]


def together(*values):
    return lax.optimization_barrier(values)


class Grid:
    axes = "yxcuw"

    def __init__(self):
        self.ep, self.tp = lax.axis_size("ep"), lax.axis_size("tp")
        chips = self.ep // 2
        nx = math.isqrt(chips)
        while chips % nx:
            nx -= 1
        nw = 2 - self.tp % 2
        self.size = {"y": chips // nx, "x": nx, "c": 2, "u": self.tp // nw, "w": nw}
        self.stride = {"y": 2 * nx, "x": 2, "c": 1, "u": nw, "w": 1}
        self.shape = tuple(self.size[axis] for axis in self.axes)

    def place(self, axis):
        whole = lax.axis_index("tp" if axis in "uw" else "ep")
        return whole // self.stride[axis] % self.size[axis]

    def shift(self, values, axis, step):
        count, stride = self.size[axis], self.stride[axis]
        pairs = []
        for i in range(self.tp if axis in "uw" else self.ep):
            own = i // stride % count
            pairs.append((i, i + ((own + step) % count - own) * stride))
        return lax.ppermute(values, "tp" if axis in "uw" else "ep", pairs)

    def gather_axis(self, values, axis):
        dim, count, own = self.axes.index(axis), self.size[axis], self.place(axis)
        parts = [values] + [self.shift(values, axis, step) for step in range(1, count)]
        shape = list(values.shape)
        shape[dim] = count
        values = jnp.zeros(shape, values.dtype)
        for step, part in enumerate(parts):
            values = lax.dynamic_update_slice_in_dim(values, part, (own - step) % count, dim)
        return values

    def gather(self, values, order):
        values = values[(None,) * len(self.axes)]
        for axis in order:
            values = self.gather_axis(values, axis)
        return values

    def gather_rows(self, values):
        rows, columns = values.shape
        values = self.gather(values, "uw")
        halves = values[..., : rows // 2, :], values[..., rows // 2 :, :]
        halves = [
            self.gather_axis(self.gather_axis(half, first), second)
            for half, (first, second) in zip(halves, ("xy", "yx"), strict=True)
        ]
        values = self.gather_axis(jnp.concatenate(halves, axis=-2), "c")
        return values.reshape(-1, columns)

    def reduce_axis(self, values, axis, axes):
        dim, count, own = axes.index(axis), self.size[axis], self.place(axis)
        values = values if isinstance(values, (list, tuple)) else [values]
        kind = values[0].dtype

        def part(step):
            return sum(
                lax.dynamic_index_in_dim(v, (own - step) % count, dim, keepdims=False).astype(wide)
                for v in values
            )

        total = part(0)
        for step in range(1, count):
            total = total + self.shift(part(step).astype(kind), axis, -step).astype(wide)
        return total.astype(kind)

    def reduce_scatter(self, values, order, axes=axes):
        for axis in order:
            values = self.reduce_axis(values, axis, axes)
            axes = axes.replace(axis, "")
        return values

    def from_line(self, values, axis):
        return [values] + [
            self.shift(values, axis, step) for step in range(1, self.size[axis])
        ]

    def columns_from_line(self, values, axis):
        rows, count, own = values.shape[0], self.size[axis], self.place(axis)
        values = values.reshape(rows, count, -1)

        def part(step):
            return lax.dynamic_index_in_dim(values, (own + step) % count, 1, keepdims=False)

        taken = jnp.stack(
            [part(0)] + [self.shift(part(step), axis, step) for step in range(1, count)]
        )
        taken = jnp.stack([taken, self.shift(taken, "c", 1)], axis=1)
        return taken.reshape(-1, taken.shape[-1])

    def rows_from_line(self, values, axis):
        count, own = self.size[axis], self.place(axis)

        def part(step):
            return lax.dynamic_index_in_dim(values, (own + step) % count, 0)

        whole = jnp.zeros(values.shape, values.dtype)
        for step in range(count):
            got = part(0) if step == 0 else self.shift(part(step), axis, step)
            whole = lax.dynamic_update_slice_in_dim(whole, got, (own - step) % count, 0)
        return whole.transpose(1, 0, 2).reshape(values.shape[1], -1)

    def reduce_first(self, pair):
        return [self.reduce_axis(v, axis, "yxuw") for v, axis in zip(pair, "yx", strict=True)]

    def reduce_both(self, pair, axis):
        left = "uw" if axis == "w" else "u"
        return [self.reduce_axis(v, axis, line + left) for v, line in zip(pair, "xy", strict=True)]

    def rows_of_both(self, pair):
        return [self.rows_from_line(v, line) for v, line in zip(pair, "xy", strict=True)]

    def reduce_second(self, pair, join):
        pair = [
            self.reduce_axis(v, axis, axis + "uw") for v, axis in zip(pair, "xy", strict=True)
        ]
        return jnp.concatenate(pair, axis=join + 2)

    def chips(self):
        return tuple(self.size[axis] for axis in "yxuw")


nt_dims = (((1,), (1,)), ((), ()))
tn_dims = (((0,), (0,)), ((), ()))


def one_hot(slots):
    experts, tokens = slots.shape
    place = lax.broadcasted_iota(jnp.int32, (experts, CAP, tokens), 1).astype(wide) + 1.0
    return (slots[:, None, :] == place).astype(wide).reshape(experts * CAP, tokens)


def dot(left, right, dims=(((1,), (0,)), ((), ()))):
    return lax.dot_general(left, right, dims, preferred_element_type=wide)


def gate_column(pick, gates):
    spread = jnp.broadcast_to(gates[:, None, :], (gates.shape[0], CAP, gates.shape[1]))
    return jnp.sum(pick * spread.reshape(pick.shape), axis=1, keepdims=True)


class Streams:
    def __init__(self, sources, targets, sems, rows_v, rows_hbm, row_sem, base):
        self.step, chunk = pl.program_id(0), rows_v.shape[0]
        experts = sources[0].shape[0]
        self.groups = [range(experts // 2), range(experts // 2, experts)]
        self.weights = [
            [
                pltpu.make_async_copy(source.at[e], target(e), sems.at[i, e])
                for i, (source, target) in enumerate(zip(sources, targets, strict=True))
                for e in group
            ]
            for group in self.groups
        ]
        block = base + self.step * chunk
        self.rows = [
            pltpu.make_async_copy(
                rows_v.at[:, e * CAP : (e + 1) * CAP, :],
                rows_hbm.at[e, pl.ds(block, chunk)],
                row_sem.at[e],
            )
            for e in range(experts)
        ]

        @pl.when(self.step == 0)
        def _():
            for copies in self.weights:
                for copy in copies:
                    copy.start()

        @pl.when(self.step > 0)
        def _():
            self.wait_rows()

    def wait_rows(self):
        for copy in self.rows:
            copy.wait()

    def send_rows(self):
        for copy in self.rows:
            copy.start()

    def wait_weights(self, group):
        @pl.when(self.step == 0)
        def _():
            for copy in self.weights[group]:
                copy.wait()

    def end(self):
        @pl.when(self.step == pl.num_programs(0) - 1)
        def _():
            self.wait_rows()


def write_parts(targets, block, total):
    share = total.shape[0] // len(targets)
    for i, target in enumerate(targets):
        target[block] = total[i * share : (i + 1) * share]


def forward_kernel(base, kept, parts, _, slots_ref, router_ref, x_ref, *refs):
    weights, refs = refs[:3], refs[3:]
    refs = refs[kept:]
    y_refs, refs = refs[:parts], refs[parts:]
    gates_ref, pre_ref, inner_ref, rows_hbm = refs[:4]
    joint_w, down_w, rows_v, out_v, gate_rows, w_sems, row_sems = refs[4:]
    chunk, _, width = x_ref.shape
    experts, hidden, _ = down_w.shape
    depth = chunk * CAP
    targets = (
        lambda e: joint_w.at[e, :, :hidden],
        lambda e: joint_w.at[e, :, hidden:],
        lambda e: down_w.at[e],
    )
    streams = Streams(weights, targets, w_sems, rows_v, rows_hbm, row_sems, base)
    picks = []
    for b in range(chunk):
        tokens = x_ref[b]
        logits = dot(tokens, router_ref[...]).T
        exponent = jnp.exp(logits - jnp.max(logits, axis=0, keepdims=True))
        gates = (exponent / jnp.sum(exponent, axis=0, keepdims=True))[:experts]
        gates_ref[b] = gates
        pick = one_hot(slots_ref[b])
        gate_rows[b] = gate_column(pick, gates)
        picks.append(pick.astype(low))
        rows_v[b] = dot(picks[b], tokens).astype(low)
    streams.send_rows()
    for e in range(experts):
        at = slice(e * CAP, (e + 1) * CAP)
        for i, group in enumerate(streams.groups):
            if e == group.start:
                streams.wait_weights(i)
        pre = dot(rows_v[:, at, :].reshape(depth, width), joint_w[e])
        pre_ref[e] = pre
        gate_pre, up_pre = pre[:, :hidden], pre[:, hidden:]
        inner = (gate_pre * jax.nn.sigmoid(gate_pre) * up_pre).astype(low).astype(wide)
        scaled = (inner * gate_rows[:, at, :].reshape(depth, 1)).astype(low)
        inner_ref[e] = scaled
        out = dot(scaled, down_w[e]).astype(low)
        out_v[:, at, :] = out.reshape(chunk, CAP, width)
    for b in range(chunk):
        write_parts(y_refs, b, dot(picks[b], out_v[b], tn_dims).astype(low))
    streams.end()


def backward_kernel(base, kept, parts, _, slots_ref, gates_ref, g_ref, pre_ref, *refs):
    weights, refs = refs[:3], refs[3:]
    refs = refs[kept:]
    x_refs, refs = refs[:parts], refs[parts:]
    grads_ref, dgate_ref, dup_ref, rows_hbm = refs[:4]
    joint_w, down_w, rows_v, out_v, gate_rows, grad_rows, w_sems, row_sems = refs[4:]
    chunk, tokens, width = g_ref.shape
    experts, _, hidden = down_w.shape
    depth = chunk * CAP
    targets = (
        lambda e: joint_w.at[e, :hidden],
        lambda e: joint_w.at[e, hidden:],
        lambda e: down_w.at[e],
    )
    streams = Streams(weights, targets, w_sems, rows_v, rows_hbm, row_sems, base)
    picks = []
    for b in range(chunk):
        pick = one_hot(slots_ref[b])
        gate_rows[b] = gate_column(pick, gates_ref[b])
        picks.append(pick.astype(low))
        rows_v[b] = dot(picks[b], g_ref[b]).astype(low)
    streams.send_rows()
    for e in range(experts):
        at = slice(e * CAP, (e + 1) * CAP)
        for i, group in enumerate(streams.groups):
            if e == group.start:
                streams.wait_weights(i)
        pulled = dot(rows_v[:, at, :].reshape(depth, width), down_w[e])
        gate_pre, up_pre = pre_ref[e, :, :hidden], pre_ref[e, :, hidden:]
        sigmoid = jax.nn.sigmoid(gate_pre)
        silu = gate_pre * sigmoid
        inner = (silu * up_pre).astype(low).astype(wide)
        grad_rows[:, at, :] = jnp.sum(inner * pulled, axis=1, keepdims=True).reshape(
            chunk, CAP, 1
        )
        grad_inner = pulled * gate_rows[:, at, :].reshape(depth, 1)
        dgate = (grad_inner * up_pre * sigmoid * (1.0 + gate_pre * (1.0 - sigmoid))).astype(low)
        dup = (grad_inner * silu).astype(low)
        dgate_ref[e] = dgate
        dup_ref[e] = dup
        out = dot(jnp.concatenate([dgate, dup], axis=1), joint_w[e]).astype(low)
        out_v[:, at, :] = out.reshape(chunk, CAP, width)
    for b in range(chunk):
        write_parts(x_refs, b, dot(picks[b], out_v[b], tn_dims).astype(low))
        per_row = picks[b].astype(wide) * grad_rows[b]
        grads_ref[b] = jnp.sum(per_row.reshape(experts, CAP, tokens), axis=1)
    streams.end()


class Experts:
    def __init__(self, blocks, chunk, tokens, width, experts, hidden):
        self.chunk, self.half = chunk, blocks // 2
        self.tokens, self.width, self.experts, self.hidden = tokens, width, experts, hidden
        self.rows = blocks * CAP

    def mine(self, first, *shape):
        return pl.BlockSpec(
            (self.chunk,) + shape,
            lambda i, core: (2 * (i + first) + core[0],) + (0,) * len(shape),
        )

    def listed(self, first, *shape):
        return pl.BlockSpec(
            (self.chunk,) + shape, lambda i, core: (i + first,) + (0,) * len(shape)
        )

    def by_row(self, last, first):
        return pl.BlockSpec(
            (self.experts, self.chunk * CAP, last), lambda i, core: (0, i + first, 0)
        )

    def call(self, kernel, name, first, count, turn, parts, core, ins, in_specs, outs, given):
        any_spec = pl.BlockSpec(memory_space=pl.ANY)
        base = turn * self.half + first * self.chunk
        joint = [self.experts, self.width, self.width]
        joint[2 if kernel is forward_kernel else 1] = 2 * self.hidden
        given = [None] * (len(outs) - len(given)) + given
        goes_on = [i for i, array in enumerate(given) if array is not None]
        rows = self.experts * count * self.chunk * CAP
        results = pl.pallas_call(
            functools.partial(kernel, base, len(goes_on), parts),
            grid_spec=pltpu.PrefetchScalarGridSpec(
                num_scalar_prefetch=1,
                grid=(count,),
                in_specs=in_specs + [any_spec] * (3 + len(goes_on)),
                out_specs=[spec or any_spec for _, _, spec in outs],
                scratch_shapes=[pltpu.VMEM(tuple(joint), low), pltpu.VMEM(ins[-1].shape, low)]
                + [pltpu.VMEM((self.chunk, self.experts * CAP, self.width), low)] * 2
                + [pltpu.VMEM((self.chunk, self.experts * CAP, 1), wide)] * (1 if kernel is forward_kernel else 2)
                + [
                    pltpu.SemaphoreType.DMA((3, self.experts)),
                    pltpu.SemaphoreType.DMA((self.experts,)),
                ],
            ),
            out_shape=[jax.ShapeDtypeStruct(shape, kind) for shape, kind, _ in outs],
            input_output_aliases={1 + len(ins) + n: i for n, i in enumerate(goes_on)},
            compiler_params=pltpu.CompilerParams(
                dimension_semantics=("arbitrary",), vmem_limit_bytes=60 * 1024 * 1024
            ),
            cost_estimate=pl.CostEstimate(
                flops=10 * rows * self.width * (3 * self.hidden + 256),
                bytes_accessed=rows * self.width * 8,
                transcendentals=0,
            ),
            name=name,
        )(core, *ins, *(given[i] for i in goes_on))
        return list(results)

    def token_outs(self, first, parts):
        share = self.tokens // parts
        part = ((self.half, share, self.width), low, self.listed(first, share, self.width))
        by_token = (
            (self.half, self.experts, self.tokens),
            wide,
            self.listed(first, self.experts, self.tokens),
        )
        return [part] * parts + [by_token]

    def row_out(self, first, turn):
        first += turn * self.half // self.chunk
        return (
            (self.experts, self.rows, self.hidden),
            low,
            self.by_row(self.hidden, first),
        )

    def taken(self):
        return ((self.experts, self.rows // CAP, CAP, self.width), low, None)

    def forward(self, first, count, turn, parts, core, slots, router, tokens, weights, given):
        pre = (
            (self.experts, self.half * CAP, 2 * self.hidden),
            wide,
            self.by_row(2 * self.hidden, first),
        )
        return self.call(
            forward_kernel,
            "experts_forward",
            first,
            count,
            turn,
            parts,
            core,
            (slots, router, tokens, *weights),
            [
                self.mine(first, self.experts, self.tokens),
                pl.BlockSpec(router.shape, lambda i, core: (0, 0)),
                self.mine(first, self.tokens, self.width),
            ],
            self.token_outs(first, parts) + [pre, self.row_out(first, turn), self.taken()],
            given,
        )

    def backward(
        self, first, count, turn, parts, core, slots, gates, grads, pre, weights, given
    ):
        return self.call(
            backward_kernel,
            "experts_backward",
            first,
            count,
            turn,
            parts,
            core,
            (slots, gates, grads, pre, *weights),
            [
                self.mine(first, self.experts, self.tokens),
                self.listed(first, self.experts, self.tokens),
                self.mine(first, self.tokens, self.width),
                self.by_row(2 * self.hidden, first),
            ],
            self.token_outs(first, parts)
            + [self.row_out(first, turn), self.row_out(first, turn), self.taken()],
            given,
        )


def on_device(
    hidden_in,
    w_query,
    w_key,
    w_value,
    w_output,
    w_router,
    gain_attn,
    gain_ffn,
    gain_query,
    gain_key,
    w_gate,
    w_up,
    w_down,
    expert_ids,
    grad_out,
):
    tokens_dev, model_width = hidden_in.shape
    local_experts, _, hidden_units = w_gate.shape
    expert_count = w_router.shape[1]
    grid = Grid()
    blocks = grid.ep * grid.tp
    weight_rows = model_width // blocks
    both = ("ep", "tp")
    inv_root = 1.0 / math.sqrt(HEAD_DIM)

    def gathered(values):
        return lax.all_gather(values, both, axis=0, tiled=True)

    named = jnp.any(
        expert_ids[None, :, :] == jnp.arange(expert_count, dtype=jnp.int32)[:, None, None], axis=2
    )
    before = (jnp.arange(tokens_dev)[:, None] <= jnp.arange(tokens_dev)[None, :]).astype(low)
    counted = jnp.dot(named.astype(low), before, preferred_element_type=wide)
    slots = jnp.where(named, counted, 0.0).astype(low)

    shared = jnp.concatenate(
        [
            w_router,
            jnp.stack([gain_attn, gain_ffn, gain_query, gain_key], axis=1),
            jnp.zeros((w_router.shape[0], tokens_dev - expert_count - 4), low),
        ],
        axis=1,
    )
    small_all = grid.gather(jnp.concatenate([shared, slots], axis=0), "xyuwc")
    projections = gathered(jnp.concatenate([w_query, w_key, w_value], axis=1))
    projections, output_full, small_all = together(
        projections, grid.gather_rows(w_output), small_all
    )
    upstream_all = gathered(after(grad_out, projections)[None])
    small_all = small_all.reshape(blocks, weight_rows + expert_count, tokens_dev)
    shared_full = small_all[:, :weight_rows].reshape(model_width, tokens_dev)
    slots_all = small_all[:, weight_rows:]
    router_full = shared_full[:, :expert_count]
    gains = shared_full[:, expert_count : expert_count + 4].astype(wide).T
    attn_gain, ffn_gain, query_gain, key_gain = gains[0], gains[1], gains[2], gains[3]

    inputs_full = hidden_in.astype(wide)
    scale_attn = lax.rsqrt(jnp.mean(inputs_full * inputs_full, axis=-1, keepdims=True) + epsilon)
    unit_attn = inputs_full * scale_attn
    normed_attn = (unit_attn * attn_gain).astype(low)
    projected = jnp.dot(normed_attn, projections, preferred_element_type=wide)
    query_raw = projected[:, :model_width]
    key_raw = projected[:, model_width : 2 * model_width]
    value_raw = projected[:, 2 * model_width :]
    scale_query = lax.rsqrt(jnp.mean(query_raw * query_raw, axis=-1, keepdims=True) + epsilon)
    unit_query = query_raw * scale_query
    scale_key = lax.rsqrt(jnp.mean(key_raw * key_raw, axis=-1, keepdims=True) + epsilon)
    unit_key = key_raw * scale_key
    cosines, sines = rope_tables(tokens_dev, HEAD_DIM)
    query_rot = rotate(
        (unit_query * query_gain).reshape(tokens_dev, HEADS, HEAD_DIM), cosines, sines
    ).astype(low)
    key_rot = rotate(
        (unit_key * key_gain).reshape(tokens_dev, HEADS, HEAD_DIM), cosines, sines
    ).astype(low)
    value_heads = value_raw.astype(low).reshape(tokens_dev, HEADS, HEAD_DIM)
    causal = jnp.arange(tokens_dev)[:, None] >= jnp.arange(tokens_dev)[None, :]
    scores = (
        jnp.einsum("qhd,khd->hqk", query_rot, key_rot, preferred_element_type=wide) * inv_root
    )
    scores = jnp.where(causal[None], scores, masked_value)
    exponent = jnp.exp(scores - jnp.max(scores, axis=-1, keepdims=True))
    att_probs = exponent / jnp.sum(exponent, axis=-1, keepdims=True)
    probs_low = att_probs.astype(low)
    attended = (
        jnp.einsum("hqk,khd->qhd", probs_low, value_heads, preferred_element_type=wide)
        .reshape(tokens_dev, model_width)
        .astype(low)
    )
    mixed = inputs_full + jnp.dot(attended, output_full, preferred_element_type=wide)
    scale_ffn = lax.rsqrt(jnp.mean(mixed * mixed, axis=-1, keepdims=True) + epsilon)
    unit_ffn = mixed * scale_ffn
    normed_ffn = (unit_ffn * ffn_gain).astype(low)
    normed_all = gathered(normed_ffn[None])
    router_probs = jax.nn.softmax(
        jnp.dot(normed_ffn, router_full, preferred_element_type=wide), axis=-1
    )

    turned = [weights.transpose(0, 2, 1) for weights in (w_gate, w_up, w_down)]
    normed_all, turned = together(normed_all, turned)

    first_expert = lax.axis_index("ep") * local_experts
    slots_here = lax.dynamic_slice_in_dim(slots_all, first_expert, local_experts, 1).astype(wide)
    router_turned = lax.dynamic_slice_in_dim(
        jnp.concatenate([router_full, router_full], axis=1), first_expert, expert_count, 1
    )
    experts = Experts(
        blocks, grid.tp, tokens_dev, model_width, local_experts, hidden_units
    )
    core = grid.place("c")
    turns = (jnp.reshape(1 - core, (1,)), jnp.reshape(core, (1,)))
    chips = grid.chips()

    def token_sums(away, kept):
        share = tokens_dev // len(kept)
        away = away.reshape(chips + away.shape[1:])
        return [
            (part.reshape(chips + part.shape[1:]), away[..., i * share : (i + 1) * share, :])
            for i, part in enumerate(kept)
        ]

    groups = blocks // 2 // grid.tp
    part = groups // 2
    forward_ins = (slots_here, router_turned, normed_all, (w_gate, w_up, w_down))
    y_ahead, gates_ahead, pre_ahead, *given = experts.forward(
        0, groups, 0, 1, turns[0], *forward_ins, []
    )
    *y_own, gates_own, pre_own, inner_scaled, rows_in = experts.forward(
        0, groups, 1, 2, turns[1], *forward_ins, given
    )
    y_away = grid.shift(y_ahead, "c", 1)
    y_own, y_away, gates_own, slots_here = together(y_own, y_away, gates_own, slots_here)
    expert_sums = token_sums(y_away, y_own)

    def backward(first, count, turn, parts, gates, pre, given):
        return experts.backward(
            first,
            count,
            turn,
            parts,
            turns[turn],
            slots_here,
            gates,
            upstream_all,
            pre,
            turned,
            given,
        )

    def by_core(values):
        values = values.reshape(tokens_dev, chips[0] * chips[1], 2, -1)
        return [
            lax.dynamic_index_in_dim(values, at, 2, keepdims=False).reshape(tokens_dev, -1)
            for at in (1 - core, core)
        ]

    away, kept = (
        jnp.concatenate(cut, axis=1)
        for cut in zip(by_core(normed_attn), by_core(attended), strict=True)
    )
    ahead = backward(0, groups, 0, 1, gates_ahead, pre_ahead, [])
    expert_sums = grid.reduce_first(expert_sums)
    (x_ahead, gate_grads_ahead, *given), expert_sums, slots_here = together(
        ahead, expert_sums, slots_here
    )
    x_away = grid.shift(x_ahead, "c", 1)
    given = backward(0, part, 1, 4, gates_own, pre_own, given)
    expert_sum = grid.reduce_second(expert_sums, 0)
    pair_rows = jnp.concatenate([kept, grid.shift(away, "c", 1)], axis=0)
    given, expert_sum, x_away, slots_here, pair_rows = together(
        given, expert_sum, x_away, slots_here, pair_rows
    )
    own = backward(part, groups - part, 1, 4, gates_own, pre_own, given)
    expert_sum = grid.reduce_axis(expert_sum, "w", "uw")
    half = model_width // 2
    x_rows = jnp.concatenate(grid.from_line(pair_rows, "x"), axis=0)
    y_rows = jnp.concatenate(grid.from_line(pair_rows[:, :half], "y"), axis=0)
    own, expert_sum, x_rows, y_rows = together(own, expert_sum, x_rows, y_rows)
    *x_own, gate_grads_own, grad_gate_part, grad_up_part, rows_up = own
    rows_in = rows_in.reshape(local_experts, -1, model_width)
    rows_up = rows_up.reshape(local_experts, -1, model_width)

    def weight_grad(subscripts, left, right):
        return jnp.einsum(subscripts, left, right, preferred_element_type=wide)

    x_own, x_away, rows_in, rows_up, inner_scaled, expert_sum = together(
        x_own, x_away, rows_in, rows_up, inner_scaled, expert_sum
    )
    sums = token_sums(x_away, x_own)
    acc_gate = weight_grad("erd,erh->edh", rows_in, grad_gate_part)
    early = grid.reduce_first(sums[:2])
    expert_sum = grid.reduce_axis(expert_sum, "u", "u")
    gate_grads = jnp.stack([gate_grads_own, gate_grads_ahead])
    early, late, acc_gate, expert_sum, rows_in, rows_up, gate_grads = together(
        early, sums[2:], acc_gate, expert_sum, rows_in, rows_up, gate_grads
    )
    acc_down = weight_grad("erh,erd->ehd", inner_scaled, rows_up)
    early = grid.reduce_second(early, 0)
    late = grid.reduce_first(late)
    early, late, acc_down, rows_in = together(early, late, acc_down, rows_in)
    acc_up = weight_grad("erd,erh->edh", rows_in, grad_up_part)
    early = grid.reduce_axis(early, "w", "uw")
    late = grid.reduce_second(late, 0)
    early, late, acc_up = together(early, late, acc_up)
    early = grid.reduce_axis(early, "u", "u")
    late = grid.reduce_axis(late, "w", "uw")
    early, late = together(early, late)
    late = grid.reduce_axis(late, "u", "u")
    block_out = (mixed + expert_sum.astype(wide)).astype(low)

    gate_grads = jnp.where(core == 0, gate_grads, gate_grads[::-1])
    gate_grads = gate_grads.reshape((2,) + chips + (local_experts, tokens_dev))
    gate_grads = grid.reduce_scatter(gate_grads, "wu", "cyxuw")
    gate_grads = lax.dynamic_update_slice_in_dim(
        jnp.zeros(gate_grads.shape[:3] + (expert_count, tokens_dev), wide),
        gate_grads,
        first_expert,
        3,
    )
    grad_probs = grid.reduce_scatter(gate_grads, "cyx", "cyx").T
    back_sum, block_out, acc_gate, acc_up, acc_down = together(
        jnp.concatenate([early, late], axis=0), block_out, acc_gate, acc_up, acc_down
    )

    upstream = grad_out.astype(wide)
    grad_logits = router_probs * (
        grad_probs - jnp.sum(router_probs * grad_probs, axis=-1, keepdims=True)
    )
    grad_ffn_normed = back_sum.astype(wide) + jnp.dot(
        grad_logits, router_full.astype(wide).T, precision=lax.Precision.HIGHEST
    )
    grad_router_local = jnp.dot(
        normed_ffn.astype(wide).T, grad_logits, precision=lax.Precision.HIGHEST
    )
    grad_ffn_gain = jnp.sum(grad_ffn_normed * unit_ffn, axis=0)
    grad_mixed = upstream + rms_back(grad_ffn_normed, unit_ffn, ffn_gain, scale_ffn)
    grad_branch = grad_mixed.astype(low)

    output_columns = grid.columns_from_line(grad_branch, "x")
    grad_attended = jnp.einsum(
        "te,de->td", grad_branch, output_full, preferred_element_type=wide
    ).astype(low)
    grad_heads = grad_attended.reshape(tokens_dev, HEADS, HEAD_DIM)
    grad_value_rows = (
        jnp.einsum("hqk,qhd->khd", probs_low, grad_heads, preferred_element_type=wide)
        .reshape(tokens_dev, model_width)
        .astype(low)
    )
    value_columns = grid.columns_from_line(grad_value_rows, "y")
    grad_probs_att = jnp.einsum(
        "qhd,khd->hqk", grad_heads, value_heads, preferred_element_type=wide
    )
    grad_scores = (
        att_probs * (grad_probs_att - jnp.sum(att_probs * grad_probs_att, axis=-1, keepdims=True))
    ).astype(low)
    grad_qrot = (
        jnp.einsum("hqk,khd->qhd", grad_scores, key_rot, preferred_element_type=wide) * inv_root
    )
    grad_krot = (
        jnp.einsum("hqk,qhd->khd", grad_scores, query_rot, preferred_element_type=wide) * inv_root
    )
    grad_qnorm = unrotate(bounce(grad_qrot), cosines, sines).reshape(tokens_dev, model_width)
    grad_knorm = unrotate(bounce(grad_krot), cosines, sines).reshape(tokens_dev, model_width)
    grad_query_gain = jnp.sum(grad_qnorm * unit_query, axis=0)
    grad_key_gain = jnp.sum(grad_knorm * unit_key, axis=0)
    grad_query_raw = rms_back(grad_qnorm, unit_query, query_gain, scale_query).astype(low)
    grad_key_raw = rms_back(grad_knorm, unit_key, key_gain, scale_key).astype(low)
    output_columns, value_columns, grad_query_raw, grad_key_raw = together(
        output_columns, value_columns, grad_query_raw, grad_key_raw
    )

    def outer(left, right):
        total = jnp.einsum("tc,te->ce", left, right, preferred_element_type=wide)
        return total.astype(low).reshape(chips + (weight_rows, -1))

    first = [outer(x_rows[:, half:], output_columns), outer(y_rows, value_columns)]
    second = [
        grid.columns_from_line(grad_query_raw, "x"),
        grid.columns_from_line(grad_key_raw, "y"),
    ]
    first, second = together(first, second)
    first = grid.reduce_first(first)
    second = [outer(x_rows[:, :half], second[0]), outer(y_rows, second[1])]
    grads = jnp.concatenate([grad_query_raw, grad_key_raw, grad_value_rows], axis=1)
    grad_attn_normed = jnp.einsum("te,ce->tc", grads, projections, preferred_element_type=wide)
    grad_attn_gain = jnp.sum(grad_attn_normed * unit_attn, axis=0)
    grad_input = grad_mixed + rms_back(grad_attn_normed, unit_attn, attn_gain, scale_attn)
    gain_sums = jnp.stack(
        [grad_attn_gain, grad_ffn_gain, grad_query_gain, grad_key_gain], axis=1
    )
    small_sums = jnp.concatenate([grad_router_local, gain_sums], axis=1).reshape(
        grid.shape + (weight_rows, expert_count + gain_sums.shape[1])
    )
    first, second, small_sums, grad_input = together(first, second, small_sums, grad_input)
    first = grid.reduce_both(first, "w")
    second = grid.reduce_first(second)
    small_sums = grid.reduce_scatter(small_sums, "c")
    first, second, small_sums = together(first, second, small_sums)
    first = grid.reduce_both(first, "u")
    second = grid.reduce_both(second, "w")
    small_sums = grid.reduce_scatter(small_sums, "y", "yxuw")
    first, second, small_sums = together(first, second, small_sums)
    grad_output, grad_value = grid.rows_of_both(first)
    second = grid.reduce_both(second, "u")
    small_sums = grid.reduce_scatter(small_sums, "x", "xuw")
    grad_output, grad_value, second, small_sums = together(
        grad_output, grad_value, second, small_sums
    )
    grad_query, grad_key = grid.rows_of_both(second)
    small_sums = grid.reduce_scatter(small_sums, "wu", "uw")
    grad_query, grad_key, grad_value, grad_output = (
        grad.astype(wide) for grad in (grad_query, grad_key, grad_value, grad_output)
    )
    return (
        block_out,
        grad_input,
        grad_query,
        grad_key,
        grad_value,
        grad_output,
        small_sums[:, :expert_count],
        *(small_sums[:, expert_count + i] for i in range(4)),
        acc_gate,
        acc_up,
        acc_down,
    )


def solution(mesh):
    placed = (
        P(("ep", "tp"), None),
        P(("ep", "tp"), None),
        P(("ep", "tp"), None),
        P(("ep", "tp"), None),
        P(("ep", "tp"), None),
        P(("ep", "tp"), None),
        P(("ep", "tp")),
        P(("ep", "tp")),
        P(("ep", "tp")),
        P(("ep", "tp")),
        P("ep", None, "tp"),
        P("ep", None, "tp"),
        P("ep", "tp", None),
        P(("ep", "tp"), None),
        P(("ep", "tp"), None),
    )
    return jax.shard_map(
        on_device,
        mesh=mesh,
        in_specs=placed,
        out_specs=(
            P(("ep", "tp"), None),
            P(("ep", "tp"), None),
            P(("ep", "tp"), None),
            P(("ep", "tp"), None),
            P(("ep", "tp"), None),
            P(("ep", "tp"), None),
            P(("ep", "tp"), None),
            P(("ep", "tp")),
            P(("ep", "tp")),
            P(("ep", "tp")),
            P(("ep", "tp")),
            P("ep", None, "tp"),
            P("ep", None, "tp"),
            P("ep", "tp", None),
        ),
        check_vma=False,
    )
```

time: 1350 us -> 993 us (0.74)
  waiting for transfers between devices: 555 us -> 379 us
  starting transfers between devices: 244 us -> 69 us
  Pallas kernels: 203 us -> 166 us
  local copies, waits for them, and re-layouts: 114 us -> 151 us
  matrix products: 135 us -> 114 us
    ppermute x144 -> x69, starting transfers between devices: 243 us -> 68.9 us  [shift(): return lax.ppermute(values, 'tp' if axis in 'uw' else 'ep', pairs)]
    ppermute x144 -> x69, waiting for transfers between devices: 404 us -> 264 us  [shift(): return lax.ppermute(values, 'tp' if axis in 'uw' else 'ep', pairs)]
    unnamed x182 -> x243, local copies, waits for them, and re-layouts: 13 us -> 58.7 us
    pallas_call x2 -> x5, Pallas kernels: 203 us -> 166 us  [call(): pl.pallas_call(functools.partial(kernel, base, len(goes_on), parts), grid...]
    all_gather x4 -> x3, waiting for transfers between devices: 150 us -> 115 us  [gathered(): return lax.all_gather(values, both, axis=0, tiled=True)]
    dot_general x13 -> x9, matrix products: 113 us -> 93.9 us  [the longest x3 62.3 us: weight_grad(): return jnp.einsum(subscripts, left, right, preferred_element_type=wide)]
    dynamic_slice x20 -> x25, local copies, waits for them, and re-layouts: 42.9 us -> 28.7 us  [the longest x9 14.2 us: part(): lax.dynamic_index_in_dim(v, (own - step) % count, dim, keepdims=False)]
    convert_element_type x47 -> x43, other arithmetic: 52.3 us -> 48 us  [the longest x30 34.9 us: reduce_axis(): return total.astype(kind)]
  transfers between devices with their start and end apart: 148 -> 72, of which waited for: 57 -> 36; matrix products, arithmetic and copies ran while one was open for 18% -> 27% of each run, Pallas kernels for 6% -> 17%
where the time goes in v2:
time: 993 us; the launch traced here: 983 us
  waiting for transfers between devices  379 us (38%)
  Pallas kernels  166 us (17%)
  local copies, waits for them, and re-layouts  151 us (15%)
  matrix products  114 us (11%)
  other arithmetic  87.3 us (9%)
  starting transfers between devices  69 us (7%)
  between operations  16.5 us (2%)
    ppermute x69, waiting for transfers between devices, shift(): return lax.ppermute(values, 'tp' if axis in 'uw' else 'ep', pairs)  264 us
    pallas_call x5, Pallas kernels, call(): pl.pallas_call(functools.partial(kernel, base, len(goes_on), parts), grid...  166 us
    all_gather x3, waiting for transfers between devices, gathered(): return lax.all_gather(values, both, axis=0, tiled=True)  115 us
    ppermute x69, starting transfers between devices, shift(): return lax.ppermute(values, 'tp' if axis in 'uw' else 'ep', pairs)  68.9 us
    dot_general x3, matrix products, weight_grad(): return jnp.einsum(subscripts, left, right, preferred_element_type=wide)  62.3 us
    unnamed x243, local copies, waits for them, and re-layouts  58.7 us
    convert_element_type x30, other arithmetic, reduce_axis(): return total.astype(kind)  34.9 us
  transfers between devices with their start and end apart: 72, of which 36 were waited for; matrix products, arithmetic and copies ran while one was open for 27% of the time, Pallas kernels for 17%

profile of v2, /device:TPU:0, one launch (start us, length us, event | category | flops | bytes accessed | tf_op | source)
XLA Modules:
  0.0 983.1 jit_solution(1882516337524924476)
XLA Ops:
  13.6 11.8 %collective-permute-done = bf16[1,1,1,1,1,64,2048]{6,5,4,3,2,1,0:T(8,128)(2,1)S(1)} collective-permute-done((bf16[1,1,1,1,1,64,2048]{6,5,4,3,2,1,0:T(8,128)(2,1)S(1)}, bf16[1,1,1,1,1,64,2048]{6,5,4,3,2,1,0:T(8,128)(2,1)S(1)}, u32[]{:S(2)}, u32[]{:S(2)}) %collective-permute-start) | collective-permute-done | bytes 262176 | tf_op jit(solution)/shard_map/ppermute | solution.py:92
  28.1 26.1 %collective-permute-done.1 = bf16[1,1,1,2,1,64,2048]{6,5,4,3,2,1,0:T(8,128)(2,1)S(1)} collective-permute-done((bf16[1,1,1,2,1,64,2048]{6,5,4,3,2,1,0:T(8,128)(2,1)S(1)}, bf16[1,1,1,2,1,64,2048]{6,5,4,3,2,1,0:T(8,128)(2,1)S(1)}, u32[]{:S(2)}, u32[]{:S(2)}) %collective-permute-start.1) | collective-permute-done | bytes 524320 | tf_op jit(solution)/shard_map/ppermute | solution.py:92
  58.5 18.9 %collective-permute-done.4 = bf16[1,1,1,2,2,32,2048]{6,5,4,3,2,1,0:T(8,128)(2,1)S(1)} collective-permute-done((bf16[1,1,1,2,2,32,2048]{6,5,4,3,2,1,0:T(8,128)(2,1)S(1)}, bf16[1,1,1,2,2,32,2048]{6,5,4,3,2,1,0:T(8,128)(2,1)S(1)}, u32[]{:S(2)}, u32[]{:S(2)}) %collective-permute-start.4) | collective-permute-done | bytes 524320 | tf_op jit(solution)/shard_map/ppermute | solution.py:92
  84.2 31.3 %collective-permute-done.5 = bf16[2,1,1,2,2,32,2048]{6,5,4,3,2,1,0:T(8,128)(2,1)S(1)} collective-permute-done((bf16[2,1,1,2,2,32,2048]{6,5,4,3,2,1,0:T(8,128)(2,1)S(1)}, bf16[2,1,1,2,2,32,2048]{6,5,4,3,2,1,0:T(8,128)(2,1)S(1)}, u32[]{:S(2)}, u32[]{:S(2)}) %collective-permute-start.5) | collective-permute-done | bytes 1048608 | tf_op jit(solution)/shard_map/ppermute | solution.py:92
  131.3 5.5 collective-permute-done.8
  138.0 16.4 %collective-permute-done.9 = bf16[2,2,1,1,1,128,128]{6,5,4,3,2,1,0:T(8,128)(2,1)S(1)} collective-permute-done((bf16[2,2,1,1,1,128,128]{6,5,4,3,2,1,0:T(8,128)(2,1)S(1)}, bf16[2,2,1,1,1,128,128]{6,5,4,3,2,1,0:T(8,128)(2,1)S(1)}, u32[]{:S(2)}, u32[]{:S(2)}) %collective-permute-start.9) | collective-permute-done | bytes 131104 | tf_op jit(solution)/shard_map/ppermute | solution.py:92
  154.8 29.2 %collective-permute-done.10 = bf16[2,2,1,2,1,128,128]{6,5,4,3,2,1,0:T(8,128)(2,1)S(1)} collective-permute-done((bf16[2,2,1,2,1,128,128]{6,5,4,3,2,1,0:T(8,128)(2,1)S(1)}, bf16[2,2,1,2,1,128,128]{6,5,4,3,2,1,0:T(8,128)(2,1)S(1)}, u32[]{:S(2)}, u32[]{:S(2)}) %collective-permute-start.10) | collective-permute-done | bytes 262176 | tf_op jit(solution)/shard_map/ppermute | solution.py:92
  191.0 15.7 %all-gather.6.cloned.1.call-done = bf16[2048,6144]{1,0:T(8,128)(2,1)} async-done(((bf16[64,6144]{1,0:T(8,128)(2,1)}), bf16[2048,6144]{1,0:T(8,128)(2,1)}) %all-gather.6.cloned.1.call-update) | async-done | bytes 25165840 | tf_op jit(solution)/shard_map/all_gather | solution.py:520
  211.4 10.5 %fusion.123 = f32[128,6144]{1,0:T(8,128)S(1)} fusion(bf16[128,2048]{1,0:T(8,128)(2,1)S(1)} %fusion.35, bf16[2048,6144]{1,0:T(8,128)(2,1)} %all-gather.6.cloned.1.call-done), kind=kOutput, calls=%fused_computation.371 | convolution fusion | flops 3221225472 | bytes 28835840 | tf_op jit(solution)/shard_map/dot_general | solution.py:554
  239.5 12.1 %copy.181 = bf16[8,2048,256]{1,2,0:T(8,128)(2,1)} copy(bf16[8,2048,256]{2,1,0:T(8,128)(2,1)} %refs_0_.3) | data formatting | bytes 16777216 | tf_op args[10]
  251.6 11.5 %copy.182 = bf16[8,2048,256]{1,2,0:T(8,128)(2,1)} copy(bf16[8,2048,256]{2,1,0:T(8,128)(2,1)} %refs_1_.3) | data formatting | bytes 16777216 | tf_op args[11]
  263.1 11.5 %copy.183 = bf16[8,256,2048]{1,2,0:T(8,128)(2,1)} copy(bf16[8,256,2048]{2,1,0:T(8,128)(2,1)} %refs_2_.3) | data formatting | bytes 16777216 | tf_op args[12]
  277.5 76.6 %all-gather.8.cloned.1.call-done = bf16[4096,2048]{1,0:T(8,128)(2,1)} async-done(((bf16[128,2048]{1,0:T(8,128)(2,1)}), bf16[4096,2048]{1,0:T(8,128)(2,1)}) %all-gather.8.cloned.1.call-update) | async-done | bytes 16777232 | tf_op jit(solution)/shard_map/all_gather | solution.py:520
  354.1 39.0 %experts_forward.2 = (bf16[16,128,2048]{2,1,0:T(8,128)(2,1)}, f32[16,8,128]{2,1,0:T(8,128)}, f32[8,512,512]{2,1,0:T(8,128)}, bf16[8,1024,256]{2,1,0:T(8,128)(2,1)}, bf16[8,32,32,2048]{3,2,1,0:T(8,128)(2,1)}) custom-call(s32[1]{0:T(128)} %bitcast.1._, f32[32,8,128]{2,1,0:T(8,128)} %dynamic-slice_convert_fusion.slots_ref, ...), custom_call_target="tpu_custom_call" | custom-call | flops 85899345920 | bytes 67108864 | tf_op jit(solution)/shard_map/experts_forward/pallas_call | solution.py:395
  393.4 38.9 %experts_forward.3 = (bf16[16,64,2048]{2,1,0:T(8,128)(2,1)}, bf16[16,64,2048]{2,1,0:T(8,128)(2,1)}, f32[16,8,128]{2,1,0:T(8,128)}, f32[8,512,512]{2,1,0:T(8,128)...) custom-call(s32[1]{0:T(128)} %bitcast._, ...), custom_call_target="tpu_custom_call", output_to_operand_aliasing={{4}: (7, {}), {5}: (8, {})} | custom-call | flops 85899345920 | bytes 67108864 | tf_op jit(solution)/shard_map/experts_forward/pallas_call | solution.py:395
  451.1 22.5 %all-gather.10.cloned.1.call-done = bf16[4096,2048]{1,0:T(8,128)(2,1)} async-done(((bf16[128,2048]{1,0:T(8,128)(2,1)}), bf16[4096,2048]{1,0:T(8,128)(2,1)}) %all-gather.10.cloned.1.call-update) | async-done | bytes 16777232 | tf_op jit(solution)/shard_map/all_gather | solution.py:520
  473.6 39.0 %experts_backward.3 = (bf16[16,128,2048]{2,1,0:T(8,128)(2,1)}, f32[16,8,128]{2,1,0:T(8,128)}, bf16[8,1024,256]{2,1,0:T(8,128)(2,1)}, bf16[8,1024,256]{2,1,0:T(8,128)(2,1)}, bf16[8,32,32,2048]{3,2,1,0:T(8,128)(2,1)}) custom-call(s32[1]{0:T(128)} %bitcast.1._, f32[32,8,128]{2,1,0:T(8,128)} %dynamic-slice_convert_fusion.slots_ref, ...), custom_call_target="tpu_custom_call" | custom-call | flops 85899345920 | bytes 67108864 | tf_op jit(solution)/shard_map/experts_backward/pallas_call | solution.py:395
  541.2 24.6 %experts_backward.4 = (bf16[16,32,2048]{2,1,0:T(8,128)(2,1)}, bf16[16,32,2048]{2,1,0:T(8,128)(2,1)}, bf16[16,32,2048]{2,1,0:T(8,128)(2,1)}, bf16[16,32,2048]{2,1...) custom-call(s32[1]{0:T(128)} %bitcast._, ...), custom_call_target="tpu_custom_call", output_to_operand_aliasing={{5}: (8, {}), {6}: (9, {}), {7}: (10, {})} | custom-call | flops 42949672960 | bytes 33554432 | tf_op jit(solution)/shard_map/experts_backward/pallas_call | solution.py:395
  576.4 24.8 %experts_backward.5 = (bf16[16,32,2048]{2,1,0:T(8,128)(2,1)}, bf16[16,32,2048]{2,1,0:T(8,128)(2,1)}, bf16[16,32,2048]{2,1,0:T(8,128)(2,1)}, bf16[16,32,2048]{2,1...) custom-call(s32[1]{0:T(128)} %bitcast._, ...), custom_call_target="tpu_custom_call", output_to_operand_aliasing={{0}: (8, {}), {1}: (9, {}), {2}: (10, {}), {3}: (11, {}), {... | custom-call | flops 42949672960 | bytes 33554432 | tf_op jit(solution)/shard_map/experts_backward/pallas_call | solution.py:395
  620.8 21.4 %fusion.124 = f32[8,2048,256]{2,1,0:T(8,128)} fusion(bf16[8,1024,2048]{2,1,0:T(8,128)(2,1)} %bitcast.479, bf16[8,1024,256]{2,1,0:T(8,128)(2,1)} %get-tuple-element.230), kind=kOutput, calls=%fused_computation.372 | convolution fusion | flops 8589934592 | bytes 54525952 | tf_op jit(solution)/shard_map/erd,erh->edh/dot_general | solution.py:677
  664.5 19.8 %fusion.125 = f32[8,256,2048]{2,1,0:T(8,128)} fusion(bf16[8,1024,256]{2,1,0:T(8,128)(2,1)} %get-tuple-element.241, bf16[8,1024,2048]{2,1,0:T(8,128)(2,1)} %bitcast.478), kind=kOutput, calls=%fused_computation.373 | convolution fusion | flops 8589934592 | bytes 54525952 | tf_op jit(solution)/shard_map/erh,erd->ehd/dot_general | solution.py:677
  700.0 21.1 %fusion.126 = f32[8,2048,256]{2,1,0:T(8,128)} fusion(bf16[8,1024,2048]{2,1,0:T(8,128)(2,1)} %bitcast.480, bf16[8,1024,256]{2,1,0:T(8,128)(2,1)} %get-tuple-element.248), kind=kOutput, calls=%fused_computation.374 | convolution fusion | flops 8589934592 | bytes 54525952 | tf_op jit(solution)/shard_map/erd,erh->edh/dot_general | solution.py:677
  724.8 10.3 %collective-permute-done.32 = bf16[64,2048]{1,0:T(8,128)(2,1)S(1)} collective-permute-done((bf16[64,2048]{1,0:T(8,128)(2,1)S(1)}, bf16[64,2048]{1,0:T(8,128)(2,1)S(1)}, u32[]{:S(2)}, u32[]{:S(2)}) %collective-permute-start.32) | collective-permute-done | bytes 262176 | tf_op jit(solution)/shard_map/ppermute | solution.py:92
  735.2 5.6 collective-permute-done.33
  745.8 8.1 collective-permute-done.34
  758.5 6.4 fusion.33
  801.2 14.8 %fusion.37 = (f32[128]{0:T(128)S(1)}, f32[2048]{0:T(1024)S(1)}, f32[128,2048]{1,0:T(8,128)}) fusion(bf16[128,2048]{1,0:T(8,128)(2,1)S(1)} %copy-done.20, f32[2048]{0:T(1024)S(1)} %copy-done.89, f32[128]{0:T(128)S(1)} %copy-done.106, bf16[2048,6144]{1,0:T(8,128)(2,1)} %all-gather.6.cloned.1.call-done, bf16[128,2048]{1,0:T(8,128)(2,1)} %copy.253, ...), kind=kOutput, calls=%fused_computation.74 | convolution fusion | flops 3227777024 | bytes 28328960 | tf_op jit(solution)/shard_map/te,ce->tc/dot_general | solution.py:778
  832.5 19.2 %collective-permute-done.48 = bf16[2,2,2,64,1024]{4,3,2,1,0:T(8,128)(2,1)S(1)} collective-permute-done((bf16[2,2,2,64,1024]{4,3,2,1,0:T(8,128)(2,1)S(1)}, bf16[2,2,2,64,1024]{4,3,2,1,0:T(8,128)(2,1)S(1)}, u32[]{:S(2)}, u32[]{:S(2)}) %collective-permute-start.48) | collective-permute-done | bytes 1048608 | tf_op jit(solution)/shard_map/ppermute | solution.py:92
  866.5 8.3 collective-permute-done.50
  876.0 9.6 collective-permute-done.51
  900.7 9.9 %collective-permute-done.55 = bf16[2,64,1024]{2,1,0:T(8,128)(2,1)S(1)} collective-permute-done((bf16[2,64,1024]{2,1,0:T(8,128)(2,1)S(1)}, bf16[2,64,1024]{2,1,0:T(8,128)(2,1)S(1)}, u32[]{:S(2)}, u32[]{:S(2)}) %collective-permute-start.55) | collective-permute-done | bytes 262176 | tf_op jit(solution)/shard_map/ppermute | solution.py:92
  920.8 8.4 collective-permute-done.58
  (625 shorter events, 337.8 us)
Async XLA Ops:
  7.2 199.6 %all-gather.6.cloned.1.call-start = ((), (), s32[]{:S(2)}) async-start(), calls=%async_computation | async-start | bytes 25952256 | tf_op jit(solution)/shard_map/all_gather | solution.py:520
  9.3 344.7 %all-gather.8.cloned.1.call-start = ((), (), s32[]{:S(2)}) async-start(), calls=%async_computation.1 | async-start | bytes 17301504 | tf_op jit(solution)/shard_map/all_gather | solution.py:520
  25.4 28.8 %collective-permute-start.1 = (bf16[1,1,1,2,1,64,2048]{6,5,4,3,2,1,0:T(8,128)(2,1)S(1)}, bf16[1,1,1,2,1,64,2048]{6,5,4,3,2,1,0:T(8,128)(2,1)S(1)}, u32[]{:S(2)}, u32[]{:S(2)}) collective-permute-start(bf16[1,1,1,2,1,64,2048]{6,5,4,3,2,1,0:T(8,128)(2,1)S(1)} %constant_dynamic-update-slice_fusion.23), channel_id=1, source_target_pairs={{0,1},{1,0},{2,3},{3,2},{4,5},{5,4},{6,7},{7,6},{8,9},{9,8},{10,11... | collective-permute-start | bytes 1572872 | tf_op jit(solution)/shard_map/ppermute | solution.py:92
  57.1 25.2 %collective-permute-start.2 = (bf16[1,1,1,2,2,32,2048]{6,5,4,3,2,1,0:T(8,128)(2,1)}, bf16[1,1,1,2,2,32,2048]{6,5,4,3,2,1,0:T(8,128)(2,1)}, u32[]{:S(2)}, u32[]{:S(2)}) collective-permute-start(bf16[1,1,1,2,2,32,2048]{6,5,4,3,2,1,0:T(8,128)(2,1)} %get-tuple-element.360), channel_id=1, source_target_pairs={{0,8},{4,12},{8,0},{12,4},{16,24},{20,28},{24,16},{28,20},{1,9},{5... | collective-permute-start | bytes 1572872 | tf_op jit(solution)/shard_map/ppermute | solution.py:92
  77.4 38.1 %collective-permute-start.5 = (bf16[2,1,1,2,2,32,2048]{6,5,4,3,2,1,0:T(8,128)(2,1)S(1)}, bf16[2,1,1,2,2,32,2048]{6,5,4,3,2,1,0:T(8,128)(2,1)S(1)}, u32[]{:S(2)}, u32[]{:S(2)}) collective-permute-start(bf16[2,1,1,2,2,32,2048]{6,5,4,3,2,1,0:T(8,128)(2,1)S(1)} %constant_dynamic-update-slice_fusion.15), channel_id=1, source_target_pairs={{0,8},{4,12},{8,0},{12,4},{16,24},{20,28},{24,16},{28,20},{1,9},{5... | collective-permute-start | bytes 3145736 | tf_op jit(solution)/shard_map/ppermute | solution.py:92
  83.3 32.3 %collective-permute-start.3 = (bf16[1,2,1,2,2,32,2048]{6,5,4,3,2,1,0:T(8,128)(2,1)S(1)}, bf16[1,2,1,2,2,32,2048]{6,5,4,3,2,1,0:T(8,128)(2,1)}, u32[]{:S(2)}, u32[]{:S(2)}) collective-permute-start(bf16[1,2,1,2,2,32,2048]{6,5,4,3,2,1,0:T(8,128)(2,1)S(1)} %constant_dynamic-update-slice_fusion.19), channel_id=1, source_target_pairs={{0,16},{4,20},{8,24},{12,28},{16,0},{20,4},{24,8},{28,12},{1,17},{... | collective-permute-start | bytes 3145736 | tf_op jit(solution)/shard_map/ppermute | solution.py:92
  125.3 60.9 %collective-permute-start.6 = (bf16[2,2,1,2,2,64,2048]{6,5,4,3,2,1,0:T(8,128)(2,1)}, bf16[2,2,1,2,2,64,2048]{6,5,4,3,2,1,0:T(8,128)(2,1)}, u32[]{:S(2)}, u32[]{:S(2)}) collective-permute-start(bf16[2,2,1,2,2,64,2048]{6,5,4,3,2,1,0:T(8,128)(2,1)} %get-tuple-element.330), channel_id=1, source_target_pairs={{0,4},{4,0},{8,12},{12,8},{16,20},{20,16},{24,28},{28,24},{1,5},{5... | collective-permute-start | bytes 12582920 | tf_op jit(solution)/shard_map/ppermute | solution.py:92
  154.4 29.7 %collective-permute-start.10 = (bf16[2,2,1,2,1,128,128]{6,5,4,3,2,1,0:T(8,128)(2,1)S(1)}, bf16[2,2,1,2,1,128,128]{6,5,4,3,2,1,0:T(8,128)(2,1)S(1)}, u32[]{:S(2)}, u32[]{:S(2)}) collective-permute-start(bf16[2,2,1,2,1,128,128]{6,5,4,3,2,1,0:T(8,128)(2,1)S(1)} %constant_dynamic-update-slice_fusion.5), channel_id=1, source_target_pairs={{0,1},{1,0},{2,3},{3,2},{4,5},{5,4},{6,7},{7,6},{8,9},{9,8},{10,11... | collective-permute-start | bytes 786440 | tf_op jit(solution)/shard_map/ppermute | solution.py:92
  238.8 234.9 %all-gather.10.cloned.1.call-start = ((), (), s32[]{:S(2)}) async-start(), calls=%async_computation.2 | async-start | bytes 17301504 | tf_op jit(solution)/shard_map/all_gather | solution.py:520
  393.1 39.2 %collective-permute-start.12 = (bf16[16,128,2048]{2,1,0:T(8,128)(2,1)}, bf16[16,128,2048]{2,1,0:T(8,128)(2,1)}, u32[]{:S(2)}, u32[]{:S(2)}) collective-permute-start(bf16[16,128,2048]{2,1,0:T(8,128)(2,1)} %get-tuple-element.162), channel_id=1, source_target_pairs={{0,4},{4,0},{8,12},{12,8},{16,20},{20,16},{24,28},{28,24},{1,5},{5... | collective-permute-start | bytes 25165832 | tf_op jit(solution)/shard_map/ppermute | solution.py:92
  442.1 70.5 %collective-permute-start.13 = (bf16[2,2,2,64,2048]{4,3,1,2,0:T(8,128)(2,1)S(1)}, bf16[2,2,2,64,2048]{4,3,1,2,0:T(8,128)(2,1)}, u32[]{:S(2)}, u32[]{:S(2)}) collective-permute-start(bf16[2,2,2,64,2048]{4,3,1,2,0:T(8,128)(2,1)S(1)} %fusion.3), channel_id=1, source_target_pairs={{0,16},{4,20},{8,24},{12,28},{16,0},{20,4},{24,8},{28,12},{1,17},{... | collective-permute-start | bytes 6291464 | tf_op jit(solution)/shard_map/ppermute | solution.py:92
  450.7 66.2 %collective-permute-start.14 = (bf16[2,2,2,64,2048]{4,3,1,2,0:T(8,128)(2,1)}, bf16[2,2,2,64,2048]{4,3,1,2,0:T(8,128)(2,1)}, u32[]{:S(2)}, u32[]{:S(2)}) collective-permute-start(bf16[2,2,2,64,2048]{4,3,1,2,0:T(8,128)(2,1)} %fusion.4), channel_id=1, source_target_pairs={{0,8},{4,12},{8,0},{12,4},{16,24},{20,28},{24,16},{28,20},{1,9},{5... | collective-permute-start | bytes 6291464 | tf_op jit(solution)/shard_map/ppermute | solution.py:92
  521.2 48.5 %collective-permute-start.17 = (bf16[16,128,2048]{2,1,0:T(8,128)(2,1)}, bf16[16,128,2048]{2,1,0:T(8,128)(2,1)}, u32[]{:S(2)}, u32[]{:S(2)}) collective-permute-start(bf16[16,128,2048]{2,1,0:T(8,128)(2,1)} %get-tuple-element.195), channel_id=1, source_target_pairs={{0,4},{4,0},{8,12},{12,8},{16,20},{20,16},{24,28},{28,24},{1,5},{5... | collective-permute-start | bytes 25165832 | tf_op jit(solution)/shard_map/ppermute | solution.py:92
  538.7 27.1 %collective-permute-start.16 = (bf16[2,2,64,2048]{3,2,0,1:T(8,128)(2,1)}, bf16[2,2,64,2048]{3,2,0,1:T(8,128)(2,1)}, u32[]{:S(2)}, u32[]{:S(2)}) collective-permute-start(bf16[2,2,64,2048]{3,2,0,1:T(8,128)(2,1)} %dynamic-slice_bitcast_fusion.5), channel_id=1, source_target_pairs={{0,16},{4,20},{8,24},{12,28},{16,0},{20,4},{24,8},{28,12},{1,17},{... | collective-permute-start | bytes 3145736 | tf_op jit(solution)/shard_map/ppermute | solution.py:92
  538.8 29.0 %collective-permute-start.15 = (bf16[2,2,64,2048]{3,2,0,1:T(8,128)(2,1)S(1)}, bf16[2,2,64,2048]{3,2,0,1:T(8,128)(2,1)}, u32[]{:S(2)}, u32[]{:S(2)}) collective-permute-start(bf16[2,2,64,2048]{3,2,0,1:T(8,128)(2,1)S(1)} %dynamic-slice_bitcast_fusion.6), channel_id=1, source_target_pairs={{0,8},{4,12},{8,0},{12,4},{16,24},{20,28},{24,16},{28,20},{1,9},{5... | collective-permute-start | bytes 3145736 | tf_op jit(solution)/shard_map/ppermute | solution.py:92
  570.7 34.4 %collective-permute-start.20 = (bf16[256,2048]{0,1:T(8,128)(2,1)S(1)}, bf16[256,2048]{0,1:T(8,128)(2,1)}, u32[]{:S(2)}, u32[]{:S(2)}) collective-permute-start(bf16[256,2048]{0,1:T(8,128)(2,1)S(1)} %copy-done.28), channel_id=1, source_target_pairs={{0,8},{4,12},{8,0},{12,4},{16,24},{20,28},{24,16},{28,20},{1,9},{5... | collective-permute-start | bytes 3145736 | tf_op jit(solution)/shard_map/ppermute | solution.py:92
  572.5 30.9 %collective-permute-start.19 = (bf16[2,128,2048]{2,1,0:T(8,128)(2,1)}, bf16[2,128,2048]{2,1,0:T(8,128)(2,1)}, u32[]{:S(2)}, u32[]{:S(2)}) collective-permute-start(bf16[2,128,2048]{2,1,0:T(8,128)(2,1)} %dynamic-slice_bitcast_fusion.4), channel_id=1, source_target_pairs={{0,1},{1,0},{2,3},{3,2},{4,5},{5,4},{6,7},{7,6},{8,9},{9,8},{10,11... | collective-permute-start | bytes 3145736 | tf_op jit(solution)/shard_map/ppermute | solution.py:92
  574.6 26.6 %collective-permute-start.21 = (bf16[256,1024]{0,1:T(8,128)(2,1)S(1)}, bf16[256,1024]{0,1:T(8,128)(2,1)}, u32[]{:S(2)}, u32[]{:S(2)}) collective-permute-start(bf16[256,1024]{0,1:T(8,128)(2,1)S(1)} %slice.125), channel_id=1, source_target_pairs={{0,16},{4,20},{8,24},{12,28},{16,0},{20,4},{24,8},{28,12},{1,17},{... | collective-permute-start | bytes 1572872 | tf_op jit(solution)/shard_map/ppermute | solution.py:92
  613.9 32.6 %collective-permute-start.22 = (bf16[2,2,2,32,2048]{4,3,1,2,0:T(8,128)(2,1)}, bf16[2,2,2,32,2048]{4,3,1,2,0:T(8,128)(2,1)}, u32[]{:S(2)}, u32[]{:S(2)}) collective-permute-start(bf16[2,2,2,32,2048]{4,3,1,2,0:T(8,128)(2,1)} %fusion.42), channel_id=1, source_target_pairs={{0,16},{4,20},{8,24},{12,28},{16,0},{20,4},{24,8},{28,12},{1,17},{... | collective-permute-start | bytes 3145736 | tf_op jit(solution)/shard_map/ppermute | solution.py:92
  617.7 30.7 %collective-permute-start.23 = (bf16[2,2,2,32,2048]{4,3,1,2,0:T(8,128)(2,1)}, bf16[2,2,2,32,2048]{4,3,1,2,0:T(8,128)(2,1)}, u32[]{:S(2)}, u32[]{:S(2)}) collective-permute-start(bf16[2,2,2,32,2048]{4,3,1,2,0:T(8,128)(2,1)} %fusion.43), channel_id=1, source_target_pairs={{0,8},{4,12},{8,0},{12,4},{16,24},{20,28},{24,16},{28,20},{1,9},{5... | collective-permute-start | bytes 3145736 | tf_op jit(solution)/shard_map/ppermute | solution.py:92
  651.4 38.9 %collective-permute-start.26 = (bf16[2,2,32,2048]{3,2,0,1:T(8,128)(2,1)}, bf16[2,2,32,2048]{3,2,0,1:T(8,128)(2,1)}, u32[]{:S(2)}, u32[]{:S(2)}) collective-permute-start(bf16[2,2,32,2048]{3,2,0,1:T(8,128)(2,1)} %dynamic-slice_bitcast_fusion.15), channel_id=1, source_target_pairs={{0,16},{4,20},{8,24},{12,28},{16,0},{20,4},{24,8},{28,12},{1,17},{... | collective-permute-start | bytes 1572872 | tf_op jit(solution)/shard_map/ppermute | solution.py:92
  653.5 38.2 %collective-permute-start.25 = (bf16[2,2,32,2048]{3,2,0,1:T(8,128)(2,1)}, bf16[2,2,32,2048]{3,2,0,1:T(8,128)(2,1)}, u32[]{:S(2)}, u32[]{:S(2)}) collective-permute-start(bf16[2,2,32,2048]{3,2,0,1:T(8,128)(2,1)} %dynamic-slice_bitcast_fusion.16), channel_id=1, source_target_pairs={{0,8},{4,12},{8,0},{12,4},{16,24},{20,28},{24,16},{28,20},{1,9},{5... | collective-permute-start | bytes 1572872 | tf_op jit(solution)/shard_map/ppermute | solution.py:92
  656.2 36.9 %collective-permute-start.27 = (bf16[2,2,2,32,2048]{4,3,1,2,0:T(8,128)(2,1)}, bf16[2,2,2,32,2048]{4,3,1,2,0:T(8,128)(2,1)}, u32[]{:S(2)}, u32[]{:S(2)}) collective-permute-start(bf16[2,2,2,32,2048]{4,3,1,2,0:T(8,128)(2,1)} %fusion.44), channel_id=1, source_target_pairs={{0,16},{4,20},{8,24},{12,28},{16,0},{20,4},{24,8},{28,12},{1,17},{... | collective-permute-start | bytes 3145736 | tf_op jit(solution)/shard_map/ppermute | solution.py:92
  660.8 34.7 %collective-permute-start.28 = (bf16[2,2,2,32,2048]{4,3,1,2,0:T(8,128)(2,1)}, bf16[2,2,2,32,2048]{4,3,1,2,0:T(8,128)(2,1)}, u32[]{:S(2)}, u32[]{:S(2)}) collective-permute-start(bf16[2,2,2,32,2048]{4,3,1,2,0:T(8,128)(2,1)} %fusion.45), channel_id=1, source_target_pairs={{0,8},{4,12},{8,0},{12,4},{16,24},{20,28},{24,16},{28,20},{1,9},{5... | collective-permute-start | bytes 3145736 | tf_op jit(solution)/shard_map/ppermute | solution.py:92
  689.4 35.4 %collective-permute-start.39 = (f32[64,128]{1,0:T(8,128)S(1)}, f32[64,128]{1,0:T(8,128)S(1)}, u32[]{:S(2)}, u32[]{:S(2)}) collective-permute-start(f32[64,128]{1,0:T(8,128)S(1)} %fusion.91), channel_id=1, source_target_pairs={{0,8},{4,12},{8,0},{12,4},{16,24},{20,28},{24,16},{28,20},{1,9},{5... | collective-permute-start | bytes 98312 | tf_op jit(solution)/shard_map/ppermute | solution.py:92
  826.1 25.5 %collective-permute-start.48 = (bf16[2,2,2,64,1024]{4,3,2,1,0:T(8,128)(2,1)S(1)}, bf16[2,2,2,64,1024]{4,3,2,1,0:T(8,128)(2,1)S(1)}, u32[]{:S(2)}, u32[]{:S(2)}) collective-permute-start(bf16[2,2,2,64,1024]{4,3,2,1,0:T(8,128)(2,1)S(1)} %dynamic-slice_bitcast_fusion.3), channel_id=1, source_target_pairs={{0,16},{4,20},{8,24},{12,28},{16,0},{20,4},{24,8},{28,12},{1,17},{... | collective-permute-start | bytes 3145736 | tf_op jit(solution)/shard_map/ppermute | solution.py:92
  827.1 25.2 %collective-permute-start.49 = (bf16[2,2,2,64,1024]{4,3,2,1,0:T(8,128)(2,1)S(1)}, bf16[2,2,2,64,1024]{4,3,2,1,0:T(8,128)(2,1)S(1)}, u32[]{:S(2)}, u32[]{:S(2)}) collective-permute-start(bf16[2,2,2,64,1024]{4,3,2,1,0:T(8,128)(2,1)S(1)} %dynamic-slice_bitcast_fusion.2), channel_id=1, source_target_pairs={{0,8},{4,12},{8,0},{12,4},{16,24},{20,28},{24,16},{28,20},{1,9},{5... | collective-permute-start | bytes 3145736 | tf_op jit(solution)/shard_map/ppermute | solution.py:92
  854.0 32.9 %collective-permute-start.52 = (bf16[2,2,2,64,1024]{4,3,2,1,0:T(8,128)(2,1)}, bf16[2,2,2,64,1024]{4,3,2,1,0:T(8,128)(2,1)}, u32[]{:S(2)}, u32[]{:S(2)}) collective-permute-start(bf16[2,2,2,64,1024]{4,3,2,1,0:T(8,128)(2,1)} %dynamic-slice_bitcast_fusion.1), channel_id=1, source_target_pairs={{0,16},{4,20},{8,24},{12,28},{16,0},{20,4},{24,8},{28,12},{1,17},{... | collective-permute-start | bytes 3145736 | tf_op jit(solution)/shard_map/ppermute | solution.py:92
  860.5 25.1 %collective-permute-start.51 = (bf16[2,2,64,1024]{3,2,1,0:T(8,128)(2,1)}, bf16[2,2,64,1024]{3,2,1,0:T(8,128)(2,1)}, u32[]{:S(2)}, u32[]{:S(2)}) collective-permute-start(bf16[2,2,64,1024]{3,2,1,0:T(8,128)(2,1)} %dynamic-slice_bitcast_fusion.9), channel_id=1, source_target_pairs={{0,1},{1,0},{2,3},{3,2},{4,5},{5,4},{6,7},{7,6},{8,9},{9,8},{10,11... | collective-permute-start | bytes 1572872 | tf_op jit(solution)/shard_map/ppermute | solution.py:92
  863.7 25.3 %collective-permute-start.53 = (bf16[2,2,2,64,1024]{4,3,2,1,0:T(8,128)(2,1)}, bf16[2,2,2,64,1024]{4,3,2,1,0:T(8,128)(2,1)}, u32[]{:S(2)}, u32[]{:S(2)}) collective-permute-start(bf16[2,2,2,64,1024]{4,3,2,1,0:T(8,128)(2,1)} %dynamic-slice_bitcast_fusion), channel_id=1, source_target_pairs={{0,8},{4,12},{8,0},{12,4},{16,24},{20,28},{24,16},{28,20},{1,9},{5... | collective-permute-start | bytes 3145736 | tf_op jit(solution)/shard_map/ppermute | solution.py:92
  894.7 25.9 %collective-permute-start.57 = (bf16[2,2,64,1024]{3,2,1,0:T(8,128)(2,1)S(1)}, bf16[2,2,64,1024]{3,2,1,0:T(8,128)(2,1)S(1)}, u32[]{:S(2)}, u32[]{:S(2)}) collective-permute-start(bf16[2,2,64,1024]{3,2,1,0:T(8,128)(2,1)S(1)} %dynamic-slice_bitcast_fusion.8), channel_id=1, source_target_pairs={{0,1},{1,0},{2,3},{3,2},{4,5},{5,4},{6,7},{7,6},{8,9},{9,8},{10,11... | collective-permute-start | bytes 1572872 | tf_op jit(solution)/shard_map/ppermute | solution.py:92
  895.7 33.5 %collective-permute-start.58 = (bf16[2,2,64,1024]{3,2,1,0:T(8,128)(2,1)S(1)}, bf16[2,2,64,1024]{3,2,1,0:T(8,128)(2,1)S(1)}, u32[]{:S(2)}, u32[]{:S(2)}) collective-permute-start(bf16[2,2,64,1024]{3,2,1,0:T(8,128)(2,1)S(1)} %dynamic-slice_bitcast_fusion.7), channel_id=1, source_target_pairs={{0,1},{1,0},{2,3},{3,2},{4,5},{5,4},{6,7},{7,6},{8,9},{9,8},{10,11... | collective-permute-start | bytes 1572872 | tf_op jit(solution)/shard_map/ppermute | solution.py:92
  (151 other events, 1262.8 us)
Sparse Core Ops, SparseCore 0:
  11.5 195.2 all-gather.5
  238.9 115.1 all-gather.7
  357.1 116.5 all-gather.9

commit v3 on v2

--- a/solution.py
+++ b/solution.py
@@ -63,6 +63,10 @@
 
 def together(*values):
     return lax.optimization_barrier(values)
+
+
+def chosen(index, cases):
+    return lax.select_n(index.astype(jnp.int32), *cases)
 
 
 class Grid:
@@ -75,21 +79,21 @@
         while chips % nx:
             nx -= 1
         nw = 2 - self.tp % 2
-        self.size = {"y": chips // nx, "x": nx, "c": 2, "u": self.tp // nw, "w": nw}
-        self.stride = {"y": 2 * nx, "x": 2, "c": 1, "u": nw, "w": 1}
+        self.size = {"y": chips // nx, "x": nx, "c": 2, "u": self.tp // nw, "w": nw, "z": self.tp}
+        self.stride = {"y": 2 * nx, "x": 2, "c": 1, "u": nw, "w": 1, "z": 1}
         self.shape = tuple(self.size[axis] for axis in self.axes)
 
     def place(self, axis):
-        whole = lax.axis_index("tp" if axis in "uw" else "ep")
+        whole = lax.axis_index("tp" if axis in "uwz" else "ep")
         return whole // self.stride[axis] % self.size[axis]
 
     def shift(self, values, axis, step):
         count, stride = self.size[axis], self.stride[axis]
         pairs = []
-        for i in range(self.tp if axis in "uw" else self.ep):
+        for i in range(self.tp if axis in "uwz" else self.ep):
             own = i // stride % count
             pairs.append((i, i + ((own + step) % count - own) * stride))
-        return lax.ppermute(values, "tp" if axis in "uw" else "ep", pairs)
+        return lax.ppermute(values, "tp" if axis in "uwz" else "ep", pairs)
 
     def gather_axis(self, values, axis):
         dim, count, own = self.axes.index(axis), self.size[axis], self.place(axis)
@@ -107,16 +111,16 @@
             values = self.gather_axis(values, axis)
         return values
 
-    def gather_rows(self, values):
-        rows, columns = values.shape
+    def gather_first(self, values):
+        rows = values.shape[0]
         values = self.gather(values, "uw")
         halves = values[..., : rows // 2, :], values[..., rows // 2 :, :]
-        halves = [
-            self.gather_axis(self.gather_axis(half, first), second)
-            for half, (first, second) in zip(halves, ("xy", "yx"), strict=True)
-        ]
+        return [self.gather_axis(half, axis) for half, axis in zip(halves, "xy", strict=True)]
+
+    def gather_second(self, halves):
+        halves = [self.gather_axis(half, axis) for half, axis in zip(halves, "yx", strict=True)]
         values = self.gather_axis(jnp.concatenate(halves, axis=-2), "c")
-        return values.reshape(-1, columns)
+        return values.reshape(-1, values.shape[-1])
 
     def reduce_axis(self, values, axis, axes):
         dim, count, own = axes.index(axis), self.size[axis], self.place(axis)
@@ -146,36 +150,37 @@
         ]
 
     def columns_from_line(self, values, axis):
-        rows, count, own = values.shape[0], self.size[axis], self.place(axis)
-        values = values.reshape(rows, count, -1)
-
-        def part(step):
-            return lax.dynamic_index_in_dim(values, (own + step) % count, 1, keepdims=False)
-
-        taken = jnp.stack(
-            [part(0)] + [self.shift(part(step), axis, step) for step in range(1, count)]
-        )
+        count, own = self.size[axis], self.place(axis)
+        parts = jnp.split(values, count, axis=1)
+        taken = [chosen(own, parts)]
+        for step in range(1, count):
+            taken.append(self.shift(chosen((own + step) % count, parts), axis, step))
+        taken = jnp.stack(taken)
         taken = jnp.stack([taken, self.shift(taken, "c", 1)], axis=1)
         return taken.reshape(-1, taken.shape[-1])
 
     def rows_from_line(self, values, axis):
         count, own = self.size[axis], self.place(axis)
-
-        def part(step):
-            return lax.dynamic_index_in_dim(values, (own + step) % count, 0)
-
-        whole = jnp.zeros(values.shape, values.dtype)
-        for step in range(count):
-            got = part(0) if step == 0 else self.shift(part(step), axis, step)
-            whole = lax.dynamic_update_slice_in_dim(whole, got, (own - step) % count, 0)
-        return whole.transpose(1, 0, 2).reshape(values.shape[1], -1)
+        got = [chosen(own, list(values))]
+        for step in range(1, count):
+            got.append(self.shift(chosen((own + step) % count, list(values)), axis, step))
+        return jnp.concatenate(
+            [chosen((own - j) % count, got) for j in range(count)], axis=1
+        ).astype(wide)
 
     def reduce_first(self, pair):
         return [self.reduce_axis(v, axis, "yxuw") for v, axis in zip(pair, "yx", strict=True)]
 
+    def alike(self, pair):
+        return jnp.stack(pair) if self.size["y"] == self.size["x"] else pair
+
     def reduce_both(self, pair, axis):
         left = "uw" if axis == "w" else "u"
-        return [self.reduce_axis(v, axis, line + left) for v, line in zip(pair, "xy", strict=True)]
+        if isinstance(pair, list):
+            return [
+                self.reduce_axis(v, axis, line + left) for v, line in zip(pair, "xy", strict=True)
+            ]
+        return self.reduce_axis(pair, axis, "pl" + left)
 
     def rows_of_both(self, pair):
         return [self.rows_from_line(v, line) for v, line in zip(pair, "xy", strict=True)]
@@ -207,6 +212,30 @@
 def gate_column(pick, gates):
     spread = jnp.broadcast_to(gates[:, None, :], (gates.shape[0], CAP, gates.shape[1]))
     return jnp.sum(pick * spread.reshape(pick.shape), axis=1, keepdims=True)
+
+
+def product_kernel(left_ref, right_ref, out_ref):
+    out_ref[...] = dot(left_ref[...], right_ref[...], nt_dims)
+
+
+def turned_product(left, right, block=256):
+    rows, depth = left.shape
+    columns = right.shape[0]
+    return pl.pallas_call(
+        product_kernel,
+        grid=(columns // block,),
+        in_specs=[
+            pl.BlockSpec((rows, depth), lambda i: (0, 0)),
+            pl.BlockSpec((block, depth), lambda i: (i, 0)),
+        ],
+        out_specs=pl.BlockSpec((rows, block), lambda i: (0, i)),
+        out_shape=jax.ShapeDtypeStruct((rows, columns), wide),
+        compiler_params=pltpu.CompilerParams(vmem_limit_bytes=40 * 1024 * 1024),
+        cost_estimate=pl.CostEstimate(
+            flops=50 * rows * depth * columns, bytes_accessed=columns * depth * 2, transcendentals=0
+        ),
+        name="turned_product",
+    )(left, right)
 
 
 class Streams:
@@ -534,12 +563,9 @@
         ],
         axis=1,
     )
-    small_all = grid.gather(jnp.concatenate([shared, slots], axis=0), "xyuwc")
-    projections = gathered(jnp.concatenate([w_query, w_key, w_value], axis=1))
-    projections, output_full, small_all = together(
-        projections, grid.gather_rows(w_output), small_all
-    )
-    upstream_all = gathered(after(grad_out, projections)[None])
+    output_full = grid.gather_second(grid.gather_first(w_output))
+    small_all = after(jnp.concatenate([shared, slots], axis=0), output_full)
+    small_all = grid.gather(small_all, "xyuwc")
     small_all = small_all.reshape(blocks, weight_rows + expert_count, tokens_dev)
     shared_full = small_all[:, :weight_rows].reshape(model_width, tokens_dev)
     slots_all = small_all[:, weight_rows:]
@@ -547,10 +573,20 @@
     gains = shared_full[:, expert_count : expert_count + 4].astype(wide).T
     attn_gain, ffn_gain, query_gain, key_gain = gains[0], gains[1], gains[2], gains[3]
 
+    projections = gathered(jnp.concatenate([w_query, w_key, w_value], axis=1))
     inputs_full = hidden_in.astype(wide)
     scale_attn = lax.rsqrt(jnp.mean(inputs_full * inputs_full, axis=-1, keepdims=True) + epsilon)
     unit_attn = inputs_full * scale_attn
     normed_attn = (unit_attn * attn_gain).astype(low)
+    projections, output_full, normed_attn, query_gain, key_gain, ffn_gain = together(
+        projections,
+        output_full,
+        normed_attn,
+        query_gain,
+        key_gain,
+        ffn_gain,
+    )
+    upstream_all = gathered(after(grad_out, projections)[None])
     projected = jnp.dot(normed_attn, projections, preferred_element_type=wide)
     query_raw = projected[:, :model_width]
     key_raw = projected[:, model_width : 2 * model_width]
@@ -613,7 +649,6 @@
         ]
 
     groups = blocks // 2 // grid.tp
-    part = groups // 2
     forward_ins = (slots_here, router_turned, normed_all, (w_gate, w_up, w_down))
     y_ahead, gates_ahead, pre_ahead, *given = experts.forward(
         0, groups, 0, 1, turns[0], *forward_ins, []
@@ -641,11 +676,9 @@
         )
 
     def by_core(values):
-        values = values.reshape(tokens_dev, chips[0] * chips[1], 2, -1)
-        return [
-            lax.dynamic_index_in_dim(values, at, 2, keepdims=False).reshape(tokens_dev, -1)
-            for at in (1 - core, core)
-        ]
+        parts = jnp.split(values, 2 * chips[0] * chips[1], axis=1)
+        cut = [jnp.concatenate(parts[at::2], axis=1) for at in range(2)]
+        return [chosen(at, cut) for at in (1 - core, core)]
 
     away, kept = (
         jnp.concatenate(cut, axis=1)
@@ -653,22 +686,14 @@
     )
     ahead = backward(0, groups, 0, 1, gates_ahead, pre_ahead, [])
     expert_sums = grid.reduce_first(expert_sums)
-    (x_ahead, gate_grads_ahead, *given), expert_sums, slots_here = together(
-        ahead, expert_sums, slots_here
+    pair_rows = [kept, grid.shift(away, "c", 1)]
+    (x_ahead, gate_grads_ahead, *given), expert_sums, slots_here, pair_rows = together(
+        ahead, expert_sums, slots_here, pair_rows
     )
     x_away = grid.shift(x_ahead, "c", 1)
-    given = backward(0, part, 1, 4, gates_own, pre_own, given)
+    own = backward(0, groups, 1, 4, gates_own, pre_own, given)
     expert_sum = grid.reduce_second(expert_sums, 0)
-    pair_rows = jnp.concatenate([kept, grid.shift(away, "c", 1)], axis=0)
-    given, expert_sum, x_away, slots_here, pair_rows = together(
-        given, expert_sum, x_away, slots_here, pair_rows
-    )
-    own = backward(part, groups - part, 1, 4, gates_own, pre_own, given)
-    expert_sum = grid.reduce_axis(expert_sum, "w", "uw")
-    half = model_width // 2
-    x_rows = jnp.concatenate(grid.from_line(pair_rows, "x"), axis=0)
-    y_rows = jnp.concatenate(grid.from_line(pair_rows[:, :half], "y"), axis=0)
-    own, expert_sum, x_rows, y_rows = together(own, expert_sum, x_rows, y_rows)
+    own, expert_sum, x_away = together(own, expert_sum, x_away)
     *x_own, gate_grads_own, grad_gate_part, grad_up_part, rows_up = own
     rows_in = rows_in.reshape(local_experts, -1, model_width)
     rows_up = rows_up.reshape(local_experts, -1, model_width)
@@ -676,41 +701,52 @@
     def weight_grad(subscripts, left, right):
         return jnp.einsum(subscripts, left, right, preferred_element_type=wide)
 
-    x_own, x_away, rows_in, rows_up, inner_scaled, expert_sum = together(
-        x_own, x_away, rows_in, rows_up, inner_scaled, expert_sum
-    )
     sums = token_sums(x_away, x_own)
+    gate_grads = jnp.stack([gate_grads_own, gate_grads_ahead])
+    gate_grads = jnp.where(core == 0, gate_grads, gate_grads[::-1])
+    gate_grads = gate_grads.reshape((2,) + chips + (local_experts, tokens_dev))
     acc_gate = weight_grad("erd,erh->edh", rows_in, grad_gate_part)
     early = grid.reduce_first(sums[:2])
-    expert_sum = grid.reduce_axis(expert_sum, "u", "u")
-    gate_grads = jnp.stack([gate_grads_own, gate_grads_ahead])
+    expert_sum = grid.reduce_axis(expert_sum, "w", "uw")
+    gate_grads = grid.reduce_axis(gate_grads, "w", "cyxuw")
     early, late, acc_gate, expert_sum, rows_in, rows_up, gate_grads = together(
         early, sums[2:], acc_gate, expert_sum, rows_in, rows_up, gate_grads
     )
     acc_down = weight_grad("erh,erd->ehd", inner_scaled, rows_up)
     early = grid.reduce_second(early, 0)
     late = grid.reduce_first(late)
-    early, late, acc_down, rows_in = together(early, late, acc_down, rows_in)
+    expert_sum = grid.reduce_axis(expert_sum, "u", "u")
+    early, late, acc_down, rows_in, expert_sum, gate_grads = together(
+        early, late, acc_down, rows_in, expert_sum, gate_grads
+    )
     acc_up = weight_grad("erd,erh->edh", rows_in, grad_up_part)
     early = grid.reduce_axis(early, "w", "uw")
     late = grid.reduce_second(late, 0)
-    early, late, acc_up = together(early, late, acc_up)
-    early = grid.reduce_axis(early, "u", "u")
-    late = grid.reduce_axis(late, "w", "uw")
-    early, late = together(early, late)
-    late = grid.reduce_axis(late, "u", "u")
-    block_out = (mixed + expert_sum.astype(wide)).astype(low)
-
-    gate_grads = jnp.where(core == 0, gate_grads, gate_grads[::-1])
-    gate_grads = gate_grads.reshape((2,) + chips + (local_experts, tokens_dev))
-    gate_grads = grid.reduce_scatter(gate_grads, "wu", "cyxuw")
+    gate_grads = grid.reduce_axis(gate_grads, "u", "cyxu")
     gate_grads = lax.dynamic_update_slice_in_dim(
         jnp.zeros(gate_grads.shape[:3] + (expert_count, tokens_dev), wide),
         gate_grads,
         first_expert,
         3,
     )
-    grad_probs = grid.reduce_scatter(gate_grads, "cyx", "cyx").T
+    block_out = (mixed + expert_sum.astype(wide)).astype(low)
+    early, late, acc_up, gate_grads, pair_rows = together(
+        early, late, acc_up, gate_grads, pair_rows
+    )
+    early = grid.reduce_axis(early, "u", "u")
+    late = grid.reduce_axis(late, "w", "uw")
+    gate_grads = grid.reduce_axis(gate_grads, "c", "cyx")
+    pair_rows = jnp.concatenate(pair_rows, axis=0)
+    normed_rows, attended_rows = jnp.split(pair_rows, 2, axis=1)
+    y_rows = grid.from_line(normed_rows, "y")
+    attended_rows = grid.from_line(attended_rows, "x")
+    early, late, gate_grads, y_rows, attended_rows, normed_rows = together(
+        early, late, gate_grads, y_rows, attended_rows, normed_rows
+    )
+    late = grid.reduce_axis(late, "u", "u")
+    x_rows = grid.from_line(normed_rows, "x")
+    grad_probs = grid.reduce_scatter(gate_grads, "yx", "yx").T
+    early, late, grad_probs, x_rows = together(early, late, grad_probs, x_rows)
     back_sum, block_out, acc_gate, acc_up, acc_down = together(
         jnp.concatenate([early, late], axis=0), block_out, acc_gate, acc_up, acc_down
     )
@@ -766,16 +802,23 @@
         total = jnp.einsum("tc,te->ce", left, right, preferred_element_type=wide)
         return total.astype(low).reshape(chips + (weight_rows, -1))
 
-    first = [outer(x_rows[:, half:], output_columns), outer(y_rows, value_columns)]
+    first = [
+        outer(jnp.concatenate(attended_rows, axis=0), output_columns),
+        outer(jnp.concatenate(y_rows, axis=0), value_columns),
+    ]
     second = [
         grid.columns_from_line(grad_query_raw, "x"),
         grid.columns_from_line(grad_key_raw, "y"),
     ]
-    first, second = together(first, second)
-    first = grid.reduce_first(first)
-    second = [outer(x_rows[:, :half], second[0]), outer(y_rows, second[1])]
     grads = jnp.concatenate([grad_query_raw, grad_key_raw, grad_value_rows], axis=1)
-    grad_attn_normed = jnp.einsum("te,ce->tc", grads, projections, preferred_element_type=wide)
+    first, second, grads = together(first, second, grads)
+    first = grid.alike(grid.reduce_first(first))
+    second = [
+        outer(jnp.concatenate(x_rows, axis=0), second[0]),
+        outer(jnp.concatenate(y_rows, axis=0), second[1]),
+    ]
+    grad_attn_normed = turned_product(grads, projections)
+    first, second, grad_attn_normed = together(first, second, grad_attn_normed)
     grad_attn_gain = jnp.sum(grad_attn_normed * unit_attn, axis=0)
     grad_input = grad_mixed + rms_back(grad_attn_normed, unit_attn, attn_gain, scale_attn)
     gain_sums = jnp.stack(
@@ -784,9 +827,8 @@
     small_sums = jnp.concatenate([grad_router_local, gain_sums], axis=1).reshape(
         grid.shape + (weight_rows, expert_count + gain_sums.shape[1])
     )
-    first, second, small_sums, grad_input = together(first, second, small_sums, grad_input)
     first = grid.reduce_both(first, "w")
-    second = grid.reduce_first(second)
+    second = grid.alike(grid.reduce_first(second))
     small_sums = grid.reduce_scatter(small_sums, "c")
     first, second, small_sums = together(first, second, small_sums)
     first = grid.reduce_both(first, "u")
@@ -800,10 +842,8 @@
         grad_output, grad_value, second, small_sums
     )
     grad_query, grad_key = grid.rows_of_both(second)
-    small_sums = grid.reduce_scatter(small_sums, "wu", "uw")
-    grad_query, grad_key, grad_value, grad_output = (
-        grad.astype(wide) for grad in (grad_query, grad_key, grad_value, grad_output)
-    )
+    small_sums = small_sums.reshape((-1,) + small_sums.shape[2:])
+    small_sums = grid.reduce_axis(small_sums, "z", "z")
     return (
         block_out,
         grad_input,

time: 993 us -> 934 us (0.941)
  local copies, waits for them, and re-layouts: 151 us -> 110 us
  matrix products: 114 us -> 104 us
    all_gather x3, waiting for transfers between devices: 115 us -> 93.3 us  [gathered(): return lax.all_gather(values, both, axis=0, tiled=True)]
    dot_general x1 -> x0, matrix products: 14.8 us -> none  [on_device(): jnp.einsum('te,ce->tc', grads, projections, preferred_element_type=wide)]
    dynamic_update_slice x8 -> x0, local copies, waits for them, and re-layouts: 14.5 us -> none  [rows_from_line(): whole = lax.dynamic_update_slice_in_dim(whole, got, (own - step) % count, 0)]
    dynamic_slice x16 -> x0, local copies, waits for them, and re-layouts: 14.5 us -> none  [the longest x6 8.44 us: part(): lax.dynamic_index_in_dim(values, (own + step) % count, 1, keepdims=False)]
    pallas_call x0 -> x1, Pallas kernels: none -> 13.9 us  [turned_product(): pl.pallas_call(product_kernel, grid=(columns // block,), in_specs=[pl.Blo...]
    ppermute x69 -> x67, waiting for transfers between devices: 264 us -> 276 us  [shift(): return lax.ppermute(values, 'tp' if axis in 'uwz' else 'ep', pairs)]
    pallas_call x5 -> x4, Pallas kernels: 166 us -> 156 us  [call(): pl.pallas_call(functools.partial(kernel, base, len(goes_on), parts), grid...]
    unnamed x243 -> x235, local copies, waits for them, and re-layouts: 58.7 us -> 49.6 us
  transfers between devices with their start and end apart: 72 -> 70, of which waited for: 36 -> 40; matrix products, arithmetic and copies ran while one was open for 27% -> 23% of each run, Pallas kernels for 17% -> 18%
where the time goes in v3:
time: 934 us; the launch traced here: 924 us
  waiting for transfers between devices  370 us (40%)
  Pallas kernels  170 us (18%)
  local copies, waits for them, and re-layouts  110 us (12%)
  matrix products  104 us (11%)
  other arithmetic  81.5 us (9%)
  starting transfers between devices  71.7 us (8%)
  between operations  16.8 us (2%)
    ppermute x67, waiting for transfers between devices, shift(): return lax.ppermute(values, 'tp' if axis in 'uwz' else 'ep', pairs)  276 us
    pallas_call x4, Pallas kernels, call(): pl.pallas_call(functools.partial(kernel, base, len(goes_on), parts), grid...  156 us
    all_gather x3, waiting for transfers between devices, gathered(): return lax.all_gather(values, both, axis=0, tiled=True)  93.3 us
    ppermute x67, starting transfers between devices, shift(): return lax.ppermute(values, 'tp' if axis in 'uwz' else 'ep', pairs)  71.6 us
    dot_general x3, matrix products, weight_grad(): return jnp.einsum(subscripts, left, right, preferred_element_type=wide)  62.4 us
    unnamed x235, local copies, waits for them, and re-layouts  49.6 us
    convert_element_type x22, other arithmetic, reduce_axis(): return total.astype(kind)  28.3 us
  transfers between devices with their start and end apart: 70, of which 40 were waited for; matrix products, arithmetic and copies ran while one was open for 23% of the time, Pallas kernels for 18%

profile of v3, /device:TPU:0, one launch (start us, length us, event | category | flops | bytes accessed | tf_op | source)
XLA Modules:
  0.0 924.3 jit_solution(9787506832205282393)
XLA Ops:
  13.6 11.8 %collective-permute-done = bf16[1,1,1,1,1,64,2048]{6,5,4,3,2,1,0:T(8,128)(2,1)S(1)} collective-permute-done((bf16[1,1,1,1,1,64,2048]{6,5,4,3,2,1,0:T(8,128)(2,1)S(1)}, bf16[1,1,1,1,1,64,2048]{6,5,4,3,2,1,0:T(8,128)(2,1)S(1)}, u32[]{:S(2)}, u32[]{:S(2)}) %collective-permute-start) | collective-permute-done | bytes 262176 | tf_op jit(solution)/shard_map/ppermute | solution.py:96
  28.1 26.1 %collective-permute-done.1 = bf16[1,1,1,2,1,64,2048]{6,5,4,3,2,1,0:T(8,128)(2,1)S(1)} collective-permute-done((bf16[1,1,1,2,1,64,2048]{6,5,4,3,2,1,0:T(8,128)(2,1)S(1)}, bf16[1,1,1,2,1,64,2048]{6,5,4,3,2,1,0:T(8,128)(2,1)S(1)}, u32[]{:S(2)}, u32[]{:S(2)}) %collective-permute-start.1) | collective-permute-done | bytes 524320 | tf_op jit(solution)/shard_map/ppermute | solution.py:96
  58.5 18.8 %collective-permute-done.2 = bf16[1,1,1,2,2,32,2048]{6,5,4,3,2,1,0:T(8,128)(2,1)S(1)} collective-permute-done((bf16[1,1,1,2,2,32,2048]{6,5,4,3,2,1,0:T(8,128)(2,1)S(1)}, bf16[1,1,1,2,2,32,2048]{6,5,4,3,2,1,0:T(8,128)(2,1)S(1)}, u32[]{:S(2)}, u32[]{:S(2)}) %collective-permute-start.2) | collective-permute-done | bytes 524320 | tf_op jit(solution)/shard_map/ppermute | solution.py:96
  84.2 20.0 %collective-permute-done.3 = bf16[1,2,1,2,2,32,2048]{6,5,4,3,2,1,0:T(8,128)(2,1)S(1)} collective-permute-done((bf16[1,2,1,2,2,32,2048]{6,5,4,3,2,1,0:T(8,128)(2,1)S(1)}, bf16[1,2,1,2,2,32,2048]{6,5,4,3,2,1,0:T(8,128)(2,1)S(1)}, u32[]{:S(2)}, u32[]{:S(2)}) %collective-permute-start.3) | collective-permute-done | bytes 1048608 | tf_op jit(solution)/shard_map/ppermute | solution.py:96
  104.4 9.9 %collective-permute-done.5 = bf16[2,1,1,2,2,32,2048]{6,5,4,3,2,1,0:T(8,128)(2,1)} collective-permute-done((bf16[2,1,1,2,2,32,2048]{6,5,4,3,2,1,0:T(8,128)(2,1)S(1)}, bf16[2,1,1,2,2,32,2048]{6,5,4,3,2,1,0:T(8,128)(2,1)}, u32[]{:S(2)}, u32[]{:S(2)}) %collective-permute-start.5) | collective-permute-done | bytes 1048608 | tf_op jit(solution)/shard_map/ppermute | solution.py:96
  120.0 5.8 pad_maximum_fusion
  126.7 9.1 collective-permute-done.6
  154.1 13.7 %collective-permute-done.9 = bf16[2,2,1,1,1,128,128]{6,5,4,3,2,1,0:T(8,128)(2,1)S(1)} collective-permute-done((bf16[2,2,1,1,1,128,128]{6,5,4,3,2,1,0:T(8,128)(2,1)S(1)}, bf16[2,2,1,1,1,128,128]{6,5,4,3,2,1,0:T(8,128)(2,1)S(1)}, u32[]{:S(2)}, u32[]{:S(2)}) %collective-permute-start.9) | collective-permute-done | bytes 131104 | tf_op jit(solution)/shard_map/ppermute | solution.py:96
  169.9 27.1 %collective-permute-done.10 = bf16[2,2,1,2,1,128,128]{6,5,4,3,2,1,0:T(8,128)(2,1)S(1)} collective-permute-done((bf16[2,2,1,2,1,128,128]{6,5,4,3,2,1,0:T(8,128)(2,1)S(1)}, bf16[2,2,1,2,1,128,128]{6,5,4,3,2,1,0:T(8,128)(2,1)S(1)}, u32[]{:S(2)}, u32[]{:S(2)}) %collective-permute-start.10) | collective-permute-done | bytes 262176 | tf_op jit(solution)/shard_map/ppermute | solution.py:96
  206.1 10.5 %fusion.118 = f32[128,6144]{1,0:T(8,128)S(1)} fusion(bf16[128,2048]{1,0:T(8,128)(2,1)} %fusion.31, bf16[2048,6144]{1,0:T(8,128)(2,1)} %all-gather.6.cloned.1.call-done.right_ref), kind=kOutput, calls=%fused_computation.377 | convolution fusion | flops 3221225472 | bytes 28835840 | tf_op jit(solution)/shard_map/dot_general | solution.py:590
  234.4 11.9 %copy.152 = bf16[8,2048,256]{1,2,0:T(8,128)(2,1)} copy(bf16[8,2048,256]{2,1,0:T(8,128)(2,1)} %refs_0_.3) | data formatting | bytes 16777216 | tf_op args[10]
  246.2 11.5 %copy.153 = bf16[8,2048,256]{1,2,0:T(8,128)(2,1)} copy(bf16[8,2048,256]{2,1,0:T(8,128)(2,1)} %refs_1_.3) | data formatting | bytes 16777216 | tf_op args[11]
  257.8 11.6 %copy.154 = bf16[8,256,2048]{1,2,0:T(8,128)(2,1)} copy(bf16[8,256,2048]{2,1,0:T(8,128)(2,1)} %refs_2_.3) | data formatting | bytes 16777216 | tf_op args[12]
  275.0 72.9 %all-gather.8.cloned.1.call-done = bf16[4096,2048]{1,0:T(8,128)(2,1)} async-done(((bf16[128,2048]{1,0:T(8,128)(2,1)}), bf16[4096,2048]{1,0:T(8,128)(2,1)}) %all-gather.8.cloned.1.call-update) | async-done | bytes 16777232 | tf_op jit(solution)/shard_map/all_gather | solution.py:549
  347.9 39.1 %experts_forward.2 = (bf16[16,128,2048]{2,1,0:T(8,128)(2,1)}, f32[16,8,128]{2,1,0:T(8,128)}, f32[8,512,512]{2,1,0:T(8,128)}, bf16[8,1024,256]{2,1,0:T(8,128)(2,1)}, bf16[8,32,32,2048]{3,2,1,0:T(8,128)(2,1)}) custom-call(s32[1]{0:T(128)} %bitcast.1._, f32[32,8,128]{2,1,0:T(8,128)} %dynamic-slice_convert_fusion.slots_ref, ...), custom_call_target="tpu_custom_call" | custom-call | flops 85899345920 | bytes 67108864 | tf_op jit(solution)/shard_map/experts_forward/pallas_call | solution.py:424
  388.7 39.2 %experts_forward.3 = (bf16[16,64,2048]{2,1,0:T(8,128)(2,1)}, bf16[16,64,2048]{2,1,0:T(8,128)(2,1)}, f32[16,8,128]{2,1,0:T(8,128)}, f32[8,512,512]{2,1,0:T(8,128)...) custom-call(s32[1]{0:T(128)} %bitcast._, ...), custom_call_target="tpu_custom_call", output_to_operand_aliasing={{4}: (7, {}), {5}: (8, {})} | custom-call | flops 85899345920 | bytes 67108864 | tf_op jit(solution)/shard_map/experts_forward/pallas_call | solution.py:424
  446.7 19.5 %all-gather.10.cloned.1.call-done = bf16[4096,2048]{1,0:T(8,128)(2,1)} async-done(((bf16[128,2048]{1,0:T(8,128)(2,1)}), bf16[4096,2048]{1,0:T(8,128)(2,1)}) %all-gather.10.cloned.1.call-update) | async-done | bytes 16777232 | tf_op jit(solution)/shard_map/all_gather | solution.py:549
  466.3 39.0 %experts_backward.2 = (bf16[16,128,2048]{2,1,0:T(8,128)(2,1)}, f32[16,8,128]{2,1,0:T(8,128)}, bf16[8,1024,256]{2,1,0:T(8,128)(2,1)}, bf16[8,1024,256]{2,1,0:T(8,128)(2,1)}, bf16[8,32,32,2048]{3,2,1,0:T(8,128)(2,1)}) custom-call(s32[1]{0:T(128)} %bitcast.1._, f32[32,8,128]{2,1,0:T(8,128)} %dynamic-slice_convert_fusion.slots_ref, ...), custom_call_target="tpu_custom_call" | custom-call | flops 85899345920 | bytes 67108864 | tf_op jit(solution)/shard_map/experts_backward/pallas_call | solution.py:424
  516.3 39.1 %experts_backward.3 = (bf16[16,32,2048]{2,1,0:T(8,128)(2,1)}, bf16[16,32,2048]{2,1,0:T(8,128)(2,1)}, bf16[16,32,2048]{2,1,0:T(8,128)(2,1)}, bf16[16,32,2048]{2,1...) custom-call(s32[1]{0:T(128)} %bitcast._, ...), custom_call_target="tpu_custom_call", output_to_operand_aliasing={{5}: (8, {}), {6}: (9, {}), {7}: (10, {})} | custom-call | flops 85899345920 | bytes 67108864 | tf_op jit(solution)/shard_map/experts_backward/pallas_call | solution.py:424
  575.8 21.4 %fusion.119 = f32[8,2048,256]{2,1,0:T(8,128)} fusion(bf16[8,1024,2048]{2,1,0:T(8,128)(2,1)} %bitcast.431, bf16[8,1024,256]{2,1,0:T(8,128)(2,1)} %get-tuple-element.192), kind=kOutput, calls=%fused_computation.378 | convolution fusion | flops 8589934592 | bytes 54525952 | tf_op jit(solution)/shard_map/erd,erh->edh/dot_general | solution.py:702
  616.8 19.8 %fusion.120 = f32[8,256,2048]{2,1,0:T(8,128)} fusion(bf16[8,1024,256]{2,1,0:T(8,128)(2,1)} %get-tuple-element.203, bf16[8,1024,2048]{2,1,0:T(8,128)(2,1)} %bitcast.430), kind=kOutput, calls=%fused_computation.379 | convolution fusion | flops 8589934592 | bytes 54525952 | tf_op jit(solution)/shard_map/erh,erd->ehd/dot_general | solution.py:702
  636.5 8.8 collective-permute-done.23
  659.5 21.1 %fusion.121 = f32[8,2048,256]{2,1,0:T(8,128)} fusion(bf16[8,1024,2048]{2,1,0:T(8,128)(2,1)} %bitcast.432, bf16[8,1024,256]{2,1,0:T(8,128)(2,1)} %get-tuple-element.212), kind=kOutput, calls=%fused_computation.380 | convolution fusion | flops 8589934592 | bytes 54525952 | tf_op jit(solution)/shard_map/erd,erh->edh/dot_general | solution.py:702
  688.7 12.1 %collective-permute-done.32 = bf16[64,2048]{1,0:T(8,128)(2,1)S(1)} collective-permute-done((bf16[64,2048]{1,0:T(8,128)(2,1)S(1)}, bf16[64,2048]{1,0:T(8,128)(2,1)S(1)}, u32[]{:S(2)}, u32[]{:S(2)}) %collective-permute-start.32) | collective-permute-done | bytes 262176 | tf_op jit(solution)/shard_map/ppermute | solution.py:96
  700.9 5.8 collective-permute-done.33
  712.6 9.8 %collective-permute-done.39 = f32[64,128]{1,0:T(8,128)S(1)} collective-permute-done((f32[64,128]{1,0:T(8,128)S(1)}, f32[64,128]{1,0:T(8,128)S(1)}, u32[]{:S(2)}, u32[]{:S(2)}) %collective-permute-start.39) | collective-permute-done | bytes 32800 | tf_op jit(solution)/shard_map/ppermute | solution.py:96
  726.3 6.5 fusion.29
  767.2 5.4 collective-permute-done.47
  779.4 13.9 %turned_product.1 = f32[128,2048]{1,0:T(8,128)S(1)} custom-call(bf16[128,6144]{1,0:T(8,128)(2,1)S(1)} %pad_maximum_fusion.4.left_ref, bf16[2048,6144]{1,0:T(8,128)(2,1)} %all-gather.6.cloned.1.call-done.right_ref), custom_call_target="tpu_custom_call" | custom-call | flops 80530636800 | bytes 25165824 | tf_op jit(solution)/shard_map/turned_product/pallas_call | solution.py:224
  817.6 15.4 %collective-permute-done.52 = bf16[2,2,2,64,1024]{4,3,0,1,2:T(8,128)(2,1)} collective-permute-done((bf16[2,2,2,64,1024]{4,3,0,1,2:T(8,128)(2,1)}, bf16[2,2,2,64,1024]{4,3,0,1,2:T(8,128)(2,1)}, u32[]{:S(2)}, u32[]{:S(2)}) %collective-permute-start.52) | collective-permute-done | bytes 1048608 | tf_op jit(solution)/shard_map/ppermute | solution.py:96
  852.6 26.4 %collective-permute-done.55 = bf16[2,2,64,1024]{3,2,1,0:T(8,128)(2,1)S(1)} collective-permute-done((bf16[2,2,64,1024]{3,2,1,0:T(8,128)(2,1)S(1)}, bf16[2,2,64,1024]{3,2,1,0:T(8,128)(2,1)S(1)}, u32[]{:S(2)}, u32[]{:S(2)}) %collective-permute-start.55) | collective-permute-done | bytes 524320 | tf_op jit(solution)/shard_map/ppermute | solution.py:96
  892.0 15.0 %collective-permute-done.60 = bf16[2,2,64,1024]{3,2,1,0:T(8,128)(2,1)S(1)} collective-permute-done((bf16[2,2,64,1024]{3,2,1,0:T(8,128)(2,1)S(1)}, bf16[2,2,64,1024]{3,2,1,0:T(8,128)(2,1)S(1)}, u32[]{:S(2)}, u32[]{:S(2)}) %collective-permute-start.60) | collective-permute-done | bytes 524320 | tf_op jit(solution)/shard_map/ppermute | solution.py:96
  (584 shorter events, 289.3 us)
Async XLA Ops:
  7.2 198.9 %all-gather.6.cloned.1.call-start = ((), (), s32[]{:S(2)}) async-start(), calls=%async_computation | async-start | bytes 25952256 | tf_op jit(solution)/shard_map/all_gather | solution.py:549
  9.3 338.6 %all-gather.8.cloned.1.call-start = ((), (), s32[]{:S(2)}) async-start(), calls=%async_computation.1 | async-start | bytes 17301504 | tf_op jit(solution)/shard_map/all_gather | solution.py:549
  25.4 28.8 %collective-permute-start.1 = (bf16[1,1,1,2,1,64,2048]{6,5,4,3,2,1,0:T(8,128)(2,1)S(1)}, bf16[1,1,1,2,1,64,2048]{6,5,4,3,2,1,0:T(8,128)(2,1)S(1)}, u32[]{:S(2)}, u32[]{:S(2)}) collective-permute-start(bf16[1,1,1,2,1,64,2048]{6,5,4,3,2,1,0:T(8,128)(2,1)S(1)} %constant_dynamic-update-slice_fusion.22), channel_id=1, source_target_pairs={{0,1},{1,0},{2,3},{3,2},{4,5},{5,4},{6,7},{7,6},{8,9},{9,8},{10,11... | collective-permute-start | bytes 1572872 | tf_op jit(solution)/shard_map/ppermute | solution.py:96
  57.0 25.2 %collective-permute-start.4 = (bf16[1,1,1,2,2,32,2048]{6,5,4,3,2,1,0:T(8,128)(2,1)}, bf16[1,1,1,2,2,32,2048]{6,5,4,3,2,1,0:T(8,128)(2,1)}, u32[]{:S(2)}, u32[]{:S(2)}) collective-permute-start(bf16[1,1,1,2,2,32,2048]{6,5,4,3,2,1,0:T(8,128)(2,1)} %get-tuple-element.335), channel_id=1, source_target_pairs={{0,16},{4,20},{8,24},{12,28},{16,0},{20,4},{24,8},{28,12},{1,17},{... | collective-permute-start | bytes 1572872 | tf_op jit(solution)/shard_map/ppermute | solution.py:96
  77.4 26.9 %collective-permute-start.3 = (bf16[1,2,1,2,2,32,2048]{6,5,4,3,2,1,0:T(8,128)(2,1)S(1)}, bf16[1,2,1,2,2,32,2048]{6,5,4,3,2,1,0:T(8,128)(2,1)S(1)}, u32[]{:S(2)}, u32[]{:S(2)}) collective-permute-start(bf16[1,2,1,2,2,32,2048]{6,5,4,3,2,1,0:T(8,128)(2,1)S(1)} %constant_dynamic-update-slice_fusion.18), channel_id=1, source_target_pairs={{0,16},{4,20},{8,24},{12,28},{16,0},{20,4},{24,8},{28,12},{1,17},{... | collective-permute-start | bytes 3145736 | tf_op jit(solution)/shard_map/ppermute | solution.py:96
  83.4 30.9 %collective-permute-start.5 = (bf16[2,1,1,2,2,32,2048]{6,5,4,3,2,1,0:T(8,128)(2,1)S(1)}, bf16[2,1,1,2,2,32,2048]{6,5,4,3,2,1,0:T(8,128)(2,1)}, u32[]{:S(2)}, u32[]{:S(2)}) collective-permute-start(bf16[2,1,1,2,2,32,2048]{6,5,4,3,2,1,0:T(8,128)(2,1)S(1)} %constant_dynamic-update-slice_fusion.14), channel_id=1, source_target_pairs={{0,8},{4,12},{8,0},{12,4},{16,24},{20,28},{24,16},{28,20},{1,9},{5... | collective-permute-start | bytes 3145736 | tf_op jit(solution)/shard_map/ppermute | solution.py:96
  167.9 29.1 %collective-permute-start.10 = (bf16[2,2,1,2,1,128,128]{6,5,4,3,2,1,0:T(8,128)(2,1)S(1)}, bf16[2,2,1,2,1,128,128]{6,5,4,3,2,1,0:T(8,128)(2,1)S(1)}, u32[]{:S(2)}, u32[]{:S(2)}) collective-permute-start(bf16[2,2,1,2,1,128,128]{6,5,4,3,2,1,0:T(8,128)(2,1)S(1)} %constant_dynamic-update-slice_fusion.4), channel_id=1, source_target_pairs={{0,1},{1,0},{2,3},{3,2},{4,5},{5,4},{6,7},{7,6},{8,9},{9,8},{10,11... | collective-permute-start | bytes 786440 | tf_op jit(solution)/shard_map/ppermute | solution.py:96
  233.5 232.8 %all-gather.10.cloned.1.call-start = ((), (), s32[]{:S(2)}) async-start(), calls=%async_computation.2 | async-start | bytes 17301504 | tf_op jit(solution)/shard_map/all_gather | solution.py:549
  274.4 238.2 %collective-permute-start.15 = (bf16[128,2048]{1,0:T(8,128)(2,1)}, bf16[128,2048]{1,0:T(8,128)(2,1)}, u32[]{:S(2)}, u32[]{:S(2)}) collective-permute-start(bf16[128,2048]{1,0:T(8,128)(2,1)} %pad_maximum_fusion.15), channel_id=1, source_target_pairs={{0,4},{4,0},{8,12},{12,8},{16,20},{20,16},{24,28},{28,24},{1,5},{5... | collective-permute-start | bytes 1572872 | tf_op jit(solution)/shard_map/ppermute | solution.py:96
  387.0 40.9 %collective-permute-start.12 = (bf16[16,128,2048]{2,1,0:T(8,128)(2,1)}, bf16[16,128,2048]{2,1,0:T(8,128)(2,1)}, u32[]{:S(2)}, u32[]{:S(2)}) collective-permute-start(bf16[16,128,2048]{2,1,0:T(8,128)(2,1)} %get-tuple-element.152), channel_id=1, source_target_pairs={{0,4},{4,0},{8,12},{12,8},{16,20},{20,16},{24,28},{28,24},{1,5},{5... | collective-permute-start | bytes 25165832 | tf_op jit(solution)/shard_map/ppermute | solution.py:96
  437.8 67.5 %collective-permute-start.14 = (bf16[2,2,2,64,2048]{4,3,1,2,0:T(8,128)(2,1)S(1)}, bf16[2,2,2,64,2048]{4,3,1,2,0:T(8,128)(2,1)}, u32[]{:S(2)}, u32[]{:S(2)}) collective-permute-start(bf16[2,2,2,64,2048]{4,3,1,2,0:T(8,128)(2,1)S(1)} %fusion.4), channel_id=1, source_target_pairs={{0,8},{4,12},{8,0},{12,4},{16,24},{20,28},{24,16},{28,20},{1,9},{5... | collective-permute-start | bytes 6291464 | tf_op jit(solution)/shard_map/ppermute | solution.py:96
  446.0 63.7 %collective-permute-start.13 = (bf16[2,2,2,64,2048]{4,3,1,2,0:T(8,128)(2,1)}, bf16[2,2,2,64,2048]{4,3,1,2,0:T(8,128)(2,1)}, u32[]{:S(2)}, u32[]{:S(2)}) collective-permute-start(bf16[2,2,2,64,2048]{4,3,1,2,0:T(8,128)(2,1)} %fusion.3), channel_id=1, source_target_pairs={{0,16},{4,20},{8,24},{12,28},{16,0},{20,4},{24,8},{28,12},{1,17},{... | collective-permute-start | bytes 6291464 | tf_op jit(solution)/shard_map/ppermute | solution.py:96
  513.8 41.6 %collective-permute-start.16 = (bf16[2,2,64,2048]{3,2,0,1:T(8,128)(2,1)}, bf16[2,2,64,2048]{3,2,0,1:T(8,128)(2,1)}, u32[]{:S(2)}, u32[]{:S(2)}) collective-permute-start(bf16[2,2,64,2048]{3,2,0,1:T(8,128)(2,1)} %dynamic-slice_bitcast_fusion.4), channel_id=1, source_target_pairs={{0,8},{4,12},{8,0},{12,4},{16,24},{20,28},{24,16},{28,20},{1,9},{5... | collective-permute-start | bytes 3145736 | tf_op jit(solution)/shard_map/ppermute | solution.py:96
  514.3 43.1 %collective-permute-start.17 = (bf16[2,2,64,2048]{3,2,0,1:T(8,128)(2,1)S(1)}, bf16[2,2,64,2048]{3,2,0,1:T(8,128)(2,1)}, u32[]{:S(2)}, u32[]{:S(2)}) collective-permute-start(bf16[2,2,64,2048]{3,2,0,1:T(8,128)(2,1)S(1)} %dynamic-slice_bitcast_fusion.3), channel_id=1, source_target_pairs={{0,16},{4,20},{8,24},{12,28},{16,0},{20,4},{24,8},{28,12},{1,17},{... | collective-permute-start | bytes 3145736 | tf_op jit(solution)/shard_map/ppermute | solution.py:96
  516.3 43.0 %collective-permute-start.18 = (bf16[16,128,2048]{2,1,0:T(8,128)(2,1)}, bf16[16,128,2048]{2,1,0:T(8,128)(2,1)}, u32[]{:S(2)}, u32[]{:S(2)}) collective-permute-start(bf16[16,128,2048]{2,1,0:T(8,128)(2,1)} %get-tuple-element.185), channel_id=1, source_target_pairs={{0,4},{4,0},{8,12},{12,8},{16,20},{20,16},{24,28},{28,24},{1,5},{5... | collective-permute-start | bytes 25165832 | tf_op jit(solution)/shard_map/ppermute | solution.py:96
  559.9 37.8 %collective-permute-start.22 = (f32[2,2,2,2,8,128]{5,4,3,2,1,0:T(8,128)S(1)}, f32[2,2,2,2,8,128]{5,4,3,2,1,0:T(8,128)S(1)}, u32[]{:S(2)}, u32[]{:S(2)}) collective-permute-start(f32[2,2,2,2,8,128]{5,4,3,2,1,0:T(8,128)S(1)} %dynamic-slice_bitcast_fusion.20), channel_id=1, source_target_pairs={{0,1},{1,0},{2,3},{3,2},{4,5},{5,4},{6,7},{7,6},{8,9},{9,8},{10,11... | collective-permute-start | bytes 196616 | tf_op jit(solution)/shard_map/ppermute | solution.py:96
  563.5 34.2 %collective-permute-start.21 = (bf16[2,128,2048]{2,1,0:T(8,128)(2,1)}, bf16[2,128,2048]{2,1,0:T(8,128)(2,1)}, u32[]{:S(2)}, u32[]{:S(2)}) collective-permute-start(bf16[2,128,2048]{2,1,0:T(8,128)(2,1)} %dynamic-slice_bitcast_fusion.2), channel_id=1, source_target_pairs={{0,1},{1,0},{2,3},{3,2},{4,5},{5,4},{6,7},{7,6},{8,9},{9,8},{10,11... | collective-permute-start | bytes 3145736 | tf_op jit(solution)/shard_map/ppermute | solution.py:96
  570.7 29.5 %collective-permute-start.20 = (bf16[2,2,2,32,2048]{4,3,1,2,0:T(8,128)(2,1)}, bf16[2,2,2,32,2048]{4,3,1,2,0:T(8,128)(2,1)}, u32[]{:S(2)}, u32[]{:S(2)}) collective-permute-start(bf16[2,2,2,32,2048]{4,3,1,2,0:T(8,128)(2,1)} %fusion.39), channel_id=1, source_target_pairs={{0,8},{4,12},{8,0},{12,4},{16,24},{20,28},{24,16},{28,20},{1,9},{5... | collective-permute-start | bytes 3145736 | tf_op jit(solution)/shard_map/ppermute | solution.py:96
  575.3 27.1 %collective-permute-start.19 = (bf16[2,2,2,32,2048]{4,3,1,2,0:T(8,128)(2,1)}, bf16[2,2,2,32,2048]{4,3,1,2,0:T(8,128)(2,1)}, u32[]{:S(2)}, u32[]{:S(2)}) collective-permute-start(bf16[2,2,2,32,2048]{4,3,1,2,0:T(8,128)(2,1)} %fusion.38), channel_id=1, source_target_pairs={{0,16},{4,20},{8,24},{12,28},{16,0},{20,4},{24,8},{28,12},{1,17},{... | collective-permute-start | bytes 3145736 | tf_op jit(solution)/shard_map/ppermute | solution.py:96
  605.4 43.2 %collective-permute-start.27 = (bf16[128,2048]{1,0:T(8,128)(2,1)}, bf16[128,2048]{1,0:T(8,128)(2,1)}, u32[]{:S(2)}, u32[]{:S(2)}) collective-permute-start(bf16[128,2048]{1,0:T(8,128)(2,1)} %dynamic-slice_bitcast_fusion.11), channel_id=1, source_target_pairs={{0,2},{1,3},{2,0},{3,1},{4,6},{5,7},{6,4},{7,5},{8,10},{9,11},{10,... | collective-permute-start | bytes 1572872 | tf_op jit(solution)/shard_map/ppermute | solution.py:96
  609.7 40.3 %collective-permute-start.26 = (bf16[2,2,2,32,2048]{4,3,1,2,0:T(8,128)(2,1)}, bf16[2,2,2,32,2048]{4,3,1,2,0:T(8,128)(2,1)}, u32[]{:S(2)}, u32[]{:S(2)}) collective-permute-start(bf16[2,2,2,32,2048]{4,3,1,2,0:T(8,128)(2,1)} %fusion.41), channel_id=1, source_target_pairs={{0,8},{4,12},{8,0},{12,4},{16,24},{20,28},{24,16},{28,20},{1,9},{5... | collective-permute-start | bytes 3145736 | tf_op jit(solution)/shard_map/ppermute | solution.py:96
  611.5 40.9 %collective-permute-start.25 = (bf16[2,2,2,32,2048]{4,3,1,2,0:T(8,128)(2,1)}, bf16[2,2,2,32,2048]{4,3,1,2,0:T(8,128)(2,1)}, u32[]{:S(2)}, u32[]{:S(2)}) collective-permute-start(bf16[2,2,2,32,2048]{4,3,1,2,0:T(8,128)(2,1)} %fusion.40), channel_id=1, source_target_pairs={{0,16},{4,20},{8,24},{12,28},{16,0},{20,4},{24,8},{28,12},{1,17},{... | collective-permute-start | bytes 3145736 | tf_op jit(solution)/shard_map/ppermute | solution.py:96
  614.0 31.4 %collective-permute-start.23 = (bf16[2,2,32,2048]{3,2,0,1:T(8,128)(2,1)}, bf16[2,2,32,2048]{3,2,0,1:T(8,128)(2,1)}, u32[]{:S(2)}, u32[]{:S(2)}) collective-permute-start(bf16[2,2,32,2048]{3,2,0,1:T(8,128)(2,1)} %dynamic-slice_bitcast_fusion.13), channel_id=1, source_target_pairs={{0,8},{4,12},{8,0},{12,4},{16,24},{20,28},{24,16},{28,20},{1,9},{5... | collective-permute-start | bytes 1572872 | tf_op jit(solution)/shard_map/ppermute | solution.py:96
  616.2 31.0 %collective-permute-start.24 = (bf16[2,2,32,2048]{3,2,0,1:T(8,128)(2,1)}, bf16[2,2,32,2048]{3,2,0,1:T(8,128)(2,1)}, u32[]{:S(2)}, u32[]{:S(2)}) collective-permute-start(bf16[2,2,32,2048]{3,2,0,1:T(8,128)(2,1)} %dynamic-slice_bitcast_fusion.12), channel_id=1, source_target_pairs={{0,16},{4,20},{8,24},{12,28},{16,0},{20,4},{24,8},{28,12},{1,17},{... | collective-permute-start | bytes 1572872 | tf_op jit(solution)/shard_map/ppermute | solution.py:96
  654.2 27.3 %collective-permute-start.31 = (f32[2,2,2,8,128]{4,3,2,1,0:T(8,128)S(1)}, f32[2,2,2,8,128]{4,3,2,1,0:T(8,128)S(1)}, u32[]{:S(2)}, u32[]{:S(2)}) collective-permute-start(f32[2,2,2,8,128]{4,3,2,1,0:T(8,128)S(1)} %dynamic-slice_bitcast_fusion.25), channel_id=1, source_target_pairs={{0,2},{1,3},{2,0},{3,1},{4,6},{5,7},{6,4},{7,5},{8,10},{9,11},{10,... | collective-permute-start | bytes 98312 | tf_op jit(solution)/shard_map/ppermute | solution.py:96
  654.7 26.9 %collective-permute-start.29 = (bf16[2,2,32,2048]{3,2,0,1:T(8,128)(2,1)S(1)}, bf16[2,2,32,2048]{3,2,0,1:T(8,128)(2,1)S(1)}, u32[]{:S(2)}, u32[]{:S(2)}) collective-permute-start(bf16[2,2,32,2048]{3,2,0,1:T(8,128)(2,1)S(1)} %dynamic-slice_bitcast_fusion.9), channel_id=1, source_target_pairs={{0,8},{4,12},{8,0},{12,4},{16,24},{20,28},{24,16},{28,20},{1,9},{5... | collective-permute-start | bytes 1572872 | tf_op jit(solution)/shard_map/ppermute | solution.py:96
  656.1 25.7 %collective-permute-start.30 = (bf16[2,2,32,2048]{3,2,0,1:T(8,128)(2,1)S(1)}, bf16[2,2,32,2048]{3,2,0,1:T(8,128)(2,1)S(1)}, u32[]{:S(2)}, u32[]{:S(2)}) collective-permute-start(bf16[2,2,32,2048]{3,2,0,1:T(8,128)(2,1)S(1)} %dynamic-slice_bitcast_fusion.8), channel_id=1, source_target_pairs={{0,16},{4,20},{8,24},{12,28},{16,0},{20,4},{24,8},{28,12},{1,17},{... | collective-permute-start | bytes 1572872 | tf_op jit(solution)/shard_map/ppermute | solution.py:96
  777.1 25.6 %collective-permute-start.49 = (bf16[2,2,2,64,1024]{4,3,0,1,2:T(8,128)(2,1)S(1)}, bf16[2,2,2,64,1024]{4,3,0,1,2:T(8,128)(2,1)S(1)}, u32[]{:S(2)}, u32[]{:S(2)}) collective-permute-start(bf16[2,2,2,64,1024]{4,3,0,1,2:T(8,128)(2,1)S(1)} %copy_bitcast_fusion.3), channel_id=1, source_target_pairs={{0,16},{4,20},{8,24},{12,28},{16,0},{20,4},{24,8},{28,12},{1,17},{... | collective-permute-start | bytes 3145736 | tf_op jit(solution)/shard_map/ppermute | solution.py:96
  778.1 25.1 %collective-permute-start.50 = (bf16[2,2,2,64,1024]{4,3,0,1,2:T(8,128)(2,1)S(1)}, bf16[2,2,2,64,1024]{4,3,0,1,2:T(8,128)(2,1)S(1)}, u32[]{:S(2)}, u32[]{:S(2)}) collective-permute-start(bf16[2,2,2,64,1024]{4,3,0,1,2:T(8,128)(2,1)S(1)} %copy_bitcast_fusion.2), channel_id=1, source_target_pairs={{0,8},{4,12},{8,0},{12,4},{16,24},{20,28},{24,16},{28,20},{1,9},{5... | collective-permute-start | bytes 3145736 | tf_op jit(solution)/shard_map/ppermute | solution.py:96
  816.9 25.9 %collective-permute-start.51 = (bf16[2,2,2,64,1024]{4,3,1,0,2:T(8,128)(2,1)}, bf16[2,2,2,64,1024]{4,3,1,0,2:T(8,128)(2,1)}, u32[]{:S(2)}, u32[]{:S(2)}) collective-permute-start(bf16[2,2,2,64,1024]{4,3,1,0,2:T(8,128)(2,1)} %dynamic-slice_bitcast_fusion.1), channel_id=1, source_target_pairs={{0,1},{1,0},{2,3},{3,2},{4,5},{5,4},{6,7},{7,6},{8,9},{9,8},{10,11... | collective-permute-start | bytes 3145736 | tf_op jit(solution)/shard_map/ppermute | solution.py:96
  845.2 35.8 %collective-permute-start.56 = (bf16[2,2,2,64,1024]{4,3,1,0,2:T(8,128)(2,1)S(1)}, bf16[2,2,2,64,1024]{4,3,1,0,2:T(8,128)(2,1)S(1)}, u32[]{:S(2)}, u32[]{:S(2)}) collective-permute-start(bf16[2,2,2,64,1024]{4,3,1,0,2:T(8,128)(2,1)S(1)} %dynamic-slice_bitcast_fusion), channel_id=1, source_target_pairs={{0,1},{1,0},{2,3},{3,2},{4,5},{5,4},{6,7},{7,6},{8,9},{9,8},{10,11... | collective-permute-start | bytes 3145736 | tf_op jit(solution)/shard_map/ppermute | solution.py:96
  845.6 33.3 %collective-permute-start.55 = (bf16[2,2,64,1024]{3,2,1,0:T(8,128)(2,1)S(1)}, bf16[2,2,64,1024]{3,2,1,0:T(8,128)(2,1)S(1)}, u32[]{:S(2)}, u32[]{:S(2)}) collective-permute-start(bf16[2,2,64,1024]{3,2,1,0:T(8,128)(2,1)S(1)} %dynamic-slice_bitcast_fusion.6), channel_id=1, source_target_pairs={{0,2},{1,3},{2,0},{3,1},{4,6},{5,7},{6,4},{7,5},{8,10},{9,11},{10,... | collective-permute-start | bytes 1572872 | tf_op jit(solution)/shard_map/ppermute | solution.py:96
  (146 other events, 1357.5 us)
Sparse Core Ops, SparseCore 0:
  11.5 194.5 all-gather.5
  233.6 114.3 all-gather.7
  350.9 115.2 all-gather.9

commit v4 on v3

--- a/solution.py
+++ b/solution.py
@@ -122,20 +122,27 @@
         values = self.gather_axis(jnp.concatenate(halves, axis=-2), "c")
         return values.reshape(-1, values.shape[-1])
 
-    def reduce_axis(self, values, axis, axes):
+    def cut(self, values, axis, axes, steps):
         dim, count, own = axes.index(axis), self.size[axis], self.place(axis)
-        values = values if isinstance(values, (list, tuple)) else [values]
-        kind = values[0].dtype
-
-        def part(step):
-            return sum(
+        return [
+            sum(
                 lax.dynamic_index_in_dim(v, (own - step) % count, dim, keepdims=False).astype(wide)
                 for v in values
             )
-
-        total = part(0)
-        for step in range(1, count):
-            total = total + self.shift(part(step).astype(kind), axis, -step).astype(wide)
+            for step in steps
+        ]
+
+    def reduce_axis(self, values, axis, axes, cuts=None):
+        values = list(values) if isinstance(values, (list, tuple)) else [values]
+        kind = values[0].dtype
+        if cuts is None:
+            cuts = self.cut(values, axis, axes, range(1, self.size[axis]))
+        got = [self.shift(cut.astype(kind), axis, -1 - i) for i, cut in enumerate(cuts)]
+        if len(values) > 1:
+            values = after(tuple(values), *got)
+        (total,) = self.cut(values, axis, axes, [0])
+        for part in got:
+            total = total + part.astype(wide)
         return total.astype(kind)
 
     def reduce_scatter(self, values, order, axes=axes):
@@ -168,19 +175,26 @@
             [chosen((own - j) % count, got) for j in range(count)], axis=1
         ).astype(wide)
 
-    def reduce_first(self, pair):
-        return [self.reduce_axis(v, axis, "yxuw") for v, axis in zip(pair, "yx", strict=True)]
-
-    def alike(self, pair):
-        return jnp.stack(pair) if self.size["y"] == self.size["x"] else pair
-
-    def reduce_both(self, pair, axis):
-        left = "uw" if axis == "w" else "u"
-        if isinstance(pair, list):
-            return [
-                self.reduce_axis(v, axis, line + left) for v, line in zip(pair, "xy", strict=True)
+    def first_cuts(self, pair):
+        return [
+            [
+                cut.astype(low)
+                for cut in self.cut(v, axis, "yxuw", range(1, self.size[axis]))
             ]
-        return self.reduce_axis(pair, axis, "pl" + left)
+            for v, axis in zip(pair, "yx", strict=True)
+        ]
+
+    def reduce_first(self, pair, cuts=(None, None)):
+        return [
+            self.reduce_axis(v, axis, "yxuw", cut)
+            for v, axis, cut in zip(pair, "yx", cuts, strict=True)
+        ]
+
+    def reduce_z(self, pair, turn, lines=("", "")):
+        return [
+            self.reduce_axis(v, axes[turn], line + (axes[1] if turn else "uw"))
+            for v, axes, line in zip(pair, ("wu", "uw"), lines, strict=True)
+        ]
 
     def rows_of_both(self, pair):
         return [self.rows_from_line(v, line) for v, line in zip(pair, "xy", strict=True)]
@@ -189,7 +203,7 @@
         pair = [
             self.reduce_axis(v, axis, axis + "uw") for v, axis in zip(pair, "xy", strict=True)
         ]
-        return jnp.concatenate(pair, axis=join + 2)
+        return pair if join is None else jnp.concatenate(pair, axis=join + 2)
 
     def chips(self):
         return tuple(self.size[axis] for axis in "yxuw")
@@ -348,7 +362,8 @@
     x_refs, refs = refs[:parts], refs[parts:]
     grads_ref, dgate_ref, dup_ref, rows_hbm = refs[:4]
     joint_w, down_w, rows_v, out_v, gate_rows, grad_rows, w_sems, row_sems = refs[4:]
-    chunk, tokens, width = g_ref.shape
+    chunk, _, width = g_ref.shape
+    tokens = slots_ref.shape[2]
     experts, _, hidden = down_w.shape
     depth = chunk * CAP
     targets = (
@@ -641,24 +656,24 @@
     chips = grid.chips()
 
     def token_sums(away, kept):
-        share = tokens_dev // len(kept)
-        away = away.reshape(chips + away.shape[1:])
         return [
-            (part.reshape(chips + part.shape[1:]), away[..., i * share : (i + 1) * share, :])
-            for i, part in enumerate(kept)
+            [half.reshape(chips + half.shape[1:]) for half in pair]
+            for pair in zip(away, kept, strict=True)
         ]
 
     groups = blocks // 2 // grid.tp
     forward_ins = (slots_here, router_turned, normed_all, (w_gate, w_up, w_down))
-    y_ahead, gates_ahead, pre_ahead, *given = experts.forward(
-        0, groups, 0, 1, turns[0], *forward_ins, []
+    *y_ahead, gates_ahead, pre_ahead, inner_scaled, rows_in = experts.forward(
+        0, groups, 0, 2, turns[0], *forward_ins, []
     )
     *y_own, gates_own, pre_own, inner_scaled, rows_in = experts.forward(
-        0, groups, 1, 2, turns[1], *forward_ins, given
-    )
-    y_away = grid.shift(y_ahead, "c", 1)
+        0, groups, 1, 2, turns[1], *forward_ins, [inner_scaled, rows_in]
+    )
+    y_away = [grid.shift(half, "c", 1) for half in y_ahead]
     y_own, y_away, gates_own, slots_here = together(y_own, y_away, gates_own, slots_here)
     expert_sums = token_sums(y_away, y_own)
+    cuts = grid.first_cuts(expert_sums)
+    cuts, upstream_all, slots_here = together(cuts, upstream_all, slots_here)
 
     def backward(first, count, turn, parts, gates, pre, given):
         return experts.backward(
@@ -684,14 +699,14 @@
         jnp.concatenate(cut, axis=1)
         for cut in zip(by_core(normed_attn), by_core(attended), strict=True)
     )
-    ahead = backward(0, groups, 0, 1, gates_ahead, pre_ahead, [])
-    expert_sums = grid.reduce_first(expert_sums)
+    ahead = backward(0, groups, 0, 2, gates_ahead, pre_ahead, [])
+    expert_sums = grid.reduce_first(expert_sums, cuts)
     pair_rows = [kept, grid.shift(away, "c", 1)]
-    (x_ahead, gate_grads_ahead, *given), expert_sums, slots_here, pair_rows = together(
+    (*x_ahead, gate_grads_ahead, dgate, dup, taken), expert_sums, slots_here, pair_rows = together(
         ahead, expert_sums, slots_here, pair_rows
     )
-    x_away = grid.shift(x_ahead, "c", 1)
-    own = backward(0, groups, 1, 4, gates_own, pre_own, given)
+    x_away = [grid.shift(half, "c", 1) for half in x_ahead]
+    own = backward(0, groups, 1, 2, gates_own, pre_own, [dgate, dup, taken])
     expert_sum = grid.reduce_second(expert_sums, 0)
     own, expert_sum, x_away = together(own, expert_sum, x_away)
     *x_own, gate_grads_own, grad_gate_part, grad_up_part, rows_up = own
@@ -706,22 +721,16 @@
     gate_grads = jnp.where(core == 0, gate_grads, gate_grads[::-1])
     gate_grads = gate_grads.reshape((2,) + chips + (local_experts, tokens_dev))
     acc_gate = weight_grad("erd,erh->edh", rows_in, grad_gate_part)
-    early = grid.reduce_first(sums[:2])
+    acc_down = weight_grad("erh,erd->ehd", inner_scaled, rows_up)
+    sums = grid.reduce_first(sums)
     expert_sum = grid.reduce_axis(expert_sum, "w", "uw")
     gate_grads = grid.reduce_axis(gate_grads, "w", "cyxuw")
-    early, late, acc_gate, expert_sum, rows_in, rows_up, gate_grads = together(
-        early, sums[2:], acc_gate, expert_sum, rows_in, rows_up, gate_grads
-    )
-    acc_down = weight_grad("erh,erd->ehd", inner_scaled, rows_up)
-    early = grid.reduce_second(early, 0)
-    late = grid.reduce_first(late)
+    sums, acc_gate, acc_down, expert_sum, rows_in, gate_grads = together(
+        sums, acc_gate, acc_down, expert_sum, rows_in, gate_grads
+    )
+    acc_up = weight_grad("erd,erh->edh", rows_in, grad_up_part)
+    sums = grid.reduce_second(sums, None)
     expert_sum = grid.reduce_axis(expert_sum, "u", "u")
-    early, late, acc_down, rows_in, expert_sum, gate_grads = together(
-        early, late, acc_down, rows_in, expert_sum, gate_grads
-    )
-    acc_up = weight_grad("erd,erh->edh", rows_in, grad_up_part)
-    early = grid.reduce_axis(early, "w", "uw")
-    late = grid.reduce_second(late, 0)
     gate_grads = grid.reduce_axis(gate_grads, "u", "cyxu")
     gate_grads = lax.dynamic_update_slice_in_dim(
         jnp.zeros(gate_grads.shape[:3] + (expert_count, tokens_dev), wide),
@@ -729,26 +738,23 @@
         first_expert,
         3,
     )
+    sums, acc_up, expert_sum, gate_grads, pair_rows = together(
+        sums, acc_up, expert_sum, gate_grads, pair_rows
+    )
     block_out = (mixed + expert_sum.astype(wide)).astype(low)
-    early, late, acc_up, gate_grads, pair_rows = together(
-        early, late, acc_up, gate_grads, pair_rows
-    )
-    early = grid.reduce_axis(early, "u", "u")
-    late = grid.reduce_axis(late, "w", "uw")
+    sums = grid.reduce_z(sums, 0)
     gate_grads = grid.reduce_axis(gate_grads, "c", "cyx")
     pair_rows = jnp.concatenate(pair_rows, axis=0)
-    normed_rows, attended_rows = jnp.split(pair_rows, 2, axis=1)
-    y_rows = grid.from_line(normed_rows, "y")
-    attended_rows = grid.from_line(attended_rows, "x")
-    early, late, gate_grads, y_rows, attended_rows, normed_rows = together(
-        early, late, gate_grads, y_rows, attended_rows, normed_rows
-    )
-    late = grid.reduce_axis(late, "u", "u")
-    x_rows = grid.from_line(normed_rows, "x")
+    half = model_width // 2
+    y_rows = grid.from_line(pair_rows[:, :half], "y")
+    x_rows = grid.from_line(pair_rows, "x")
+    sums, gate_grads, y_rows, x_rows = together(sums, gate_grads, y_rows, x_rows)
+    back_sum = jnp.concatenate(grid.reduce_z(sums, 1), axis=0)
     grad_probs = grid.reduce_scatter(gate_grads, "yx", "yx").T
-    early, late, grad_probs, x_rows = together(early, late, grad_probs, x_rows)
+    back_sum, grad_probs = together(back_sum, grad_probs)
+    y_rows, x_rows = jnp.concatenate(y_rows, axis=0), jnp.concatenate(x_rows, axis=0)
     back_sum, block_out, acc_gate, acc_up, acc_down = together(
-        jnp.concatenate([early, late], axis=0), block_out, acc_gate, acc_up, acc_down
+        back_sum, block_out, acc_gate, acc_up, acc_down
     )
 
     upstream = grad_out.astype(wide)
@@ -757,9 +763,6 @@
     )
     grad_ffn_normed = back_sum.astype(wide) + jnp.dot(
         grad_logits, router_full.astype(wide).T, precision=lax.Precision.HIGHEST
-    )
-    grad_router_local = jnp.dot(
-        normed_ffn.astype(wide).T, grad_logits, precision=lax.Precision.HIGHEST
     )
     grad_ffn_gain = jnp.sum(grad_ffn_normed * unit_ffn, axis=0)
     grad_mixed = upstream + rms_back(grad_ffn_normed, unit_ffn, ffn_gain, scale_ffn)
@@ -803,8 +806,8 @@
         return total.astype(low).reshape(chips + (weight_rows, -1))
 
     first = [
-        outer(jnp.concatenate(attended_rows, axis=0), output_columns),
-        outer(jnp.concatenate(y_rows, axis=0), value_columns),
+        outer(x_rows[:, half:], output_columns),
+        outer(y_rows, value_columns),
     ]
     second = [
         grid.columns_from_line(grad_query_raw, "x"),
@@ -812,13 +815,18 @@
     ]
     grads = jnp.concatenate([grad_query_raw, grad_key_raw, grad_value_rows], axis=1)
     first, second, grads = together(first, second, grads)
-    first = grid.alike(grid.reduce_first(first))
+    first = grid.reduce_first(first)
     second = [
-        outer(jnp.concatenate(x_rows, axis=0), second[0]),
-        outer(jnp.concatenate(y_rows, axis=0), second[1]),
+        outer(x_rows[:, :half], second[0]),
+        outer(y_rows, second[1]),
     ]
     grad_attn_normed = turned_product(grads, projections)
-    first, second, grad_attn_normed = together(first, second, grad_attn_normed)
+    first, second, grad_attn_normed, grad_logits = together(
+        first, second, grad_attn_normed, grad_logits
+    )
+    grad_router_local = jnp.dot(
+        normed_ffn.astype(wide).T, grad_logits, precision=lax.Precision.HIGHEST
+    )
     grad_attn_gain = jnp.sum(grad_attn_normed * unit_attn, axis=0)
     grad_input = grad_mixed + rms_back(grad_attn_normed, unit_attn, attn_gain, scale_attn)
     gain_sums = jnp.stack(
@@ -827,16 +835,15 @@
     small_sums = jnp.concatenate([grad_router_local, gain_sums], axis=1).reshape(
         grid.shape + (weight_rows, expert_count + gain_sums.shape[1])
     )
-    first = grid.reduce_both(first, "w")
-    second = grid.alike(grid.reduce_first(second))
-    small_sums = grid.reduce_scatter(small_sums, "c")
+    first = grid.reduce_z(first, 0, "xy")
+    second = grid.reduce_first(second)
     first, second, small_sums = together(first, second, small_sums)
-    first = grid.reduce_both(first, "u")
-    second = grid.reduce_both(second, "w")
-    small_sums = grid.reduce_scatter(small_sums, "y", "yxuw")
+    first = grid.reduce_z(first, 1, "xy")
+    second = grid.reduce_z(second, 0, "xy")
+    small_sums = grid.reduce_scatter(small_sums, "cy")
     first, second, small_sums = together(first, second, small_sums)
     grad_output, grad_value = grid.rows_of_both(first)
-    second = grid.reduce_both(second, "u")
+    second = grid.reduce_z(second, 1, "xy")
     small_sums = grid.reduce_scatter(small_sums, "x", "xuw")
     grad_output, grad_value, second, small_sums = together(
         grad_output, grad_value, second, small_sums

time: 934 us -> 908 us (0.972)
  local copies, waits for them, and re-layouts: 110 us -> 81.2 us
    ppermute x67 -> x68, waiting for transfers between devices: 276 us -> 270 us  [shift(): return lax.ppermute(values, 'tp' if axis in 'uwz' else 'ep', pairs)]
    unnamed x235 -> x214, local copies, waits for them, and re-layouts: 49.6 us -> 43.7 us
    convert_element_type x22 -> x26, other arithmetic: 28.3 us -> 30.2 us  [reduce_axis(): return total.astype(kind)]
    ppermute x67 -> x68, starting transfers between devices: 71.6 us -> 71.3 us  [shift(): return lax.ppermute(values, 'tp' if axis in 'uwz' else 'ep', pairs)]
  transfers between devices with their start and end apart: 70 -> 71, of which waited for: 40 -> 38; matrix products, arithmetic and copies ran while one was open for 23% -> 22% of each run, Pallas kernels for 18% -> 19%
where the time goes in v4:
time: 908 us; the launch traced here: 899 us
  waiting for transfers between devices  373 us (41%)
  Pallas kernels  170 us (19%)
  matrix products  102 us (11%)
  other arithmetic  84.4 us (9%)
  local copies, waits for them, and re-layouts  81.2 us (9%)
  starting transfers between devices  71.5 us (8%)
  between operations  16.7 us (2%)
    ppermute x68, waiting for transfers between devices, shift(): return lax.ppermute(values, 'tp' if axis in 'uwz' else 'ep', pairs)  270 us
    pallas_call x4, Pallas kernels, call(): pl.pallas_call(functools.partial(kernel, base, len(goes_on), parts), grid...  156 us
    all_gather x3, waiting for transfers between devices, gathered(): return lax.all_gather(values, both, axis=0, tiled=True)  103 us
    ppermute x68, starting transfers between devices, shift(): return lax.ppermute(values, 'tp' if axis in 'uwz' else 'ep', pairs)  71.3 us
    dot_general x3, matrix products, weight_grad(): return jnp.einsum(subscripts, left, right, preferred_element_type=wide)  62.2 us
    unnamed x214, local copies, waits for them, and re-layouts  43.7 us
    convert_element_type x26, other arithmetic, reduce_axis(): return total.astype(kind)  30.2 us
  transfers between devices with their start and end apart: 71, of which 38 were waited for; matrix products, arithmetic and copies ran while one was open for 22% of the time, Pallas kernels for 19%

profile of v4, /device:TPU:0, one launch (start us, length us, event | category | flops | bytes accessed | tf_op | source)
XLA Modules:
  0.0 898.8 jit_solution(11749766121955799522)
XLA Ops:
  13.6 12.0 %collective-permute-done = bf16[1,1,1,1,1,64,2048]{6,5,4,3,2,1,0:T(8,128)(2,1)S(1)} collective-permute-done((bf16[1,1,1,1,1,64,2048]{6,5,4,3,2,1,0:T(8,128)(2,1)}, bf16[1,1,1,1,1,64,2048]{6,5,4,3,2,1,0:T(8,128)(2,1)S(1)}, u32[]{:S(2)}, u32[]{:S(2)}) %collective-permute-start) | collective-permute-done | bytes 262176 | tf_op jit(solution)/shard_map/ppermute | solution.py:96
  28.6 25.6 %collective-permute-done.1 = bf16[1,1,1,2,1,64,2048]{6,5,4,3,2,1,0:T(8,128)(2,1)S(1)} collective-permute-done((bf16[1,1,1,2,1,64,2048]{6,5,4,3,2,1,0:T(8,128)(2,1)S(1)}, bf16[1,1,1,2,1,64,2048]{6,5,4,3,2,1,0:T(8,128)(2,1)S(1)}, u32[]{:S(2)}, u32[]{:S(2)}) %collective-permute-start.1) | collective-permute-done | bytes 524320 | tf_op jit(solution)/shard_map/ppermute | solution.py:96
  58.5 18.9 %collective-permute-done.2 = bf16[1,1,1,2,2,32,2048]{6,5,4,3,2,1,0:T(8,128)(2,1)S(1)} collective-permute-done((bf16[1,1,1,2,2,32,2048]{6,5,4,3,2,1,0:T(8,128)(2,1)S(1)}, bf16[1,1,1,2,2,32,2048]{6,5,4,3,2,1,0:T(8,128)(2,1)S(1)}, u32[]{:S(2)}, u32[]{:S(2)}) %collective-permute-start.2) | collective-permute-done | bytes 524320 | tf_op jit(solution)/shard_map/ppermute | solution.py:96
  84.2 20.1 %collective-permute-done.3 = bf16[1,2,1,2,2,32,2048]{6,5,4,3,2,1,0:T(8,128)(2,1)S(1)} collective-permute-done((bf16[1,2,1,2,2,32,2048]{6,5,4,3,2,1,0:T(8,128)(2,1)S(1)}, bf16[1,2,1,2,2,32,2048]{6,5,4,3,2,1,0:T(8,128)(2,1)S(1)}, u32[]{:S(2)}, u32[]{:S(2)}) %collective-permute-start.3) | collective-permute-done | bytes 1048608 | tf_op jit(solution)/shard_map/ppermute | solution.py:96
  104.4 9.7 %collective-permute-done.5 = bf16[2,1,1,2,2,32,2048]{6,5,4,3,2,1,0:T(8,128)(2,1)} collective-permute-done((bf16[2,1,1,2,2,32,2048]{6,5,4,3,2,1,0:T(8,128)(2,1)S(1)}, bf16[2,1,1,2,2,32,2048]{6,5,4,3,2,1,0:T(8,128)(2,1)}, u32[]{:S(2)}, u32[]{:S(2)}) %collective-permute-start.5) | collective-permute-done | bytes 1048608 | tf_op jit(solution)/shard_map/ppermute | solution.py:96
  119.9 5.4 pad_maximum_fusion
  126.2 9.9 %collective-permute-done.6 = bf16[2,2,1,2,2,64,2048]{6,5,4,3,2,1,0:T(8,128)(2,1)} collective-permute-done((bf16[2,2,1,2,2,64,2048]{6,5,4,3,2,1,0:T(8,128)(2,1)}, bf16[2,2,1,2,2,64,2048]{6,5,4,3,2,1,0:T(8,128)(2,1)}, u32[]{:S(2)}, u32[]{:S(2)}) %collective-permute-start.6) | collective-permute-done | bytes 4194336 | tf_op jit(solution)/shard_map/ppermute | solution.py:96
  136.1 5.0 constant_dynamic-update-slice_fusion.10
  154.3 13.7 %collective-permute-done.9 = bf16[2,2,1,1,1,128,128]{6,5,4,3,2,1,0:T(8,128)(2,1)S(1)} collective-permute-done((bf16[2,2,1,1,1,128,128]{6,5,4,3,2,1,0:T(8,128)(2,1)S(1)}, bf16[2,2,1,1,1,128,128]{6,5,4,3,2,1,0:T(8,128)(2,1)S(1)}, u32[]{:S(2)}, u32[]{:S(2)}) %collective-permute-start.9) | collective-permute-done | bytes 131104 | tf_op jit(solution)/shard_map/ppermute | solution.py:96
  170.0 27.0 %collective-permute-done.10 = bf16[2,2,1,2,1,128,128]{6,5,4,3,2,1,0:T(8,128)(2,1)S(1)} collective-permute-done((bf16[2,2,1,2,1,128,128]{6,5,4,3,2,1,0:T(8,128)(2,1)S(1)}, bf16[2,2,1,2,1,128,128]{6,5,4,3,2,1,0:T(8,128)(2,1)S(1)}, u32[]{:S(2)}, u32[]{:S(2)}) %collective-permute-start.10) | collective-permute-done | bytes 262176 | tf_op jit(solution)/shard_map/ppermute | solution.py:96
  206.2 10.4 %fusion.100 = f32[128,6144]{1,0:T(8,128)S(1)} fusion(bf16[128,2048]{1,0:T(8,128)(2,1)} %fusion.31, bf16[2048,6144]{1,0:T(8,128)(2,1)} %all-gather.6.cloned.1.call-done.right_ref), kind=kOutput, calls=%fused_computation.349 | convolution fusion | flops 3221225472 | bytes 28835840 | tf_op jit(solution)/shard_map/dot_general | solution.py:605
  234.3 11.8 %copy.145 = bf16[8,2048,256]{1,2,0:T(8,128)(2,1)} copy(bf16[8,2048,256]{2,1,0:T(8,128)(2,1)} %refs_0_.3) | data formatting | bytes 16777216 | tf_op args[10]
  246.1 11.5 %copy.146 = bf16[8,2048,256]{1,2,0:T(8,128)(2,1)} copy(bf16[8,2048,256]{2,1,0:T(8,128)(2,1)} %refs_1_.3) | data formatting | bytes 16777216 | tf_op args[11]
  257.6 11.5 %copy.147 = bf16[8,256,2048]{1,2,0:T(8,128)(2,1)} copy(bf16[8,256,2048]{2,1,0:T(8,128)(2,1)} %refs_2_.3) | data formatting | bytes 16777216 | tf_op args[12]
  276.7 71.3 %all-gather.8.cloned.1.call-done = bf16[4096,2048]{1,0:T(8,128)(2,1)} async-done(((bf16[128,2048]{1,0:T(8,128)(2,1)}), bf16[4096,2048]{1,0:T(8,128)(2,1)}) %all-gather.8.cloned.1.call-update) | async-done | bytes 16777232 | tf_op jit(solution)/shard_map/all_gather | solution.py:564
  347.9 39.0 %experts_forward.2 = (bf16[16,64,2048]{2,1,0:T(8,128)(2,1)}, bf16[16,64,2048]{2,1,0:T(8,128)(2,1)}, f32[16,8,128]{2,1,0:T(8,128)}, f32[8,512,512]{2,1,0:T(8,128)...) custom-call(s32[1]{0:T(128)} %bitcast.1._, f32[32,8,128]{2,1,0:T(8,128)} %dynamic-slice_convert_fusion.slots_ref, ...), custom_call_target="tpu_custom_call" | custom-call | flops 85899345920 | bytes 67108864 | tf_op jit(solution)/shard_map/experts_forward/pallas_call | solution.py:439
  387.5 39.2 %experts_forward.3 = (bf16[16,64,2048]{2,1,0:T(8,128)(2,1)}, bf16[16,64,2048]{2,1,0:T(8,128)(2,1)}, f32[16,8,128]{2,1,0:T(8,128)}, f32[8,512,512]{2,1,0:T(8,128)...) custom-call(s32[1]{0:T(128)} %bitcast._, ...), custom_call_target="tpu_custom_call", output_to_operand_aliasing={{4}: (7, {}), {5}: (8, {})} | custom-call | flops 85899345920 | bytes 67108864 | tf_op jit(solution)/shard_map/experts_forward/pallas_call | solution.py:439
  433.8 30.3 %all-gather.10.cloned.1.call-done = bf16[4096,2048]{1,0:T(8,128)(2,1)} async-done(((bf16[128,2048]{1,0:T(8,128)(2,1)}), bf16[4096,2048]{1,0:T(8,128)(2,1)}) %all-gather.10.cloned.1.call-update) | async-done | bytes 16777232 | tf_op jit(solution)/shard_map/all_gather | solution.py:564
  466.1 39.0 %experts_backward.2 = (bf16[16,64,2048]{2,1,0:T(8,128)(2,1)}, bf16[16,64,2048]{2,1,0:T(8,128)(2,1)}, f32[16,8,128]{2,1,0:T(8,128)}, bf16[8,1024,256]{2,1,0:T(8,1...) custom-call(s32[1]{0:T(128)} %bitcast.1._, ...), custom_call_target="tpu_custom_call" | custom-call | flops 85899345920 | bytes 67108864 | tf_op jit(solution)/shard_map/experts_backward/pallas_call | solution.py:439
  505.1 7.1 collective-permute-done.15
  526.0 39.1 %experts_backward.3 = (bf16[16,64,2048]{2,1,0:T(8,128)(2,1)}, bf16[16,64,2048]{2,1,0:T(8,128)(2,1)}, f32[16,8,128]{2,1,0:T(8,128)}, bf16[8,1024,256]{2,1,0:T(8,1...) custom-call(s32[1]{0:T(128)} %bitcast._, ...), custom_call_target="tpu_custom_call", output_to_operand_aliasing={{3}: (8, {}), {4}: (9, {}), {5}: (10, {})} | custom-call | flops 85899345920 | bytes 67108864 | tf_op jit(solution)/shard_map/experts_backward/pallas_call | solution.py:439
  581.4 20.1 %fusion.102 = f32[8,256,2048]{2,1,0:T(8,128)} fusion(bf16[8,1024,256]{2,1,0:T(8,128)(2,1)} %get-tuple-element.212, bf16[8,1024,2048]{2,1,0:T(8,128)(2,1)} %bitcast.426), kind=kOutput, calls=%fused_computation.351 | convolution fusion | flops 8589934592 | bytes 54525952 | tf_op jit(solution)/shard_map/erh,erd->ehd/dot_general | solution.py:717
  601.5 21.0 %fusion.101 = f32[8,2048,256]{2,1,0:T(8,128)} fusion(bf16[8,1024,2048]{2,1,0:T(8,128)(2,1)} %bitcast.427, bf16[8,1024,256]{2,1,0:T(8,128)(2,1)} %get-tuple-element.211), kind=kOutput, calls=%fused_computation.350 | convolution fusion | flops 8589934592 | bytes 54525952 | tf_op jit(solution)/shard_map/erd,erh->edh/dot_general | solution.py:717
  641.2 21.1 %fusion.103 = f32[8,2048,256]{2,1,0:T(8,128)} fusion(bf16[8,1024,2048]{2,1,0:T(8,128)(2,1)} %bitcast.428, bf16[8,1024,256]{2,1,0:T(8,128)(2,1)} %get-tuple-element.220), kind=kOutput, calls=%fused_computation.352 | convolution fusion | flops 8589934592 | bytes 54525952 | tf_op jit(solution)/shard_map/erd,erh->edh/dot_general | solution.py:717
  671.2 23.4 %collective-permute-done.30 = bf16[2,64,2048]{2,1,0:T(8,128)(2,1)S(1)} collective-permute-done((bf16[2,64,2048]{2,1,0:T(8,128)(2,1)S(1)}, bf16[2,64,2048]{2,1,0:T(8,128)(2,1)S(1)}, u32[]{:S(2)}, u32[]{:S(2)}) %collective-permute-start.30) | collective-permute-done | bytes 524320 | tf_op jit(solution)/shard_map/ppermute | solution.py:96
  703.5 6.9 collective-permute-done.34
  713.7 6.5 fusion.29
  750.6 6.4 collective-permute-done.44
  764.0 13.9 %turned_product.1 = f32[128,2048]{1,0:T(8,128)S(1)} custom-call(bf16[128,6144]{1,0:T(8,128)(2,1)S(1)} %pad_maximum_fusion.2.left_ref, bf16[2048,6144]{1,0:T(8,128)(2,1)} %all-gather.6.cloned.1.call-done.right_ref), custom_call_target="tpu_custom_call" | custom-call | flops 80530636800 | bytes 25165824 | tf_op jit(solution)/shard_map/turned_product/pallas_call | solution.py:238
  801.0 19.6 %collective-permute-done.49 = bf16[2,2,64,1024]{3,2,0,1:T(8,128)(2,1)S(1)} collective-permute-done((bf16[2,2,64,1024]{3,2,0,1:T(8,128)(2,1)S(1)}, bf16[2,2,64,1024]{3,2,0,1:T(8,128)(2,1)S(1)}, u32[]{:S(2)}, u32[]{:S(2)}) %collective-permute-start.49) | collective-permute-done | bytes 524320 | tf_op jit(solution)/shard_map/ppermute | solution.py:96
  833.7 5.5 collective-permute-done.53
  842.0 23.6 %collective-permute-done.52 = bf16[2,64,1024]{2,1,0:T(8,128)(2,1)S(1)} collective-permute-done((bf16[2,64,1024]{2,1,0:T(8,128)(2,1)S(1)}, bf16[2,64,1024]{2,1,0:T(8,128)(2,1)S(1)}, u32[]{:S(2)}, u32[]{:S(2)}) %collective-permute-start.52) | collective-permute-done | bytes 262176 | tf_op jit(solution)/shard_map/ppermute | solution.py:96
  (558 shorter events, 256.6 us)
Async XLA Ops:
  7.2 199.0 %all-gather.6.cloned.1.call-start = ((), (), s32[]{:S(2)}) async-start(), calls=%async_computation | async-start | bytes 25952256 | tf_op jit(solution)/shard_map/all_gather | solution.py:564
  9.3 338.6 %all-gather.8.cloned.1.call-start = ((), (), s32[]{:S(2)}) async-start(), calls=%async_computation.1 | async-start | bytes 17301504 | tf_op jit(solution)/shard_map/all_gather | solution.py:564
  25.6 28.6 %collective-permute-start.1 = (bf16[1,1,1,2,1,64,2048]{6,5,4,3,2,1,0:T(8,128)(2,1)S(1)}, bf16[1,1,1,2,1,64,2048]{6,5,4,3,2,1,0:T(8,128)(2,1)S(1)}, u32[]{:S(2)}, u32[]{:S(2)}) collective-permute-start(bf16[1,1,1,2,1,64,2048]{6,5,4,3,2,1,0:T(8,128)(2,1)S(1)} %constant_dynamic-update-slice_fusion.22), channel_id=1, source_target_pairs={{0,1},{1,0},{2,3},{3,2},{4,5},{5,4},{6,7},{7,6},{8,9},{9,8},{10,11... | collective-permute-start | bytes 1572872 | tf_op jit(solution)/shard_map/ppermute | solution.py:96
  77.4 26.9 %collective-permute-start.3 = (bf16[1,2,1,2,2,32,2048]{6,5,4,3,2,1,0:T(8,128)(2,1)S(1)}, bf16[1,2,1,2,2,32,2048]{6,5,4,3,2,1,0:T(8,128)(2,1)S(1)}, u32[]{:S(2)}, u32[]{:S(2)}) collective-permute-start(bf16[1,2,1,2,2,32,2048]{6,5,4,3,2,1,0:T(8,128)(2,1)S(1)} %constant_dynamic-update-slice_fusion.18), channel_id=1, source_target_pairs={{0,16},{4,20},{8,24},{12,28},{16,0},{20,4},{24,8},{28,12},{1,17},{... | collective-permute-start | bytes 3145736 | tf_op jit(solution)/shard_map/ppermute | solution.py:96
  83.4 30.8 %collective-permute-start.5 = (bf16[2,1,1,2,2,32,2048]{6,5,4,3,2,1,0:T(8,128)(2,1)S(1)}, bf16[2,1,1,2,2,32,2048]{6,5,4,3,2,1,0:T(8,128)(2,1)}, u32[]{:S(2)}, u32[]{:S(2)}) collective-permute-start(bf16[2,1,1,2,2,32,2048]{6,5,4,3,2,1,0:T(8,128)(2,1)S(1)} %constant_dynamic-update-slice_fusion.14), channel_id=1, source_target_pairs={{0,8},{4,12},{8,0},{12,4},{16,24},{20,28},{24,16},{28,20},{1,9},{5... | collective-permute-start | bytes 3145736 | tf_op jit(solution)/shard_map/ppermute | solution.py:96
  168.0 29.0 %collective-permute-start.10 = (bf16[2,2,1,2,1,128,128]{6,5,4,3,2,1,0:T(8,128)(2,1)S(1)}, bf16[2,2,1,2,1,128,128]{6,5,4,3,2,1,0:T(8,128)(2,1)S(1)}, u32[]{:S(2)}, u32[]{:S(2)}) collective-permute-start(bf16[2,2,1,2,1,128,128]{6,5,4,3,2,1,0:T(8,128)(2,1)S(1)} %constant_dynamic-update-slice_fusion.4), channel_id=1, source_target_pairs={{0,1},{1,0},{2,3},{3,2},{4,5},{5,4},{6,7},{7,6},{8,9},{9,8},{10,11... | collective-permute-start | bytes 786440 | tf_op jit(solution)/shard_map/ppermute | solution.py:96
  233.5 230.6 %all-gather.10.cloned.1.call-start = ((), (), s32[]{:S(2)}) async-start(), calls=%async_computation.2 | async-start | bytes 17301504 | tf_op jit(solution)/shard_map/all_gather | solution.py:564
  274.1 246.6 %collective-permute-start.16 = (bf16[128,2048]{1,0:T(8,128)(2,1)}, bf16[128,2048]{1,0:T(8,128)(2,1)}, u32[]{:S(2)}, u32[]{:S(2)}) collective-permute-start(bf16[128,2048]{1,0:T(8,128)(2,1)} %pad_maximum_fusion.11), channel_id=1, source_target_pairs={{0,4},{4,0},{8,12},{12,8},{16,20},{20,16},{24,28},{28,24},{1,5},{5... | collective-permute-start | bytes 1572872 | tf_op jit(solution)/shard_map/ppermute | solution.py:96
  387.0 39.8 %collective-permute-start.12 = (bf16[16,64,2048]{2,1,0:T(8,128)(2,1)}, bf16[16,64,2048]{2,1,0:T(8,128)(2,1)}, u32[]{:S(2)}, u32[]{:S(2)}) collective-permute-start(bf16[16,64,2048]{2,1,0:T(8,128)(2,1)} %get-tuple-element.158), channel_id=1, source_target_pairs={{0,4},{4,0},{8,12},{12,8},{16,20},{20,16},{24,28},{28,24},{1,5},{5... | collective-permute-start | bytes 12582920 | tf_op jit(solution)/shard_map/ppermute | solution.py:96
  387.3 39.5 %collective-permute-start.13 = (bf16[16,64,2048]{2,1,0:T(8,128)(2,1)}, bf16[16,64,2048]{2,1,0:T(8,128)(2,1)}, u32[]{:S(2)}, u32[]{:S(2)}) collective-permute-start(bf16[16,64,2048]{2,1,0:T(8,128)(2,1)} %get-tuple-element.159), channel_id=1, source_target_pairs={{0,4},{4,0},{8,12},{12,8},{16,20},{20,16},{24,28},{28,24},{1,5},{5... | collective-permute-start | bytes 12582920 | tf_op jit(solution)/shard_map/ppermute | solution.py:96
  464.1 48.1 %collective-permute-start.15 = (bf16[2,2,2,64,2048]{4,3,1,2,0:T(8,128)(2,1)}, bf16[2,2,2,64,2048]{4,3,1,2,0:T(8,128)(2,1)}, u32[]{:S(2)}, u32[]{:S(2)}) collective-permute-start(bf16[2,2,2,64,2048]{4,3,1,2,0:T(8,128)(2,1)} %fusion.6), channel_id=1, source_target_pairs={{0,8},{4,12},{8,0},{12,4},{16,24},{20,28},{24,16},{28,20},{1,9},{5... | collective-permute-start | bytes 6291464 | tf_op jit(solution)/shard_map/ppermute | solution.py:96
  465.3 47.6 %collective-permute-start.14 = (bf16[2,2,2,64,2048]{4,3,1,2,0:T(8,128)(2,1)S(1)}, bf16[2,2,2,64,2048]{4,3,1,2,0:T(8,128)(2,1)}, u32[]{:S(2)}, u32[]{:S(2)}) collective-permute-start(bf16[2,2,2,64,2048]{4,3,1,2,0:T(8,128)(2,1)S(1)} %fusion.5), channel_id=1, source_target_pairs={{0,16},{4,20},{8,24},{12,28},{16,0},{20,4},{24,8},{28,12},{1,17},{... | collective-permute-start | bytes 6291464 | tf_op jit(solution)/shard_map/ppermute | solution.py:96
  523.1 42.0 %collective-permute-start.17 = (bf16[2,2,64,2048]{3,2,0,1:T(8,128)(2,1)}, bf16[2,2,64,2048]{3,2,0,1:T(8,128)(2,1)}, u32[]{:S(2)}, u32[]{:S(2)}) collective-permute-start(bf16[2,2,64,2048]{3,2,0,1:T(8,128)(2,1)} %dynamic-slice_bitcast_fusion.4), channel_id=1, source_target_pairs={{0,8},{4,12},{8,0},{12,4},{16,24},{20,28},{24,16},{28,20},{1,9},{5... | collective-permute-start | bytes 3145736 | tf_op jit(solution)/shard_map/ppermute | solution.py:96
  524.0 43.2 %collective-permute-start.18 = (bf16[2,2,64,2048]{3,2,0,1:T(8,128)(2,1)S(1)}, bf16[2,2,64,2048]{3,2,0,1:T(8,128)(2,1)}, u32[]{:S(2)}, u32[]{:S(2)}) collective-permute-start(bf16[2,2,64,2048]{3,2,0,1:T(8,128)(2,1)S(1)} %dynamic-slice_bitcast_fusion.3), channel_id=1, source_target_pairs={{0,16},{4,20},{8,24},{12,28},{16,0},{20,4},{24,8},{28,12},{1,17},{... | collective-permute-start | bytes 3145736 | tf_op jit(solution)/shard_map/ppermute | solution.py:96
  525.5 43.5 %collective-permute-start.19 = (bf16[16,64,2048]{2,1,0:T(8,128)(2,1)}, bf16[16,64,2048]{2,1,0:T(8,128)(2,1)}, u32[]{:S(2)}, u32[]{:S(2)}) collective-permute-start(bf16[16,64,2048]{2,1,0:T(8,128)(2,1)} %get-tuple-element.200), channel_id=1, source_target_pairs={{0,4},{4,0},{8,12},{12,8},{16,20},{20,16},{24,28},{28,24},{1,5},{5... | collective-permute-start | bytes 12582920 | tf_op jit(solution)/shard_map/ppermute | solution.py:96
  525.5 43.5 %collective-permute-start.20 = (bf16[16,64,2048]{2,1,0:T(8,128)(2,1)}, bf16[16,64,2048]{2,1,0:T(8,128)(2,1)}, u32[]{:S(2)}, u32[]{:S(2)}) collective-permute-start(bf16[16,64,2048]{2,1,0:T(8,128)(2,1)} %get-tuple-element.201), channel_id=1, source_target_pairs={{0,4},{4,0},{8,12},{12,8},{16,20},{20,16},{24,28},{28,24},{1,5},{5... | collective-permute-start | bytes 12582920 | tf_op jit(solution)/shard_map/ppermute | solution.py:96
  569.1 53.4 %collective-permute-start.24 = (f32[2,2,2,2,8,128]{5,4,3,2,1,0:T(8,128)S(1)}, f32[2,2,2,2,8,128]{5,4,3,2,1,0:T(8,128)S(1)}, u32[]{:S(2)}, u32[]{:S(2)}) collective-permute-start(f32[2,2,2,2,8,128]{5,4,3,2,1,0:T(8,128)S(1)} %dynamic-slice_bitcast_fusion.22), channel_id=1, source_target_pairs={{0,1},{1,0},{2,3},{3,2},{4,5},{5,4},{6,7},{7,6},{8,9},{9,8},{10,11... | collective-permute-start | bytes 196616 | tf_op jit(solution)/shard_map/ppermute | solution.py:96
  569.7 52.9 %collective-permute-start.23 = (bf16[2,128,2048]{2,1,0:T(8,128)(2,1)S(1)}, bf16[2,128,2048]{2,1,0:T(8,128)(2,1)}, u32[]{:S(2)}, u32[]{:S(2)}) collective-permute-start(bf16[2,128,2048]{2,1,0:T(8,128)(2,1)S(1)} %dynamic-slice_bitcast_fusion.2), channel_id=1, source_target_pairs={{0,1},{1,0},{2,3},{3,2},{4,5},{5,4},{6,7},{7,6},{8,9},{9,8},{10,11... | collective-permute-start | bytes 3145736 | tf_op jit(solution)/shard_map/ppermute | solution.py:96
  575.2 49.0 %collective-permute-start.22 = (bf16[2,2,2,64,2048]{4,3,2,1,0:T(8,128)(2,1)}, bf16[2,2,2,64,2048]{4,3,2,1,0:T(8,128)(2,1)}, u32[]{:S(2)}, u32[]{:S(2)}) collective-permute-start(bf16[2,2,2,64,2048]{4,3,2,1,0:T(8,128)(2,1)} %fusion.8), channel_id=1, source_target_pairs={{0,8},{4,12},{8,0},{12,4},{16,24},{20,28},{24,16},{28,20},{1,9},{5... | collective-permute-start | bytes 6291464 | tf_op jit(solution)/shard_map/ppermute | solution.py:96
  580.2 47.2 %collective-permute-start.21 = (bf16[2,2,2,64,2048]{4,3,1,2,0:T(8,128)(2,1)}, bf16[2,2,2,64,2048]{4,3,1,2,0:T(8,128)(2,1)}, u32[]{:S(2)}, u32[]{:S(2)}) collective-permute-start(bf16[2,2,2,64,2048]{4,3,1,2,0:T(8,128)(2,1)} %fusion.7), channel_id=1, source_target_pairs={{0,16},{4,20},{8,24},{12,28},{16,0},{20,4},{24,8},{28,12},{1,17},{... | collective-permute-start | bytes 6291464 | tf_op jit(solution)/shard_map/ppermute | solution.py:96
  635.0 27.4 %collective-permute-start.28 = (f32[2,2,2,8,128]{4,3,2,1,0:T(8,128)S(1)}, f32[2,2,2,8,128]{4,3,2,1,0:T(8,128)S(1)}, u32[]{:S(2)}, u32[]{:S(2)}) collective-permute-start(f32[2,2,2,8,128]{4,3,2,1,0:T(8,128)S(1)} %dynamic-slice_bitcast_fusion.27), channel_id=1, source_target_pairs={{0,2},{1,3},{2,0},{3,1},{4,6},{5,7},{6,4},{7,5},{8,10},{9,11},{10,... | collective-permute-start | bytes 98312 | tf_op jit(solution)/shard_map/ppermute | solution.py:96
  665.9 29.2 %collective-permute-start.33 = (bf16[256,2048]{1,0:T(8,128)(2,1)S(1)}, bf16[256,2048]{1,0:T(8,128)(2,1)S(1)}, u32[]{:S(2)}, u32[]{:S(2)}) collective-permute-start(bf16[256,2048]{1,0:T(8,128)(2,1)S(1)} %constant_dynamic-update-slice_fusion.24), channel_id=1, source_target_pairs={{0,8},{4,12},{8,0},{12,4},{16,24},{20,28},{24,16},{28,20},{1,9},{5... | collective-permute-start | bytes 3145736 | tf_op jit(solution)/shard_map/ppermute | solution.py:96
  667.5 27.7 %collective-permute-start.32 = (bf16[256,1024]{1,0:T(8,128)(2,1)S(1)}, bf16[256,1024]{1,0:T(8,128)(2,1)S(1)}, u32[]{:S(2)}, u32[]{:S(2)}) collective-permute-start(bf16[256,1024]{1,0:T(8,128)(2,1)S(1)} %slice.134), channel_id=1, source_target_pairs={{0,16},{4,20},{8,24},{12,28},{16,0},{20,4},{24,8},{28,12},{1,17},{... | collective-permute-start | bytes 1572872 | tf_op jit(solution)/shard_map/ppermute | solution.py:96
  668.2 26.4 %collective-permute-start.30 = (bf16[2,64,2048]{2,1,0:T(8,128)(2,1)S(1)}, bf16[2,64,2048]{2,1,0:T(8,128)(2,1)S(1)}, u32[]{:S(2)}, u32[]{:S(2)}) collective-permute-start(bf16[2,64,2048]{2,1,0:T(8,128)(2,1)S(1)} %dynamic-slice_bitcast_fusion.9), channel_id=1, source_target_pairs={{0,2},{1,3},{2,0},{3,1},{4,6},{5,7},{6,4},{7,5},{8,10},{9,11},{10,... | collective-permute-start | bytes 1572872 | tf_op jit(solution)/shard_map/ppermute | solution.py:96
  669.7 25.3 %collective-permute-start.29 = (bf16[2,64,2048]{2,1,0:T(8,128)(2,1)S(1)}, bf16[2,64,2048]{2,1,0:T(8,128)(2,1)S(1)}, u32[]{:S(2)}, u32[]{:S(2)}) collective-permute-start(bf16[2,64,2048]{2,1,0:T(8,128)(2,1)S(1)} %dynamic-slice_bitcast_fusion.10), channel_id=1, source_target_pairs={{0,1},{1,0},{2,3},{3,2},{4,5},{5,4},{6,7},{7,6},{8,9},{9,8},{10,11... | collective-permute-start | bytes 1572872 | tf_op jit(solution)/shard_map/ppermute | solution.py:96
  761.5 25.4 %collective-permute-start.47 = (bf16[2,2,2,64,1024]{4,3,0,2,1:T(8,128)(2,1)S(1)}, bf16[2,2,2,64,1024]{4,3,0,2,1:T(8,128)(2,1)S(1)}, u32[]{:S(2)}, u32[]{:S(2)}) collective-permute-start(bf16[2,2,2,64,1024]{4,3,0,2,1:T(8,128)(2,1)S(1)} %copy_bitcast_fusion.2), channel_id=1, source_target_pairs={{0,8},{4,12},{8,0},{12,4},{16,24},{20,28},{24,16},{28,20},{1,9},{5... | collective-permute-start | bytes 3145736 | tf_op jit(solution)/shard_map/ppermute | solution.py:96
  762.5 25.9 %collective-permute-start.46 = (bf16[2,2,2,64,1024]{4,3,0,1,2:T(8,128)(2,1)S(1)}, bf16[2,2,2,64,1024]{4,3,0,1,2:T(8,128)(2,1)S(1)}, u32[]{:S(2)}, u32[]{:S(2)}) collective-permute-start(bf16[2,2,2,64,1024]{4,3,0,1,2:T(8,128)(2,1)S(1)} %copy_bitcast_fusion.3), channel_id=1, source_target_pairs={{0,16},{4,20},{8,24},{12,28},{16,0},{20,4},{24,8},{28,12},{1,17},{... | collective-permute-start | bytes 3145736 | tf_op jit(solution)/shard_map/ppermute | solution.py:96
  793.0 29.7 %collective-permute-start.51 = (bf16[2,2,2,64,1024]{4,3,0,2,1:T(8,128)(2,1)S(1)}, bf16[2,2,2,64,1024]{4,3,0,2,1:T(8,128)(2,1)S(1)}, u32[]{:S(2)}, u32[]{:S(2)}) collective-permute-start(bf16[2,2,2,64,1024]{4,3,0,2,1:T(8,128)(2,1)S(1)} %copy_bitcast_fusion), channel_id=1, source_target_pairs={{0,8},{4,12},{8,0},{12,4},{16,24},{20,28},{24,16},{28,20},{1,9},{5... | collective-permute-start | bytes 3145736 | tf_op jit(solution)/shard_map/ppermute | solution.py:96
  795.1 28.0 %collective-permute-start.50 = (bf16[2,2,2,64,1024]{4,3,0,1,2:T(8,128)(2,1)S(1)}, bf16[2,2,2,64,1024]{4,3,0,1,2:T(8,128)(2,1)S(1)}, u32[]{:S(2)}, u32[]{:S(2)}) collective-permute-start(bf16[2,2,2,64,1024]{4,3,0,1,2:T(8,128)(2,1)S(1)} %copy_bitcast_fusion.1), channel_id=1, source_target_pairs={{0,16},{4,20},{8,24},{12,28},{16,0},{20,4},{24,8},{28,12},{1,17},{... | collective-permute-start | bytes 3145736 | tf_op jit(solution)/shard_map/ppermute | solution.py:96
  827.6 38.2 %collective-permute-start.55 = (bf16[2,2,64,1024]{3,2,0,1:T(8,128)(2,1)}, bf16[2,2,64,1024]{3,2,0,1:T(8,128)(2,1)S(1)}, u32[]{:S(2)}, u32[]{:S(2)}) collective-permute-start(bf16[2,2,64,1024]{3,2,0,1:T(8,128)(2,1)} %dynamic-slice_bitcast_fusion.5), channel_id=1, source_target_pairs={{0,2},{1,3},{2,0},{3,1},{4,6},{5,7},{6,4},{7,5},{8,10},{9,11},{10,... | collective-permute-start | bytes 1572872 | tf_op jit(solution)/shard_map/ppermute | solution.py:96
  830.5 35.5 %collective-permute-start.54 = (bf16[2,2,64,1024]{3,2,0,1:T(8,128)(2,1)S(1)}, bf16[2,2,64,1024]{3,2,0,1:T(8,128)(2,1)S(1)}, u32[]{:S(2)}, u32[]{:S(2)}) collective-permute-start(bf16[2,2,64,1024]{3,2,0,1:T(8,128)(2,1)S(1)} %dynamic-slice_bitcast_fusion.6), channel_id=1, source_target_pairs={{0,1},{1,0},{2,3},{3,2},{4,5},{5,4},{6,7},{7,6},{8,9},{9,8},{10,11... | collective-permute-start | bytes 1572872 | tf_op jit(solution)/shard_map/ppermute | solution.py:96
  831.6 34.1 %collective-permute-start.52 = (bf16[2,64,1024]{2,1,0:T(8,128)(2,1)S(1)}, bf16[2,64,1024]{2,1,0:T(8,128)(2,1)S(1)}, u32[]{:S(2)}, u32[]{:S(2)}) collective-permute-start(bf16[2,64,1024]{2,1,0:T(8,128)(2,1)S(1)} %dynamic-slice_bitcast_fusion.16), channel_id=1, source_target_pairs={{0,2},{1,3},{2,0},{3,1},{4,6},{5,7},{6,4},{7,5},{8,10},{9,11},{10,... | collective-permute-start | bytes 786440 | tf_op jit(solution)/shard_map/ppermute | solution.py:96
  (136 other events, 1130.4 us)
Sparse Core Ops, SparseCore 0:
  11.5 194.6 all-gather.5
  233.6 114.2 all-gather.7
  350.9 113.0 all-gather.9

commit v5 on v4

--- a/solution.py
+++ b/solution.py
@@ -751,8 +751,8 @@
     sums, gate_grads, y_rows, x_rows = together(sums, gate_grads, y_rows, x_rows)
     back_sum = jnp.concatenate(grid.reduce_z(sums, 1), axis=0)
     grad_probs = grid.reduce_scatter(gate_grads, "yx", "yx").T
-    back_sum, grad_probs = together(back_sum, grad_probs)
     y_rows, x_rows = jnp.concatenate(y_rows, axis=0), jnp.concatenate(x_rows, axis=0)
+    back_sum, grad_probs, y_rows, x_rows = together(back_sum, grad_probs, y_rows, x_rows)
     back_sum, block_out, acc_gate, acc_up, acc_down = together(
         back_sum, block_out, acc_gate, acc_up, acc_down
     )

time: 908 us -> 908 us (level)
    unnamed x214 -> x208, local copies, waits for them, and re-layouts: 43.7 us -> 43.6 us
  transfers between devices with their start and end apart: 71 -> 71, of which waited for: 38 -> 36; matrix products, arithmetic and copies ran while one was open for 22% -> 22% of each run, Pallas kernels for 19% -> 19%
where the time goes in v5:
time: 908 us; the launch traced here: 899 us
  waiting for transfers between devices  371 us (41%)
  Pallas kernels  170 us (19%)
  matrix products  102 us (11%)
  other arithmetic  87.1 us (10%)
  local copies, waits for them, and re-layouts  81 us (9%)
  starting transfers between devices  71.1 us (8%)
  between operations  16.6 us (2%)
    ppermute x68, waiting for transfers between devices, shift(): return lax.ppermute(values, 'tp' if axis in 'uwz' else 'ep', pairs)  268 us
    pallas_call x4, Pallas kernels, call(): pl.pallas_call(functools.partial(kernel, base, len(goes_on), parts), grid...  156 us
    all_gather x3, waiting for transfers between devices, gathered(): return lax.all_gather(values, both, axis=0, tiled=True)  102 us
    ppermute x68, starting transfers between devices, shift(): return lax.ppermute(values, 'tp' if axis in 'uwz' else 'ep', pairs)  70.9 us
    dot_general x3, matrix products, weight_grad(): return jnp.einsum(subscripts, left, right, preferred_element_type=wide)  62.2 us
    unnamed x208, local copies, waits for them, and re-layouts  43.6 us
    convert_element_type x26, other arithmetic, reduce_axis(): return total.astype(kind)  30.3 us
  transfers between devices with their start and end apart: 71, of which 36 were waited for; matrix products, arithmetic and copies ran while one was open for 22% of the time, Pallas kernels for 19%

profile of v5, /device:TPU:0, one launch (start us, length us, event | category | flops | bytes accessed | tf_op | source)
XLA Modules:
  0.0 898.9 jit_solution(3237054136240859837)
XLA Ops:
  13.6 12.0 %collective-permute-done = bf16[1,1,1,1,1,64,2048]{6,5,4,3,2,1,0:T(8,128)(2,1)S(1)} collective-permute-done((bf16[1,1,1,1,1,64,2048]{6,5,4,3,2,1,0:T(8,128)(2,1)}, bf16[1,1,1,1,1,64,2048]{6,5,4,3,2,1,0:T(8,128)(2,1)S(1)}, u32[]{:S(2)}, u32[]{:S(2)}) %collective-permute-start) | collective-permute-done | bytes 262176 | tf_op jit(solution)/shard_map/ppermute | solution.py:96
  28.6 25.6 %collective-permute-done.1 = bf16[1,1,1,2,1,64,2048]{6,5,4,3,2,1,0:T(8,128)(2,1)S(1)} collective-permute-done((bf16[1,1,1,2,1,64,2048]{6,5,4,3,2,1,0:T(8,128)(2,1)S(1)}, bf16[1,1,1,2,1,64,2048]{6,5,4,3,2,1,0:T(8,128)(2,1)S(1)}, u32[]{:S(2)}, u32[]{:S(2)}) %collective-permute-start.1) | collective-permute-done | bytes 524320 | tf_op jit(solution)/shard_map/ppermute | solution.py:96
  58.5 18.9 %collective-permute-done.2 = bf16[1,1,1,2,2,32,2048]{6,5,4,3,2,1,0:T(8,128)(2,1)S(1)} collective-permute-done((bf16[1,1,1,2,2,32,2048]{6,5,4,3,2,1,0:T(8,128)(2,1)S(1)}, bf16[1,1,1,2,2,32,2048]{6,5,4,3,2,1,0:T(8,128)(2,1)S(1)}, u32[]{:S(2)}, u32[]{:S(2)}) %collective-permute-start.2) | collective-permute-done | bytes 524320 | tf_op jit(solution)/shard_map/ppermute | solution.py:96
  84.2 20.1 %collective-permute-done.3 = bf16[1,2,1,2,2,32,2048]{6,5,4,3,2,1,0:T(8,128)(2,1)S(1)} collective-permute-done((bf16[1,2,1,2,2,32,2048]{6,5,4,3,2,1,0:T(8,128)(2,1)S(1)}, bf16[1,2,1,2,2,32,2048]{6,5,4,3,2,1,0:T(8,128)(2,1)S(1)}, u32[]{:S(2)}, u32[]{:S(2)}) %collective-permute-start.3) | collective-permute-done | bytes 1048608 | tf_op jit(solution)/shard_map/ppermute | solution.py:96
  104.4 9.7 %collective-permute-done.5 = bf16[2,1,1,2,2,32,2048]{6,5,4,3,2,1,0:T(8,128)(2,1)} collective-permute-done((bf16[2,1,1,2,2,32,2048]{6,5,4,3,2,1,0:T(8,128)(2,1)S(1)}, bf16[2,1,1,2,2,32,2048]{6,5,4,3,2,1,0:T(8,128)(2,1)}, u32[]{:S(2)}, u32[]{:S(2)}) %collective-permute-start.5) | collective-permute-done | bytes 1048608 | tf_op jit(solution)/shard_map/ppermute | solution.py:96
  119.9 5.4 pad_maximum_fusion
  126.2 9.9 %collective-permute-done.6 = bf16[2,2,1,2,2,64,2048]{6,5,4,3,2,1,0:T(8,128)(2,1)} collective-permute-done((bf16[2,2,1,2,2,64,2048]{6,5,4,3,2,1,0:T(8,128)(2,1)}, bf16[2,2,1,2,2,64,2048]{6,5,4,3,2,1,0:T(8,128)(2,1)}, u32[]{:S(2)}, u32[]{:S(2)}) %collective-permute-start.6) | collective-permute-done | bytes 4194336 | tf_op jit(solution)/shard_map/ppermute | solution.py:96
  136.1 5.0 constant_dynamic-update-slice_fusion.10
  154.3 13.7 %collective-permute-done.9 = bf16[2,2,1,1,1,128,128]{6,5,4,3,2,1,0:T(8,128)(2,1)S(1)} collective-permute-done((bf16[2,2,1,1,1,128,128]{6,5,4,3,2,1,0:T(8,128)(2,1)S(1)}, bf16[2,2,1,1,1,128,128]{6,5,4,3,2,1,0:T(8,128)(2,1)S(1)}, u32[]{:S(2)}, u32[]{:S(2)}) %collective-permute-start.9) | collective-permute-done | bytes 131104 | tf_op jit(solution)/shard_map/ppermute | solution.py:96
  170.1 27.0 %collective-permute-done.10 = bf16[2,2,1,2,1,128,128]{6,5,4,3,2,1,0:T(8,128)(2,1)S(1)} collective-permute-done((bf16[2,2,1,2,1,128,128]{6,5,4,3,2,1,0:T(8,128)(2,1)S(1)}, bf16[2,2,1,2,1,128,128]{6,5,4,3,2,1,0:T(8,128)(2,1)S(1)}, u32[]{:S(2)}, u32[]{:S(2)}) %collective-permute-start.10) | collective-permute-done | bytes 262176 | tf_op jit(solution)/shard_map/ppermute | solution.py:96
  206.3 10.4 %fusion.100 = f32[128,6144]{1,0:T(8,128)S(1)} fusion(bf16[128,2048]{1,0:T(8,128)(2,1)} %fusion.31, bf16[2048,6144]{1,0:T(8,128)(2,1)} %all-gather.6.cloned.1.call-done.right_ref), kind=kOutput, calls=%fused_computation.347 | convolution fusion | flops 3221225472 | bytes 28835840 | tf_op jit(solution)/shard_map/dot_general | solution.py:605
  234.4 11.8 %copy.145 = bf16[8,2048,256]{1,2,0:T(8,128)(2,1)} copy(bf16[8,2048,256]{2,1,0:T(8,128)(2,1)} %refs_0_.3) | data formatting | bytes 16777216 | tf_op args[10]
  246.2 11.5 %copy.146 = bf16[8,2048,256]{1,2,0:T(8,128)(2,1)} copy(bf16[8,2048,256]{2,1,0:T(8,128)(2,1)} %refs_1_.3) | data formatting | bytes 16777216 | tf_op args[11]
  257.7 11.5 %copy.147 = bf16[8,256,2048]{1,2,0:T(8,128)(2,1)} copy(bf16[8,256,2048]{2,1,0:T(8,128)(2,1)} %refs_2_.3) | data formatting | bytes 16777216 | tf_op args[12]
  276.8 71.2 %all-gather.8.cloned.1.call-done = bf16[4096,2048]{1,0:T(8,128)(2,1)} async-done(((bf16[128,2048]{1,0:T(8,128)(2,1)}), bf16[4096,2048]{1,0:T(8,128)(2,1)}) %all-gather.8.cloned.1.call-update) | async-done | bytes 16777232 | tf_op jit(solution)/shard_map/all_gather | solution.py:564
  348.0 39.1 %experts_forward.2 = (bf16[16,64,2048]{2,1,0:T(8,128)(2,1)}, bf16[16,64,2048]{2,1,0:T(8,128)(2,1)}, f32[16,8,128]{2,1,0:T(8,128)}, f32[8,512,512]{2,1,0:T(8,128)...) custom-call(s32[1]{0:T(128)} %bitcast.1._, f32[32,8,128]{2,1,0:T(8,128)} %dynamic-slice_convert_fusion.slots_ref, ...), custom_call_target="tpu_custom_call" | custom-call | flops 85899345920 | bytes 67108864 | tf_op jit(solution)/shard_map/experts_forward/pallas_call | solution.py:439
  387.6 39.2 %experts_forward.3 = (bf16[16,64,2048]{2,1,0:T(8,128)(2,1)}, bf16[16,64,2048]{2,1,0:T(8,128)(2,1)}, f32[16,8,128]{2,1,0:T(8,128)}, f32[8,512,512]{2,1,0:T(8,128)...) custom-call(s32[1]{0:T(128)} %bitcast._, ...), custom_call_target="tpu_custom_call", output_to_operand_aliasing={{4}: (7, {}), {5}: (8, {})} | custom-call | flops 85899345920 | bytes 67108864 | tf_op jit(solution)/shard_map/experts_forward/pallas_call | solution.py:439
  433.9 30.2 %all-gather.10.cloned.1.call-done = bf16[4096,2048]{1,0:T(8,128)(2,1)} async-done(((bf16[128,2048]{1,0:T(8,128)(2,1)}), bf16[4096,2048]{1,0:T(8,128)(2,1)}) %all-gather.10.cloned.1.call-update) | async-done | bytes 16777232 | tf_op jit(solution)/shard_map/all_gather | solution.py:564
  466.1 39.0 %experts_backward.2 = (bf16[16,64,2048]{2,1,0:T(8,128)(2,1)}, bf16[16,64,2048]{2,1,0:T(8,128)(2,1)}, f32[16,8,128]{2,1,0:T(8,128)}, bf16[8,1024,256]{2,1,0:T(8,1...) custom-call(s32[1]{0:T(128)} %bitcast.1._, ...), custom_call_target="tpu_custom_call" | custom-call | flops 85899345920 | bytes 67108864 | tf_op jit(solution)/shard_map/experts_backward/pallas_call | solution.py:439
  505.2 7.0 collective-permute-done.15
  526.1 39.1 %experts_backward.3 = (bf16[16,64,2048]{2,1,0:T(8,128)(2,1)}, bf16[16,64,2048]{2,1,0:T(8,128)(2,1)}, f32[16,8,128]{2,1,0:T(8,128)}, bf16[8,1024,256]{2,1,0:T(8,1...) custom-call(s32[1]{0:T(128)} %bitcast._, ...), custom_call_target="tpu_custom_call", output_to_operand_aliasing={{3}: (8, {}), {4}: (9, {}), {5}: (10, {})} | custom-call | flops 85899345920 | bytes 67108864 | tf_op jit(solution)/shard_map/experts_backward/pallas_call | solution.py:439
  581.5 20.1 %fusion.102 = f32[8,256,2048]{2,1,0:T(8,128)} fusion(bf16[8,1024,256]{2,1,0:T(8,128)(2,1)} %get-tuple-element.214, bf16[8,1024,2048]{2,1,0:T(8,128)(2,1)} %bitcast.426), kind=kOutput, calls=%fused_computation.349 | convolution fusion | flops 8589934592 | bytes 54525952 | tf_op jit(solution)/shard_map/erh,erd->ehd/dot_general | solution.py:717
  601.6 21.0 %fusion.101 = f32[8,2048,256]{2,1,0:T(8,128)} fusion(bf16[8,1024,2048]{2,1,0:T(8,128)(2,1)} %bitcast.427, bf16[8,1024,256]{2,1,0:T(8,128)(2,1)} %get-tuple-element.213), kind=kOutput, calls=%fused_computation.348 | convolution fusion | flops 8589934592 | bytes 54525952 | tf_op jit(solution)/shard_map/erd,erh->edh/dot_general | solution.py:717
  641.2 21.1 %fusion.103 = f32[8,2048,256]{2,1,0:T(8,128)} fusion(bf16[8,1024,2048]{2,1,0:T(8,128)(2,1)} %bitcast.428, bf16[8,1024,256]{2,1,0:T(8,128)(2,1)} %get-tuple-element.222), kind=kOutput, calls=%fused_computation.350 | convolution fusion | flops 8589934592 | bytes 54525952 | tf_op jit(solution)/shard_map/erd,erh->edh/dot_general | solution.py:717
  671.2 23.4 %collective-permute-done.30 = bf16[2,64,2048]{2,1,0:T(8,128)(2,1)S(1)} collective-permute-done((bf16[2,64,2048]{2,1,0:T(8,128)(2,1)S(1)}, bf16[2,64,2048]{2,1,0:T(8,128)(2,1)S(1)}, u32[]{:S(2)}, u32[]{:S(2)}) %collective-permute-start.30) | collective-permute-done | bytes 524320 | tf_op jit(solution)/shard_map/ppermute | solution.py:96
  704.3 6.2 collective-permute-done.34
  713.8 6.5 fusion.29
  750.7 6.4 collective-permute-done.44
  764.0 13.9 %turned_product.1 = f32[128,2048]{1,0:T(8,128)S(1)} custom-call(bf16[128,6144]{1,0:T(8,128)(2,1)S(1)} %pad_maximum_fusion.3.left_ref, bf16[2048,6144]{1,0:T(8,128)(2,1)} %all-gather.6.cloned.1.call-done.right_ref), custom_call_target="tpu_custom_call" | custom-call | flops 80530636800 | bytes 25165824 | tf_op jit(solution)/shard_map/turned_product/pallas_call | solution.py:238
  801.0 19.6 %collective-permute-done.49 = bf16[2,2,64,1024]{3,2,0,1:T(8,128)(2,1)S(1)} collective-permute-done((bf16[2,2,64,1024]{3,2,0,1:T(8,128)(2,1)S(1)}, bf16[2,2,64,1024]{3,2,0,1:T(8,128)(2,1)S(1)}, u32[]{:S(2)}, u32[]{:S(2)}) %collective-permute-start.49) | collective-permute-done | bytes 524320 | tf_op jit(solution)/shard_map/ppermute | solution.py:96
  833.7 5.5 collective-permute-done.53
  842.1 23.5 %collective-permute-done.52 = bf16[2,64,1024]{2,1,0:T(8,128)(2,1)S(1)} collective-permute-done((bf16[2,64,1024]{2,1,0:T(8,128)(2,1)S(1)}, bf16[2,64,1024]{2,1,0:T(8,128)(2,1)S(1)}, u32[]{:S(2)}, u32[]{:S(2)}) %collective-permute-start.52) | collective-permute-done | bytes 262176 | tf_op jit(solution)/shard_map/ppermute | solution.py:96
  (552 shorter events, 257.6 us)
Async XLA Ops:
  7.2 199.1 %all-gather.6.cloned.1.call-start = ((), (), s32[]{:S(2)}) async-start(), calls=%async_computation | async-start | bytes 25952256 | tf_op jit(solution)/shard_map/all_gather | solution.py:564
  9.3 338.7 %all-gather.8.cloned.1.call-start = ((), (), s32[]{:S(2)}) async-start(), calls=%async_computation.1 | async-start | bytes 17301504 | tf_op jit(solution)/shard_map/all_gather | solution.py:564
  25.6 28.6 %collective-permute-start.1 = (bf16[1,1,1,2,1,64,2048]{6,5,4,3,2,1,0:T(8,128)(2,1)S(1)}, bf16[1,1,1,2,1,64,2048]{6,5,4,3,2,1,0:T(8,128)(2,1)S(1)}, u32[]{:S(2)}, u32[]{:S(2)}) collective-permute-start(bf16[1,1,1,2,1,64,2048]{6,5,4,3,2,1,0:T(8,128)(2,1)S(1)} %constant_dynamic-update-slice_fusion.22), channel_id=1, source_target_pairs={{0,1},{1,0},{2,3},{3,2},{4,5},{5,4},{6,7},{7,6},{8,9},{9,8},{10,11... | collective-permute-start | bytes 1572872 | tf_op jit(solution)/shard_map/ppermute | solution.py:96
  77.4 26.9 %collective-permute-start.3 = (bf16[1,2,1,2,2,32,2048]{6,5,4,3,2,1,0:T(8,128)(2,1)S(1)}, bf16[1,2,1,2,2,32,2048]{6,5,4,3,2,1,0:T(8,128)(2,1)S(1)}, u32[]{:S(2)}, u32[]{:S(2)}) collective-permute-start(bf16[1,2,1,2,2,32,2048]{6,5,4,3,2,1,0:T(8,128)(2,1)S(1)} %constant_dynamic-update-slice_fusion.18), channel_id=1, source_target_pairs={{0,16},{4,20},{8,24},{12,28},{16,0},{20,4},{24,8},{28,12},{1,17},{... | collective-permute-start | bytes 3145736 | tf_op jit(solution)/shard_map/ppermute | solution.py:96
  83.4 30.8 %collective-permute-start.5 = (bf16[2,1,1,2,2,32,2048]{6,5,4,3,2,1,0:T(8,128)(2,1)S(1)}, bf16[2,1,1,2,2,32,2048]{6,5,4,3,2,1,0:T(8,128)(2,1)}, u32[]{:S(2)}, u32[]{:S(2)}) collective-permute-start(bf16[2,1,1,2,2,32,2048]{6,5,4,3,2,1,0:T(8,128)(2,1)S(1)} %constant_dynamic-update-slice_fusion.14), channel_id=1, source_target_pairs={{0,8},{4,12},{8,0},{12,4},{16,24},{20,28},{24,16},{28,20},{1,9},{5... | collective-permute-start | bytes 3145736 | tf_op jit(solution)/shard_map/ppermute | solution.py:96
  168.1 29.0 %collective-permute-start.10 = (bf16[2,2,1,2,1,128,128]{6,5,4,3,2,1,0:T(8,128)(2,1)S(1)}, bf16[2,2,1,2,1,128,128]{6,5,4,3,2,1,0:T(8,128)(2,1)S(1)}, u32[]{:S(2)}, u32[]{:S(2)}) collective-permute-start(bf16[2,2,1,2,1,128,128]{6,5,4,3,2,1,0:T(8,128)(2,1)S(1)} %constant_dynamic-update-slice_fusion.4), channel_id=1, source_target_pairs={{0,1},{1,0},{2,3},{3,2},{4,5},{5,4},{6,7},{7,6},{8,9},{9,8},{10,11... | collective-permute-start | bytes 786440 | tf_op jit(solution)/shard_map/ppermute | solution.py:96
  233.5 230.6 %all-gather.10.cloned.1.call-start = ((), (), s32[]{:S(2)}) async-start(), calls=%async_computation.2 | async-start | bytes 17301504 | tf_op jit(solution)/shard_map/all_gather | solution.py:564
  274.2 246.5 %collective-permute-start.16 = (bf16[128,2048]{1,0:T(8,128)(2,1)}, bf16[128,2048]{1,0:T(8,128)(2,1)}, u32[]{:S(2)}, u32[]{:S(2)}) collective-permute-start(bf16[128,2048]{1,0:T(8,128)(2,1)} %pad_maximum_fusion.13), channel_id=1, source_target_pairs={{0,4},{4,0},{8,12},{12,8},{16,20},{20,16},{24,28},{28,24},{1,5},{5... | collective-permute-start | bytes 1572872 | tf_op jit(solution)/shard_map/ppermute | solution.py:96
  387.1 39.8 %collective-permute-start.12 = (bf16[16,64,2048]{2,1,0:T(8,128)(2,1)}, bf16[16,64,2048]{2,1,0:T(8,128)(2,1)}, u32[]{:S(2)}, u32[]{:S(2)}) collective-permute-start(bf16[16,64,2048]{2,1,0:T(8,128)(2,1)} %get-tuple-element.160), channel_id=1, source_target_pairs={{0,4},{4,0},{8,12},{12,8},{16,20},{20,16},{24,28},{28,24},{1,5},{5... | collective-permute-start | bytes 12582920 | tf_op jit(solution)/shard_map/ppermute | solution.py:96
  387.4 39.4 %collective-permute-start.13 = (bf16[16,64,2048]{2,1,0:T(8,128)(2,1)}, bf16[16,64,2048]{2,1,0:T(8,128)(2,1)}, u32[]{:S(2)}, u32[]{:S(2)}) collective-permute-start(bf16[16,64,2048]{2,1,0:T(8,128)(2,1)} %get-tuple-element.161), channel_id=1, source_target_pairs={{0,4},{4,0},{8,12},{12,8},{16,20},{20,16},{24,28},{28,24},{1,5},{5... | collective-permute-start | bytes 12582920 | tf_op jit(solution)/shard_map/ppermute | solution.py:96
  464.1 48.1 %collective-permute-start.15 = (bf16[2,2,2,64,2048]{4,3,1,2,0:T(8,128)(2,1)}, bf16[2,2,2,64,2048]{4,3,1,2,0:T(8,128)(2,1)}, u32[]{:S(2)}, u32[]{:S(2)}) collective-permute-start(bf16[2,2,2,64,2048]{4,3,1,2,0:T(8,128)(2,1)} %fusion.6), channel_id=1, source_target_pairs={{0,8},{4,12},{8,0},{12,4},{16,24},{20,28},{24,16},{28,20},{1,9},{5... | collective-permute-start | bytes 6291464 | tf_op jit(solution)/shard_map/ppermute | solution.py:96
  465.3 47.6 %collective-permute-start.14 = (bf16[2,2,2,64,2048]{4,3,1,2,0:T(8,128)(2,1)S(1)}, bf16[2,2,2,64,2048]{4,3,1,2,0:T(8,128)(2,1)}, u32[]{:S(2)}, u32[]{:S(2)}) collective-permute-start(bf16[2,2,2,64,2048]{4,3,1,2,0:T(8,128)(2,1)S(1)} %fusion.5), channel_id=1, source_target_pairs={{0,16},{4,20},{8,24},{12,28},{16,0},{20,4},{24,8},{28,12},{1,17},{... | collective-permute-start | bytes 6291464 | tf_op jit(solution)/shard_map/ppermute | solution.py:96
  523.1 42.0 %collective-permute-start.17 = (bf16[2,2,64,2048]{3,2,0,1:T(8,128)(2,1)}, bf16[2,2,64,2048]{3,2,0,1:T(8,128)(2,1)}, u32[]{:S(2)}, u32[]{:S(2)}) collective-permute-start(bf16[2,2,64,2048]{3,2,0,1:T(8,128)(2,1)} %dynamic-slice_bitcast_fusion.4), channel_id=1, source_target_pairs={{0,8},{4,12},{8,0},{12,4},{16,24},{20,28},{24,16},{28,20},{1,9},{5... | collective-permute-start | bytes 3145736 | tf_op jit(solution)/shard_map/ppermute | solution.py:96
  524.0 43.2 %collective-permute-start.18 = (bf16[2,2,64,2048]{3,2,0,1:T(8,128)(2,1)S(1)}, bf16[2,2,64,2048]{3,2,0,1:T(8,128)(2,1)}, u32[]{:S(2)}, u32[]{:S(2)}) collective-permute-start(bf16[2,2,64,2048]{3,2,0,1:T(8,128)(2,1)S(1)} %dynamic-slice_bitcast_fusion.3), channel_id=1, source_target_pairs={{0,16},{4,20},{8,24},{12,28},{16,0},{20,4},{24,8},{28,12},{1,17},{... | collective-permute-start | bytes 3145736 | tf_op jit(solution)/shard_map/ppermute | solution.py:96
  525.5 43.5 %collective-permute-start.19 = (bf16[16,64,2048]{2,1,0:T(8,128)(2,1)}, bf16[16,64,2048]{2,1,0:T(8,128)(2,1)}, u32[]{:S(2)}, u32[]{:S(2)}) collective-permute-start(bf16[16,64,2048]{2,1,0:T(8,128)(2,1)} %get-tuple-element.202), channel_id=1, source_target_pairs={{0,4},{4,0},{8,12},{12,8},{16,20},{20,16},{24,28},{28,24},{1,5},{5... | collective-permute-start | bytes 12582920 | tf_op jit(solution)/shard_map/ppermute | solution.py:96
  525.5 43.5 %collective-permute-start.20 = (bf16[16,64,2048]{2,1,0:T(8,128)(2,1)}, bf16[16,64,2048]{2,1,0:T(8,128)(2,1)}, u32[]{:S(2)}, u32[]{:S(2)}) collective-permute-start(bf16[16,64,2048]{2,1,0:T(8,128)(2,1)} %get-tuple-element.203), channel_id=1, source_target_pairs={{0,4},{4,0},{8,12},{12,8},{16,20},{20,16},{24,28},{28,24},{1,5},{5... | collective-permute-start | bytes 12582920 | tf_op jit(solution)/shard_map/ppermute | solution.py:96
  569.2 53.4 %collective-permute-start.24 = (f32[2,2,2,2,8,128]{5,4,3,2,1,0:T(8,128)S(1)}, f32[2,2,2,2,8,128]{5,4,3,2,1,0:T(8,128)S(1)}, u32[]{:S(2)}, u32[]{:S(2)}) collective-permute-start(f32[2,2,2,2,8,128]{5,4,3,2,1,0:T(8,128)S(1)} %dynamic-slice_bitcast_fusion.22), channel_id=1, source_target_pairs={{0,1},{1,0},{2,3},{3,2},{4,5},{5,4},{6,7},{7,6},{8,9},{9,8},{10,11... | collective-permute-start | bytes 196616 | tf_op jit(solution)/shard_map/ppermute | solution.py:96
  569.7 52.9 %collective-permute-start.23 = (bf16[2,128,2048]{2,1,0:T(8,128)(2,1)S(1)}, bf16[2,128,2048]{2,1,0:T(8,128)(2,1)}, u32[]{:S(2)}, u32[]{:S(2)}) collective-permute-start(bf16[2,128,2048]{2,1,0:T(8,128)(2,1)S(1)} %dynamic-slice_bitcast_fusion.2), channel_id=1, source_target_pairs={{0,1},{1,0},{2,3},{3,2},{4,5},{5,4},{6,7},{7,6},{8,9},{9,8},{10,11... | collective-permute-start | bytes 3145736 | tf_op jit(solution)/shard_map/ppermute | solution.py:96
  575.3 49.0 %collective-permute-start.22 = (bf16[2,2,2,64,2048]{4,3,2,1,0:T(8,128)(2,1)}, bf16[2,2,2,64,2048]{4,3,2,1,0:T(8,128)(2,1)}, u32[]{:S(2)}, u32[]{:S(2)}) collective-permute-start(bf16[2,2,2,64,2048]{4,3,2,1,0:T(8,128)(2,1)} %fusion.8), channel_id=1, source_target_pairs={{0,8},{4,12},{8,0},{12,4},{16,24},{20,28},{24,16},{28,20},{1,9},{5... | collective-permute-start | bytes 6291464 | tf_op jit(solution)/shard_map/ppermute | solution.py:96
  580.2 47.2 %collective-permute-start.21 = (bf16[2,2,2,64,2048]{4,3,1,2,0:T(8,128)(2,1)}, bf16[2,2,2,64,2048]{4,3,1,2,0:T(8,128)(2,1)}, u32[]{:S(2)}, u32[]{:S(2)}) collective-permute-start(bf16[2,2,2,64,2048]{4,3,1,2,0:T(8,128)(2,1)} %fusion.7), channel_id=1, source_target_pairs={{0,16},{4,20},{8,24},{12,28},{16,0},{20,4},{24,8},{28,12},{1,17},{... | collective-permute-start | bytes 6291464 | tf_op jit(solution)/shard_map/ppermute | solution.py:96
  635.0 27.4 %collective-permute-start.28 = (f32[2,2,2,8,128]{4,3,2,1,0:T(8,128)S(1)}, f32[2,2,2,8,128]{4,3,2,1,0:T(8,128)S(1)}, u32[]{:S(2)}, u32[]{:S(2)}) collective-permute-start(f32[2,2,2,8,128]{4,3,2,1,0:T(8,128)S(1)} %dynamic-slice_bitcast_fusion.27), channel_id=1, source_target_pairs={{0,2},{1,3},{2,0},{3,1},{4,6},{5,7},{6,4},{7,5},{8,10},{9,11},{10,... | collective-permute-start | bytes 98312 | tf_op jit(solution)/shard_map/ppermute | solution.py:96
  665.9 29.3 %collective-permute-start.33 = (bf16[256,2048]{1,0:T(8,128)(2,1)S(1)}, bf16[256,2048]{1,0:T(8,128)(2,1)S(1)}, u32[]{:S(2)}, u32[]{:S(2)}) collective-permute-start(bf16[256,2048]{1,0:T(8,128)(2,1)S(1)} %constant_dynamic-update-slice_fusion.24), channel_id=1, source_target_pairs={{0,8},{4,12},{8,0},{12,4},{16,24},{20,28},{24,16},{28,20},{1,9},{5... | collective-permute-start | bytes 3145736 | tf_op jit(solution)/shard_map/ppermute | solution.py:96
  667.5 27.8 %collective-permute-start.32 = (bf16[256,1024]{1,0:T(8,128)(2,1)S(1)}, bf16[256,1024]{1,0:T(8,128)(2,1)S(1)}, u32[]{:S(2)}, u32[]{:S(2)}) collective-permute-start(bf16[256,1024]{1,0:T(8,128)(2,1)S(1)} %slice.134), channel_id=1, source_target_pairs={{0,16},{4,20},{8,24},{12,28},{16,0},{20,4},{24,8},{28,12},{1,17},{... | collective-permute-start | bytes 1572872 | tf_op jit(solution)/shard_map/ppermute | solution.py:96
  668.2 26.4 %collective-permute-start.30 = (bf16[2,64,2048]{2,1,0:T(8,128)(2,1)S(1)}, bf16[2,64,2048]{2,1,0:T(8,128)(2,1)S(1)}, u32[]{:S(2)}, u32[]{:S(2)}) collective-permute-start(bf16[2,64,2048]{2,1,0:T(8,128)(2,1)S(1)} %dynamic-slice_bitcast_fusion.9), channel_id=1, source_target_pairs={{0,2},{1,3},{2,0},{3,1},{4,6},{5,7},{6,4},{7,5},{8,10},{9,11},{10,... | collective-permute-start | bytes 1572872 | tf_op jit(solution)/shard_map/ppermute | solution.py:96
  669.8 25.3 %collective-permute-start.29 = (bf16[2,64,2048]{2,1,0:T(8,128)(2,1)S(1)}, bf16[2,64,2048]{2,1,0:T(8,128)(2,1)S(1)}, u32[]{:S(2)}, u32[]{:S(2)}) collective-permute-start(bf16[2,64,2048]{2,1,0:T(8,128)(2,1)S(1)} %dynamic-slice_bitcast_fusion.10), channel_id=1, source_target_pairs={{0,1},{1,0},{2,3},{3,2},{4,5},{5,4},{6,7},{7,6},{8,9},{9,8},{10,11... | collective-permute-start | bytes 1572872 | tf_op jit(solution)/shard_map/ppermute | solution.py:96
  761.6 25.4 %collective-permute-start.47 = (bf16[2,2,2,64,1024]{4,3,0,2,1:T(8,128)(2,1)S(1)}, bf16[2,2,2,64,1024]{4,3,0,2,1:T(8,128)(2,1)S(1)}, u32[]{:S(2)}, u32[]{:S(2)}) collective-permute-start(bf16[2,2,2,64,1024]{4,3,0,2,1:T(8,128)(2,1)S(1)} %copy_bitcast_fusion.2), channel_id=1, source_target_pairs={{0,8},{4,12},{8,0},{12,4},{16,24},{20,28},{24,16},{28,20},{1,9},{5... | collective-permute-start | bytes 3145736 | tf_op jit(solution)/shard_map/ppermute | solution.py:96
  762.5 25.9 %collective-permute-start.46 = (bf16[2,2,2,64,1024]{4,3,0,1,2:T(8,128)(2,1)S(1)}, bf16[2,2,2,64,1024]{4,3,0,1,2:T(8,128)(2,1)S(1)}, u32[]{:S(2)}, u32[]{:S(2)}) collective-permute-start(bf16[2,2,2,64,1024]{4,3,0,1,2:T(8,128)(2,1)S(1)} %copy_bitcast_fusion.3), channel_id=1, source_target_pairs={{0,16},{4,20},{8,24},{12,28},{16,0},{20,4},{24,8},{28,12},{1,17},{... | collective-permute-start | bytes 3145736 | tf_op jit(solution)/shard_map/ppermute | solution.py:96
  793.0 29.6 %collective-permute-start.51 = (bf16[2,2,2,64,1024]{4,3,0,2,1:T(8,128)(2,1)S(1)}, bf16[2,2,2,64,1024]{4,3,0,2,1:T(8,128)(2,1)S(1)}, u32[]{:S(2)}, u32[]{:S(2)}) collective-permute-start(bf16[2,2,2,64,1024]{4,3,0,2,1:T(8,128)(2,1)S(1)} %copy_bitcast_fusion), channel_id=1, source_target_pairs={{0,8},{4,12},{8,0},{12,4},{16,24},{20,28},{24,16},{28,20},{1,9},{5... | collective-permute-start | bytes 3145736 | tf_op jit(solution)/shard_map/ppermute | solution.py:96
  795.2 27.9 %collective-permute-start.50 = (bf16[2,2,2,64,1024]{4,3,0,1,2:T(8,128)(2,1)S(1)}, bf16[2,2,2,64,1024]{4,3,0,1,2:T(8,128)(2,1)S(1)}, u32[]{:S(2)}, u32[]{:S(2)}) collective-permute-start(bf16[2,2,2,64,1024]{4,3,0,1,2:T(8,128)(2,1)S(1)} %copy_bitcast_fusion.1), channel_id=1, source_target_pairs={{0,16},{4,20},{8,24},{12,28},{16,0},{20,4},{24,8},{28,12},{1,17},{... | collective-permute-start | bytes 3145736 | tf_op jit(solution)/shard_map/ppermute | solution.py:96
  827.6 38.2 %collective-permute-start.55 = (bf16[2,2,64,1024]{3,2,0,1:T(8,128)(2,1)}, bf16[2,2,64,1024]{3,2,0,1:T(8,128)(2,1)S(1)}, u32[]{:S(2)}, u32[]{:S(2)}) collective-permute-start(bf16[2,2,64,1024]{3,2,0,1:T(8,128)(2,1)} %dynamic-slice_bitcast_fusion.5), channel_id=1, source_target_pairs={{0,2},{1,3},{2,0},{3,1},{4,6},{5,7},{6,4},{7,5},{8,10},{9,11},{10,... | collective-permute-start | bytes 1572872 | tf_op jit(solution)/shard_map/ppermute | solution.py:96
  830.6 35.4 %collective-permute-start.54 = (bf16[2,2,64,1024]{3,2,0,1:T(8,128)(2,1)S(1)}, bf16[2,2,64,1024]{3,2,0,1:T(8,128)(2,1)S(1)}, u32[]{:S(2)}, u32[]{:S(2)}) collective-permute-start(bf16[2,2,64,1024]{3,2,0,1:T(8,128)(2,1)S(1)} %dynamic-slice_bitcast_fusion.6), channel_id=1, source_target_pairs={{0,1},{1,0},{2,3},{3,2},{4,5},{5,4},{6,7},{7,6},{8,9},{9,8},{10,11... | collective-permute-start | bytes 1572872 | tf_op jit(solution)/shard_map/ppermute | solution.py:96
  831.6 34.0 %collective-permute-start.52 = (bf16[2,64,1024]{2,1,0:T(8,128)(2,1)S(1)}, bf16[2,64,1024]{2,1,0:T(8,128)(2,1)S(1)}, u32[]{:S(2)}, u32[]{:S(2)}) collective-permute-start(bf16[2,64,1024]{2,1,0:T(8,128)(2,1)S(1)} %dynamic-slice_bitcast_fusion.16), channel_id=1, source_target_pairs={{0,2},{1,3},{2,0},{3,1},{4,6},{5,7},{6,4},{7,5},{8,10},{9,11},{10,... | collective-permute-start | bytes 786440 | tf_op jit(solution)/shard_map/ppermute | solution.py:96
  (134 other events, 1097.3 us)
Sparse Core Ops, SparseCore 0:
  11.5 194.7 all-gather.5
  233.7 114.2 all-gather.7
  351.0 113.0 all-gather.9
